TPU v7x, 32 devices: a whole 2x2x4 slice. The times are simulated.
32 devices in a mesh: groups: 2 (over y), expert: 8 (over z, core), blk: 2 (over x).
Axes of the slice: x: 2, y: 2, z: 4, core: 2. Of those that a mesh axis runs over, the one named last changes fastest.
Arguments:
- tokens: bfloat16 [128, 6144], P(('groups', 'expert'), 'blk'), parts along dimension 0, may hold values from -6 to 6
- expert_ids: int32 [128, 4], P(('groups', 'expert')), parts along dimension 0, may hold values from 0 to 7, all different within a row; in each aligned block of 8 rows (0 to 7, 8 to 15, ...) at most 5 rows name the same one
- route_weight: float32 [128, 4], P(('groups', 'expert')), parts along dimension 0, may hold values from 0.05 to 0.6
- w_gate: bfloat16 [8, 5376, 6144], P('expert', 'blk'), may hold values from -0.078125 to 0.078125
- w_up: bfloat16 [8, 5376, 6144], P('expert', 'blk'), may hold values from -0.078125 to 0.078125
- w_down: bfloat16 [8, 5376, 6144], P('expert', 'blk'), may hold values from -0.078125 to 0.078125
Outputs:
- mixed: bfloat16 [128, 6144], P(('groups', 'expert'), 'blk'), parts along dimension 0
There are 2 independent parts, one for each index of `groups`. A program takes and returns all parts, laid end to end along the dimension named above; an argument that names none is the same for every part. Nothing has to cross between parts.
Inputs may be any that keep to these rules, and one draw needn't show every extreme that they name: `expert_ids`: each token names 4 different experts. In each aligned block of 8 rows (the tokens of one index of expert) no expert is named by more than 5 tokens, and in every draw some expert is named by exactly 5 tokens of some block.
All inputs are finite; a program needn't handle non-finite values.
Results may differ from a plain program's by a relative error of at most 0.0085.
Values may be sent and summed in bfloat16 or wider, within the bound.
No kernel may reach another device: no remote copies, remote signals or barrier semaphores. Data moves between devices by JAX's collectives and lax.ppermute only.
A program may use at most 192 MiB of HBM per device.

v0:
```python
import functools

import jax
import jax.numpy as jnp
from jax import lax
from jax.experimental import pallas as pl
from jax.experimental.pallas import tpu as pltpu
from jax.sharding import PartitionSpec as P

FFW = 5376
PAIR = 2
LANES = 128
SLOTS = 3
MIB = 1024 * 1024
F32 = jnp.float32
BF16 = jnp.bfloat16


def dot_rows(left, right):
    return lax.dot_general(left, right, (((1,), (1,)), ((), ())), preferred_element_type=F32)


def largest_step(total, choices):
    for step in choices:
        if total % step == 0:
            return step
    return total


def call(kernel, outs, operands, spaces, scratch, limit, flops, moved):
    return pl.pallas_call(
        kernel,
        out_shape=outs,
        in_specs=[pl.BlockSpec(memory_space=space) for space in spaces],
        out_specs=jax.tree.map(lambda unused: pl.BlockSpec(memory_space=pltpu.VMEM), outs),
        scratch_shapes=scratch,
        compiler_params=pltpu.CompilerParams(vmem_limit_bytes=limit * MIB),
        cost_estimate=pl.CostEstimate(flops=flops, bytes_accessed=moved, transcendentals=0),
    )(*operands)


def stream(count, copies, begin, work):
    for step in range(min(SLOTS - 1, count)):
        for copy in copies(step, step):
            copy.start()
    begin()

    def one(step, carry):
        slot = lax.rem(step, SLOTS)
        later = step + SLOTS - 1

        @pl.when(later < count)
        def _():
            for copy in copies(later, lax.rem(later, SLOTS)):
                copy.start()

        work(step, slot, copies(step, slot))
        return carry

    lax.fori_loop(0, count, one, 0)


def pack_kernel(experts, tokens, ids, weights, out):
    rows, width = tokens.shape
    out[:, :width] = tokens[...]
    shape = (rows, out.shape[1] - width)
    lane = lax.broadcasted_iota(jnp.int32, shape, 1)
    diagonal = lax.broadcasted_iota(jnp.int32, (rows, rows), 0) == lax.broadcasted_iota(
        jnp.int32, (rows, rows), 1
    )
    coef = jnp.zeros(shape, F32)
    for k in range(ids.shape[0]):
        name = jnp.sum(jnp.where(diagonal, ids[k : k + 1], 0), axis=1, keepdims=True)
        weight = jnp.sum(jnp.where(diagonal, weights[k : k + 1], 0.0), axis=1, keepdims=True)
        coef += jnp.where(lax.rem(lane, experts) == name, weight, 0.0)
    high = coef.astype(BF16).astype(F32)
    middle = (coef - high).astype(BF16).astype(F32)
    low = coef - high - middle
    part = jnp.where(lane < experts, high, jnp.where(lane < 2 * experts, middle, low))
    out[:, width:] = jnp.where(lane < 3 * experts, part, 0.0).astype(BF16)


def first_kernel(hb, own, other, w_gate, w_up, gate, up, x, gate_buf, up_buf, sems):
    half, width = own.shape[0], x.shape[1]
    column = pl.multiple_of(lax.axis_index("blk") * width, LANES)

    def copies(step, slot):
        rows = pl.ds(pl.multiple_of(step * hb, 8), hb)
        window = (0, rows, pl.ds(column, width))
        return (
            pltpu.make_async_copy(w_gate.at[window], gate_buf.at[slot], sems.at[0, slot]),
            pltpu.make_async_copy(w_up.at[window], up_buf.at[slot], sems.at[1, slot]),
        )

    def begin():
        x[:half] = own[:, :width]
        x[half:] = other[:, :width]

    def work(step, slot, waits):
        units = pl.ds(pl.multiple_of(step * hb, LANES), hb)
        waits[0].wait()
        gate[:, units] = dot_rows(x[...], gate_buf[slot])
        waits[1].wait()
        up[:, units] = dot_rows(x[...], up_buf[slot])

    stream(w_gate.shape[1] // hb, copies, begin, work)


def second_kernel(hb, others, *refs):
    sent = refs[: 2 * others]
    gate, up, w_gate, w_up, hidden, x, gate_buf, up_buf, sems = refs[2 * others :]
    half, width = sent[0].shape
    here = lax.axis_index("blk")

    def copies(step, slot):
        rows = pl.ds(pl.multiple_of(step * hb, 8), hb)
        made = []
        for place, (weight, buf) in enumerate(((w_gate, gate_buf), (w_up, up_buf))):
            for j in range(others):
                column = pl.multiple_of(lax.rem(here + 1 + j, others + 1) * width, LANES)
                made.append(
                    pltpu.make_async_copy(
                        weight.at[0, rows, pl.ds(column, width)],
                        buf.at[slot, j],
                        sems.at[place, slot, j],
                    )
                )
        return made

    def begin():
        for j in range(others):
            x[j, :half] = sent[2 * j][...]
            x[j, half:] = sent[2 * j + 1][...]

    def work(step, slot, waits):
        units = pl.ds(pl.multiple_of(step * hb, LANES), hb)
        gate_acc, up_acc = gate[:, units], up[:, units]
        for j in range(others):
            waits[j].wait()
            gate_acc += dot_rows(x[j], gate_buf[slot, j])
        for j in range(others):
            waits[others + j].wait()
            up_acc += dot_rows(x[j], up_buf[slot, j])
        value = gate_acc / (1.0 + jnp.exp(-gate_acc)) * up_acc
        hidden[:, units] = value.astype(BF16)

    stream(w_gate.shape[1] // hb, copies, begin, work)


def third_kernel(fb, parts, experts, shares, hidden, own, other, w_down, *refs):
    outs, (buf, sems) = refs[: 2 * len(parts)], refs[2 * len(parts) :]
    half, width = outs[0].shape
    steps = width // fb
    here, cycle = lax.axis_index("blk"), lax.axis_size("blk")
    expert = lax.axis_index("expert") // shares
    packed = jnp.concatenate([own[:, width:], other[:, width:]], axis=0).astype(F32)
    lane = lax.broadcasted_iota(jnp.int32, packed.shape, 1)
    mine = (lax.rem(lane, experts) == expert) & (lane < 3 * experts)
    coef = jnp.sum(jnp.where(mine, packed, 0.0), axis=1, keepdims=True)
    for place, part in enumerate(parts):
        first = lax.rem(here + part, cycle) * width

        def copies(step, slot):
            column = pl.multiple_of(first + step * fb, LANES)
            return (
                pltpu.make_async_copy(
                    w_down.at[0, :, pl.ds(column, fb)], buf.at[slot], sems.at[slot]
                ),
            )

        def work(step, slot, waits):
            waits[0].wait()
            value = jnp.dot(hidden[...], buf[slot], preferred_element_type=F32) * coef
            columns = pl.ds(pl.multiple_of(step * fb, LANES), fb)
            for at in range(2):
                out = outs[2 * place + at]
                out[:, columns] = value[at * half : (at + 1) * half].astype(out.dtype)

        stream(steps, copies, lambda: None, work)


def body(tokens, expert_ids, route_weight, w_gate, w_up, w_down):
    n_expert = lax.axis_size("expert")
    n_blk = lax.axis_size("blk")
    rows, width = tokens.shape
    hid, model = w_gate.shape[1:]
    shares = FFW // (hid * n_blk)
    experts = n_expert // shares
    places = n_expert // PAIR
    half = places * rows
    others = n_blk - 1

    room = -(-3 * experts // LANES) * LANES
    vmem, hbm = pltpu.VMEM, pl.ANY
    packed = call(
        functools.partial(pack_kernel, experts),
        jax.ShapeDtypeStruct((rows, width + room), BF16),
        (tokens, expert_ids.T, route_weight.T),
        (vmem,) * 3,
        [],
        8,
        rows * room,
        4 * rows * width,
    )

    def along(k):
        return [(s, ((s // PAIR + k) % places) * PAIR + s % PAIR) for s in range(n_expert)]

    def across(k):
        return [(s, (s + k) % n_blk) for s in range(n_blk)]

    def across_other(k):
        return [
            (s * n_blk + b, (s ^ 1) * n_blk + (b + k) % n_blk)
            for s in range(n_expert)
            for b in range(n_blk)
        ]

    swap = [(s, s ^ 1) for s in range(n_expert)]

    pieces = [packed] + [lax.ppermute(packed, "expert", along(k)) for k in range(1, places)]
    own = jnp.concatenate(pieces, axis=0)
    other = lax.ppermute(own, "expert", swap)
    bare = own[:, :width]
    sent = []
    for j in range(1, n_blk):
        sent.append(lax.ppermute(bare, "blk", across(-j)))
        sent.append(lax.ppermute(bare, ("expert", "blk"), across_other(-j)))

    hb = largest_step(hid, (384,))
    fb = largest_step(width, (512, 384, 256, 128))
    tokens_all = 2 * half
    w_gate = pltpu.with_memory_space_constraint(w_gate, pltpu.HBM)
    w_up = pltpu.with_memory_space_constraint(w_up, pltpu.HBM)
    w_down = pltpu.with_memory_space_constraint(w_down, pltpu.HBM)
    gate, up = call(
        functools.partial(first_kernel, hb),
        [jax.ShapeDtypeStruct((tokens_all, hid), F32)] * 2,
        (own, other, w_gate, w_up),
        (vmem, vmem, hbm, hbm),
        [
            pltpu.VMEM((tokens_all, width), BF16),
            pltpu.VMEM((SLOTS, hb, width), BF16),
            pltpu.VMEM((SLOTS, hb, width), BF16),
            pltpu.SemaphoreType.DMA((2, SLOTS)),
        ],
        24,
        4 * tokens_all * hid * width,
        4 * hid * width,
    )
    hidden = call(
        functools.partial(second_kernel, hb, others),
        jax.ShapeDtypeStruct((tokens_all, hid), BF16),
        (*sent, gate, up, w_gate, w_up),
        (vmem,) * (len(sent) + 2) + (hbm, hbm),
        [
            pltpu.VMEM((others, tokens_all, width), BF16),
            pltpu.VMEM((SLOTS, others, hb, width), BF16),
            pltpu.VMEM((SLOTS, others, hb, width), BF16),
            pltpu.SemaphoreType.DMA((2, SLOTS, others)),
        ],
        24,
        4 * tokens_all * hid * width * others,
        4 * hid * width * others,
    )

    def down(parts, kinds):
        return call(
            functools.partial(third_kernel, fb, parts, experts, shares),
            [jax.ShapeDtypeStruct((half, width), kind) for unused in parts for kind in kinds],
            (hidden, own, other, w_down),
            (vmem, vmem, vmem, hbm),
            [pltpu.VMEM((SLOTS, hid, fb), BF16), pltpu.SemaphoreType.DMA((SLOTS,))],
            20,
            2 * tokens_all * hid * width * len(parts),
            2 * hid * width * len(parts),
        )

    away = down(tuple(range(1, n_blk)), (BF16, BF16))
    total = []
    for j in range(1, n_blk):
        total.append(lax.ppermute(away[2 * j - 2], "blk", across(j)))
        total.append(lax.ppermute(away[2 * j - 1], ("expert", "blk"), across_other(j)))
    kept, given = down((0,), (F32, BF16))
    total.append(lax.ppermute(given, "expert", swap))
    summed = kept
    for term in total:
        summed = summed + term.astype(F32)
    mixed = summed[:rows]
    for k in range(1, places):
        piece = summed[k * rows : (k + 1) * rows].astype(BF16)
        mixed = mixed + lax.ppermute(piece, "expert", along(-k)).astype(F32)
    return mixed.astype(BF16)


def solution(mesh):
    placed = (
        P(("groups", "expert"), "blk"),
        P(("groups", "expert"), None),
        P(("groups", "expert"), None),
        P("expert", "blk", None),
        P("expert", "blk", None),
        P("expert", "blk", None),
    )
    return jax.shard_map(
        body, mesh=mesh, in_specs=placed, out_specs=P(("groups", "expert"), "blk"), check_vma=False
    )
```

profile of v0, /device:TPU:0, one launch (start us, length us, event | category | flops | bytes accessed | tf_op | source)
XLA Modules:
  0.0 74.3 jit_solution(11058712328287285631)
XLA Ops:
  0.0 0.8 %copy-done = bf16[8,3072]{1,0:T(8,128)(2,1)S(1)} copy-done((bf16[8,3072]{1,0:T(8,128)(2,1)S(1)}, bf16[8,3072]{1,0:T(8,128)(2,1)}, u32[]{:S(2)}) %copy-start) | copy-done | bytes 49176
  0.8 0.7 copy-done.1
  1.5 0.7 copy-done.2
  2.2 0.1 shard_map.64
  2.3 5.1 %collective-permute-start.2 = (bf16[8,3200]{1,0:T(8,128)(2,1)S(1)}, bf16[8,3200]{1,0:T(8,128)(2,1)S(1)}, u32[]{:S(2)}, u32[]{:S(2)}) collective-permute-start(bf16[8,3200]{1,0:T(8,128)(2,1)S(1)} %shard_map.64), channel_id=1, source_target_pairs={{0,12},{2,14},{4,0},{6,2},{8,4},{10,6},{12,8},{14,10},{1,13},{3,15... | collective-permute-start | bytes 153608 | tf_op jit(solution)/shard_map/ppermute | solution.py:221
  7.4 1.0 %collective-permute-start = (bf16[8,3200]{1,0:T(8,128)(2,1)S(1)}, bf16[8,3200]{1,0:T(8,128)(2,1)S(1)}, u32[]{:S(2)}, u32[]{:S(2)}) collective-permute-start(bf16[8,3200]{1,0:T(8,128)(2,1)S(1)} %shard_map.64), channel_id=1, source_target_pairs={{0,4},{2,6},{4,8},{6,10},{8,12},{10,14},{12,0},{14,2},{1,5},{3,7},... | collective-permute-start | bytes 153608 | tf_op jit(solution)/shard_map/ppermute | solution.py:221
  8.4 1.2 %collective-permute-done.2 = bf16[8,3200]{1,0:T(8,128)(2,1)S(1)} collective-permute-done((bf16[8,3200]{1,0:T(8,128)(2,1)S(1)}, bf16[8,3200]{1,0:T(8,128)(2,1)S(1)}, u32[]{:S(2)}, u32[]{:S(2)}) %collective-permute-start.2) | collective-permute-done | bytes 51232 | tf_op jit(solution)/shard_map/ppermute | solution.py:221
  9.5 2.9 %collective-permute-done.1 = bf16[8,3200]{1,0:T(8,128)(2,1)S(1)} collective-permute-done((bf16[8,3200]{1,0:T(8,128)(2,1)S(1)}, bf16[8,3200]{1,0:T(8,128)(2,1)S(1)}, u32[]{:S(2)}, u32[]{:S(2)}) %collective-permute-start.1) | collective-permute-done | bytes 51232 | tf_op jit(solution)/shard_map/ppermute | solution.py:221
  12.4 0.9 %collective-permute-done = bf16[8,3200]{1,0:T(8,128)(2,1)S(1)} collective-permute-done((bf16[8,3200]{1,0:T(8,128)(2,1)S(1)}, bf16[8,3200]{1,0:T(8,128)(2,1)S(1)}, u32[]{:S(2)}, u32[]{:S(2)}) %collective-permute-start) | collective-permute-done | bytes 51232 | tf_op jit(solution)/shard_map/ppermute | solution.py:221
  13.3 0.1 collective-permute-start.5
  13.4 1.7 %collective-permute-start.4 = (bf16[32,3072]{1,0:T(8,128)(2,1)S(1)}, bf16[32,3072]{1,0:T(8,128)(2,1)S(1)}, u32[]{:S(2)}, u32[]{:S(2)}) collective-permute-start(bf16[32,3072]{1,0:T(8,128)(2,1)S(1)} %slice.23), channel_id=1, source_target_pairs={{0,3},{1,2},{2,1},{3,0},{4,7},{5,6},{6,5},{7,4},{8,11},{9,10},{10,... | collective-permute-start | bytes 589832 | tf_op jit(solution)/shard_map/ppermute | solution.py:228
  15.1 0.5 collective-permute-start.3
  15.6 0.0 collective-permute-done.5.other
  15.6 16.1 %shard_map.65 = (f32[64,2688]{1,0:T(8,128)S(1)}, f32[64,2688]{1,0:T(8,128)S(1)}) custom-call(bf16[32,3200]{1,0:T(8,128)(2,1)S(1)} %pad_maximum_fusion.own, bf16[32,3200]{1,0:T(8,128)(2,1)S(1)} %collective-permute-done.5.other, bf16[1,2688,6144]{2,1,0:T(8,128)(2,1)} %refs_4_.1, bf16[1,2688,6144]{2,1,0:T(8,128)(2,1)} %refs_5_.1), custom_call_target="tpu_custom_call" | custom-call | flops 2113929216 | bytes 33030144 | tf_op jit(solution)/shard_map/pallas_call | solution.py:31
  31.7 0.0 collective-permute-done.4.refs_1_
  31.7 0.0 collective-permute-done.3.refs_0_
  31.7 16.2 %shard_map.66.hidden = bf16[64,2688]{1,0:T(8,128)(2,1)S(1)} custom-call(bf16[32,3072]{1,0:T(8,128)(2,1)S(1)} %collective-permute-done.3.refs_0_, bf16[32,3072]{1,0:T(8,128)(2,1)S(1)} %collective-permute-done.4.refs_1_, f32[64,2688]{1,0:T(8,128)S(1)} %get-tuple-element.11.refs_2_, f32[64,2688]{1,0:T(8,128)S(1)} %get-tuple-element.12.refs_3_, ...), custom_call_target="tpu_custom_call" | custom-call | flops 2113929216 | bytes 33030144 | tf_op jit(solution)/shard_map/pallas_call | solution.py:31
  48.0 6.7 %shard_map.68 = (bf16[32,3072]{1,0:T(8,128)(2,1)S(1)}, bf16[32,3072]{1,0:T(8,128)(2,1)S(1)}) custom-call(bf16[64,2688]{1,0:T(8,128)(2,1)S(1)} %shard_map.66.hidden, bf16[32,3200]{1,0:T(8,128)(2,1)S(1)} %pad_maximum_fusion.own, bf16[32,3200]{1,0:T(8,128)(2,1)S(1)} %collective-permute-done.5.other, bf16[1,2688,6144]{2,1,0:T(8,128)(2,1)} %w_down.3), custom_call_target="tpu_custom_call" | custom-call | flops 1056964608 | bytes 16515072 | tf_op jit(solution)/shard_map/pallas_call | solution.py:31
  54.7 1.6 %collective-permute-start.6 = (bf16[32,3072]{1,0:T(8,128)(2,1)S(1)}, bf16[32,3072]{1,0:T(8,128)(2,1)S(1)}, u32[]{:S(2)}, u32[]{:S(2)}) collective-permute-start(bf16[32,3072]{1,0:T(8,128)(2,1)S(1)} %get-tuple-element.14), channel_id=1, source_target_pairs={{0,1},{1,0},{2,3},{3,2},{4,5},{5,4},{6,7},{7,6},{8,9},{9,8},{10,11... | collective-permute-start | bytes 589832 | tf_op jit(solution)/shard_map/ppermute | solution.py:282
  56.3 6.7 %shard_map.67 = (f32[32,3072]{1,0:T(8,128)S(1)}, bf16[32,3072]{1,0:T(8,128)(2,1)S(1)}) custom-call(bf16[64,2688]{1,0:T(8,128)(2,1)S(1)} %shard_map.66.hidden, bf16[32,3200]{1,0:T(8,128)(2,1)S(1)} %pad_maximum_fusion.own, bf16[32,3200]{1,0:T(8,128)(2,1)S(1)} %collective-permute-done.5.other, bf16[1,2688,6144]{2,1,0:T(8,128)(2,1)} %w_down.3), custom_call_target="tpu_custom_call" | custom-call | flops 1056964608 | bytes 16515072 | tf_op jit(solution)/shard_map/pallas_call | solution.py:31
  63.0 0.7 collective-permute-start.8
  63.7 0.0 collective-permute-done.6
  63.7 0.8 %collective-permute-done.7 = bf16[32,3072]{1,0:T(8,128)(2,1)S(1)} collective-permute-done((bf16[32,3072]{1,0:T(8,128)(2,1)S(1)}, bf16[32,3072]{1,0:T(8,128)(2,1)S(1)}, u32[]{:S(2)}, u32[]{:S(2)}) %collective-permute-start.7) | collective-permute-done | bytes 196640 | tf_op jit(solution)/shard_map/ppermute | solution.py:283
  64.6 0.2 collective-permute-done.8
  64.8 0.1 fusion.3
  64.9 1.5 %collective-permute-start.9 = (bf16[8,3072]{1,0:T(8,128)(2,1)S(1)}, bf16[8,3072]{1,0:T(8,128)(2,1)S(1)}, u32[]{:S(2)}, u32[]{:S(2)}) collective-permute-start(bf16[8,3072]{1,0:T(8,128)(2,1)S(1)} %get-tuple-element.19), channel_id=1, source_target_pairs={{0,12},{2,14},{4,0},{6,2},{8,4},{10,6},{12,8},{14,10},{1,13},{3,15... | collective-permute-start | bytes 147464 | tf_op jit(solution)/shard_map/ppermute | solution.py:292
  66.4 0.6 collective-permute-start.11
  67.0 1.3 %collective-permute-start.10 = (bf16[8,3072]{1,0:T(8,128)(2,1)S(1)}, bf16[8,3072]{1,0:T(8,128)(2,1)S(1)}, u32[]{:S(2)}, u32[]{:S(2)}) collective-permute-start(bf16[8,3072]{1,0:T(8,128)(2,1)S(1)} %get-tuple-element.21), channel_id=1, source_target_pairs={{0,8},{2,10},{4,12},{6,14},{8,0},{10,2},{12,4},{14,6},{1,9},{3,11}... | collective-permute-start | bytes 147464 | tf_op jit(solution)/shard_map/ppermute | solution.py:292
  68.3 0.9 %collective-permute-done.9 = bf16[8,3072]{1,0:T(8,128)(2,1)S(1)} collective-permute-done((bf16[8,3072]{1,0:T(8,128)(2,1)S(1)}, bf16[8,3072]{1,0:T(8,128)(2,1)S(1)}, u32[]{:S(2)}, u32[]{:S(2)}) %collective-permute-start.9) | collective-permute-done | bytes 49184 | tf_op jit(solution)/shard_map/ppermute | solution.py:292
  69.2 3.5 %collective-permute-done.11 = bf16[8,3072]{1,0:T(8,128)(2,1)S(1)} collective-permute-done((bf16[8,3072]{1,0:T(8,128)(2,1)S(1)}, bf16[8,3072]{1,0:T(8,128)(2,1)S(1)}, u32[]{:S(2)}, u32[]{:S(2)}) %collective-permute-start.11) | collective-permute-done | bytes 49184 | tf_op jit(solution)/shard_map/ppermute | solution.py:292
  72.7 1.0 %collective-permute-done.10 = bf16[8,3072]{1,0:T(8,128)(2,1)S(1)} collective-permute-done((bf16[8,3072]{1,0:T(8,128)(2,1)S(1)}, bf16[8,3072]{1,0:T(8,128)(2,1)S(1)}, u32[]{:S(2)}, u32[]{:S(2)}) %collective-permute-start.10) | collective-permute-done | bytes 49184 | tf_op jit(solution)/shard_map/ppermute | solution.py:292
  73.7 0.6 fusion.2
  (8 shorter events, 0.1 us)
Async XLA Ops:
  0.0 0.8 %copy-start = (bf16[8,3072]{1,0:T(8,128)(2,1)S(1)}, bf16[8,3072]{1,0:T(8,128)(2,1)}, u32[]{:S(2)}) copy-start(bf16[8,3072]{1,0:T(8,128)(2,1)} %tokens.1) | copy-start | bytes 147460
  0.8 0.7 copy-start.1
  1.5 0.7 copy-start.2
  2.3 7.3 %collective-permute-start.2 = (bf16[8,3200]{1,0:T(8,128)(2,1)S(1)}, bf16[8,3200]{1,0:T(8,128)(2,1)S(1)}, u32[]{:S(2)}, u32[]{:S(2)}) collective-permute-start(bf16[8,3200]{1,0:T(8,128)(2,1)S(1)} %shard_map.64), channel_id=1, source_target_pairs={{0,12},{2,14},{4,0},{6,2},{8,4},{10,6},{12,8},{14,10},{1,13},{3,15... | collective-permute-start | bytes 153608 | tf_op jit(solution)/shard_map/ppermute | solution.py:221
  7.4 5.0 %collective-permute-start.1 = (bf16[8,3200]{1,0:T(8,128)(2,1)S(1)}, bf16[8,3200]{1,0:T(8,128)(2,1)S(1)}, u32[]{:S(2)}, u32[]{:S(2)}) collective-permute-start(bf16[8,3200]{1,0:T(8,128)(2,1)S(1)} %shard_map.64), channel_id=1, source_target_pairs={{0,8},{2,10},{4,12},{6,14},{8,0},{10,2},{12,4},{14,6},{1,9},{3,11}... | collective-permute-start | bytes 153608 | tf_op jit(solution)/shard_map/ppermute | solution.py:221
  7.4 5.9 %collective-permute-start = (bf16[8,3200]{1,0:T(8,128)(2,1)S(1)}, bf16[8,3200]{1,0:T(8,128)(2,1)S(1)}, u32[]{:S(2)}, u32[]{:S(2)}) collective-permute-start(bf16[8,3200]{1,0:T(8,128)(2,1)S(1)} %shard_map.64), channel_id=1, source_target_pairs={{0,4},{2,6},{4,8},{6,10},{8,12},{10,14},{12,0},{14,2},{1,5},{3,7},... | collective-permute-start | bytes 153608 | tf_op jit(solution)/shard_map/ppermute | solution.py:221
  13.3 2.3 %collective-permute-start.5 = (bf16[32,3200]{1,0:T(8,128)(2,1)S(1)}, bf16[32,3200]{1,0:T(8,128)(2,1)S(1)}, u32[]{:S(2)}, u32[]{:S(2)}) collective-permute-start(bf16[32,3200]{1,0:T(8,128)(2,1)S(1)} %pad_maximum_fusion.own), channel_id=1, source_target_pairs={{0,2},{2,0},{4,6},{6,4},{8,10},{10,8},{12,14},{14,12},{1,3},{3,1},... | collective-permute-start | bytes 614408 | tf_op jit(solution)/shard_map/ppermute | solution.py:223
  13.4 18.3 %collective-permute-start.4 = (bf16[32,3072]{1,0:T(8,128)(2,1)S(1)}, bf16[32,3072]{1,0:T(8,128)(2,1)S(1)}, u32[]{:S(2)}, u32[]{:S(2)}) collective-permute-start(bf16[32,3072]{1,0:T(8,128)(2,1)S(1)} %slice.23), channel_id=1, source_target_pairs={{0,3},{1,2},{2,1},{3,0},{4,7},{5,6},{6,5},{7,4},{8,11},{9,10},{10,... | collective-permute-start | bytes 589832 | tf_op jit(solution)/shard_map/ppermute | solution.py:228
  15.1 16.7 %collective-permute-start.3 = (bf16[32,3072]{1,0:T(8,128)(2,1)S(1)}, bf16[32,3072]{1,0:T(8,128)(2,1)S(1)}, u32[]{:S(2)}, u32[]{:S(2)}) collective-permute-start(bf16[32,3072]{1,0:T(8,128)(2,1)S(1)} %slice.23), channel_id=1, source_target_pairs={{0,1},{1,0},{2,3},{3,2},{4,5},{5,4},{6,7},{7,6},{8,9},{9,8},{10,11... | collective-permute-start | bytes 589832 | tf_op jit(solution)/shard_map/ppermute | solution.py:227
  54.7 9.0 %collective-permute-start.6 = (bf16[32,3072]{1,0:T(8,128)(2,1)S(1)}, bf16[32,3072]{1,0:T(8,128)(2,1)S(1)}, u32[]{:S(2)}, u32[]{:S(2)}) collective-permute-start(bf16[32,3072]{1,0:T(8,128)(2,1)S(1)} %get-tuple-element.14), channel_id=1, source_target_pairs={{0,1},{1,0},{2,3},{3,2},{4,5},{5,4},{6,7},{7,6},{8,9},{9,8},{10,11... | collective-permute-start | bytes 589832 | tf_op jit(solution)/shard_map/ppermute | solution.py:282
  56.3 8.3 %collective-permute-start.7 = (bf16[32,3072]{1,0:T(8,128)(2,1)S(1)}, bf16[32,3072]{1,0:T(8,128)(2,1)S(1)}, u32[]{:S(2)}, u32[]{:S(2)}) collective-permute-start(bf16[32,3072]{1,0:T(8,128)(2,1)S(1)} %get-tuple-element.15), channel_id=1, source_target_pairs={{0,3},{1,2},{2,1},{3,0},{4,7},{5,6},{6,5},{7,4},{8,11},{9,10},{10,... | collective-permute-start | bytes 589832 | tf_op jit(solution)/shard_map/ppermute | solution.py:283
  63.0 1.8 %collective-permute-start.8 = (bf16[32,3072]{1,0:T(8,128)(2,1)S(1)}, bf16[32,3072]{1,0:T(8,128)(2,1)S(1)}, u32[]{:S(2)}, u32[]{:S(2)}) collective-permute-start(bf16[32,3072]{1,0:T(8,128)(2,1)S(1)} %get-tuple-element.16), channel_id=1, source_target_pairs={{0,2},{2,0},{4,6},{6,4},{8,10},{10,8},{12,14},{14,12},{1,3},{3,1},... | collective-permute-start | bytes 589832 | tf_op jit(solution)/shard_map/ppermute | solution.py:285
  64.9 4.3 %collective-permute-start.9 = (bf16[8,3072]{1,0:T(8,128)(2,1)S(1)}, bf16[8,3072]{1,0:T(8,128)(2,1)S(1)}, u32[]{:S(2)}, u32[]{:S(2)}) collective-permute-start(bf16[8,3072]{1,0:T(8,128)(2,1)S(1)} %get-tuple-element.19), channel_id=1, source_target_pairs={{0,12},{2,14},{4,0},{6,2},{8,4},{10,6},{12,8},{14,10},{1,13},{3,15... | collective-permute-start | bytes 147464 | tf_op jit(solution)/shard_map/ppermute | solution.py:292
  66.4 6.4 %collective-permute-start.11 = (bf16[8,3072]{1,0:T(8,128)(2,1)S(1)}, bf16[8,3072]{1,0:T(8,128)(2,1)S(1)}, u32[]{:S(2)}, u32[]{:S(2)}) collective-permute-start(bf16[8,3072]{1,0:T(8,128)(2,1)S(1)} %get-tuple-element.20), channel_id=1, source_target_pairs={{0,4},{2,6},{4,8},{6,10},{8,12},{10,14},{12,0},{14,2},{1,5},{3,7},... | collective-permute-start | bytes 147464 | tf_op jit(solution)/shard_map/ppermute | solution.py:292
  67.0 6.7 %collective-permute-start.10 = (bf16[8,3072]{1,0:T(8,128)(2,1)S(1)}, bf16[8,3072]{1,0:T(8,128)(2,1)S(1)}, u32[]{:S(2)}, u32[]{:S(2)}) collective-permute-start(bf16[8,3072]{1,0:T(8,128)(2,1)S(1)} %get-tuple-element.21), channel_id=1, source_target_pairs={{0,8},{2,10},{4,12},{6,14},{8,0},{10,2},{12,4},{14,6},{1,9},{3,11}... | collective-permute-start | bytes 147464 | tf_op jit(solution)/shard_map/ppermute | solution.py:292
where the time goes:
time: 74.6 us; the launch traced here: 74.3 us
  Pallas kernels  45.9 us (62%)
  starting transfers between devices  14 us (19%)
  waiting for transfers between devices  11.4 us (15%)
  local copies, waits for them, and re-layouts  2.19 us (3%)
  other arithmetic  0.76 us (1%)
    pallas_call x5, Pallas kernels, call(): pl.pallas_call(kernel, out_shape=outs, in_specs=[pl.BlockSpec(memory_spac...  45.9 us
    ppermute x3, starting transfers between devices, body(): lax.ppermute(packed, 'expert', along(k))  6.11 us
    ppermute x3, waiting for transfers between devices, body(): mixed = mixed + lax.ppermute(piece, 'expert', along(-k)).astype(F32)  5.42 us
    ppermute x3, waiting for transfers between devices, body(): lax.ppermute(packed, 'expert', along(k))  4.9 us
    ppermute x3, starting transfers between devices, body(): mixed = mixed + lax.ppermute(piece, 'expert', along(-k)).astype(F32)  3.34 us
    unnamed x6, local copies, waits for them, and re-layouts  2.16 us
    ppermute x1, starting transfers between devices, body(): sent.append(lax.ppermute(bare, ('expert', 'blk'), across_other(-j)))  1.65 us
    ppermute x1, starting transfers between devices, body(): total.append(lax.ppermute(away[2 * j - 2], 'blk', across(j)))  1.56 us
  transfers between devices with their start and end apart: 12, of which 8 were waited for; matrix products, arithmetic and copies ran while one was open for 0% of the time, Pallas kernels for 31%

commit v1 on v0

v1 whole, which is shorter than its diff:
```python
import functools

import jax
import jax.numpy as jnp
from jax import lax
from jax.experimental import pallas as pl
from jax.experimental.pallas import tpu as pltpu
from jax.sharding import PartitionSpec as P

FFW = 5376
PAIR = 2
LANES = 128
SLOTS = 3
MIB = 1024 * 1024
F32 = jnp.float32
BF16 = jnp.bfloat16


def dot_rows(left, right):
    return lax.dot_general(left, right, (((1,), (1,)), ((), ())), preferred_element_type=F32)


def largest_step(total, choices):
    for step in choices:
        if total % step == 0:
            return step
    return total


def call(kernel, outs, operands, spaces, scratch, limit, flops, moved):
    return pl.pallas_call(
        kernel,
        out_shape=outs,
        in_specs=[pl.BlockSpec(memory_space=space) for space in spaces],
        out_specs=jax.tree.map(lambda unused: pl.BlockSpec(memory_space=pltpu.VMEM), outs),
        scratch_shapes=scratch,
        compiler_params=pltpu.CompilerParams(vmem_limit_bytes=limit * MIB),
        cost_estimate=pl.CostEstimate(flops=flops, bytes_accessed=moved, transcendentals=0),
    )(*operands)


def in_hbm(*arrays):
    return [pltpu.with_memory_space_constraint(array, pltpu.HBM) for array in arrays]


def stream(count, copies, begin, work):
    for step in range(min(SLOTS - 1, count)):
        for copy in copies(step, step):
            copy.start()
    begin()

    def one(step, carry):
        slot = lax.rem(step, SLOTS)
        later = step + SLOTS - 1

        @pl.when(later < count)
        def _():
            for copy in copies(later, lax.rem(later, SLOTS)):
                copy.start()

        work(step, slot, copies(step, slot))
        return carry

    lax.fori_loop(0, count, one, 0)


def pack_kernel(experts, tokens, ids, weights, out, held, named, weighed, sems):
    moves = [
        pltpu.make_async_copy(source, target, sems.at[at])
        for at, (source, target) in enumerate(((ids, named), (weights, weighed), (tokens, held)))
    ]
    for move in moves:
        move.start()
    rows, width = tokens.shape
    shape = (rows, out.shape[1] - width)
    lane = lax.broadcasted_iota(jnp.int32, shape, 1)
    diagonal = lax.broadcasted_iota(jnp.int32, (rows, rows), 0) == lax.broadcasted_iota(
        jnp.int32, (rows, rows), 1
    )
    coef = jnp.zeros(shape, F32)
    moves[0].wait()
    moves[1].wait()
    for k in range(ids.shape[0]):
        name = jnp.sum(jnp.where(diagonal, named[k : k + 1], 0), axis=1, keepdims=True)
        weight = jnp.sum(jnp.where(diagonal, weighed[k : k + 1], 0.0), axis=1, keepdims=True)
        coef += jnp.where(lax.rem(lane, experts) == name, weight, 0.0)
    high = coef.astype(BF16).astype(F32)
    middle = (coef - high).astype(BF16).astype(F32)
    low = coef - high - middle
    part = jnp.where(lane < experts, high, jnp.where(lane < 2 * experts, middle, low))
    out[:, width:] = jnp.where(lane < 3 * experts, part, 0.0).astype(BF16)
    moves[2].wait()
    out[:, :width] = held[...]


def up_kernel(hb, rows, width, experts, shares, gathered, w_gate, w_up, *refs):
    hidden, coef_out, x, zero, gate_buf, up_buf, sems = refs
    n_blk, tokens_all = x.shape[:2]
    device, n_expert = lax.axis_index("expert"), lax.axis_size("expert")
    places = n_expert // PAIR
    chunk = gathered.shape[1] // (n_expert * n_blk)

    def copies(step, slot):
        units = pl.ds(pl.multiple_of(step * hb, 8), hb)
        return [
            pltpu.make_async_copy(
                weight.at[0, units, pl.ds(j * width, width)],
                buf.at[slot, j],
                sems.at[place, slot, j],
            )
            for place, (weight, buf) in enumerate(((w_gate, gate_buf), (w_up, up_buf)))
            for j in range(n_blk)
        ]

    def owned(j, column, size):
        pieces = []
        for other in range(PAIR):
            core = lax.rem(device + other, PAIR)
            for k in range(places):
                place = lax.rem(device // PAIR + places - k, places)
                first = ((place * PAIR + core) * n_blk + j) * chunk + column
                pieces.append(gathered[:, pl.ds(pl.multiple_of(first, LANES), size)])
        return jnp.concatenate(pieces, axis=0)

    def begin():
        for j in range(n_blk):
            x[j] = owned(j, 0, width)
        packed = owned(0, width, chunk - width).astype(F32)
        lane = lax.broadcasted_iota(jnp.int32, packed.shape, 1)
        mine = (lax.rem(lane, experts) == device // shares) & (lane < 3 * experts)
        coef = jnp.sum(jnp.where(mine, packed, 0.0), axis=1, keepdims=True)
        coef_out[...] = jnp.broadcast_to(coef, coef_out.shape)
        zero[...] = jnp.zeros_like(zero)

    def work(step, slot, waits):
        gate_acc = up_acc = zero[...]
        for j in range(n_blk):
            waits[j].wait()
            gate_acc += dot_rows(gate_buf[slot, j], x[j])
        for j in range(n_blk):
            waits[n_blk + j].wait()
            up_acc += dot_rows(up_buf[slot, j], x[j])
        value = gate_acc / (1.0 + jnp.exp(-gate_acc)) * up_acc
        hidden[:, pl.ds(pl.multiple_of(step * hb, LANES), hb)] = value.T.astype(BF16)

    stream(w_gate.shape[1] // hb, copies, begin, work)


def down_kernel(fb, parts, hidden, coef, w_down, *refs):
    outs, (buf, sems) = refs[: len(parts)], refs[len(parts) :]
    width = outs[0].shape[1]
    here, cycle = lax.axis_index("blk"), lax.axis_size("blk")
    for part, out in zip(parts, outs):
        first = lax.rem(here + part, cycle) * width

        def copies(step, slot):
            columns = pl.ds(pl.multiple_of(first + step * fb, LANES), fb)
            return [pltpu.make_async_copy(w_down.at[0, :, columns], buf.at[slot], sems.at[slot])]

        def work(step, slot, waits):
            waits[0].wait()
            value = jnp.dot(hidden[...], buf[slot], preferred_element_type=F32) * coef[:, :1]
            columns = pl.ds(pl.multiple_of(step * fb, LANES), fb)
            out[:, columns] = value.astype(out.dtype)

        stream(width // fb, copies, lambda: None, work)


def body(tokens, expert_ids, route_weight, w_gate, w_up, w_down):
    n_expert = lax.axis_size("expert")
    n_blk = lax.axis_size("blk")
    rows, width = tokens.shape
    top = expert_ids.shape[1]
    hid, model = w_gate.shape[1:]
    shares = FFW // (hid * n_blk)
    experts = n_expert // shares
    places = n_expert // PAIR
    half = places * rows
    tokens_all = PAIR * half
    room = -(-3 * experts // LANES) * LANES
    vmem, hbm = pltpu.VMEM, pl.ANY
    w_gate, w_up, w_down = in_hbm(w_gate, w_up, w_down)

    packed = call(
        functools.partial(pack_kernel, experts),
        jax.ShapeDtypeStruct((rows, width + room), BF16),
        in_hbm(tokens, expert_ids.T, route_weight.T),
        (hbm,) * 3,
        [
            pltpu.VMEM((rows, width), BF16),
            pltpu.VMEM((top, rows), jnp.int32),
            pltpu.VMEM((top, rows), F32),
            pltpu.SemaphoreType.DMA((3,)),
        ],
        8,
        rows * room,
        4 * rows * width,
    )
    gathered = lax.all_gather(packed, ("expert", "blk"), axis=1, tiled=True)

    hb = largest_step(hid, (384,))
    hidden, coef = call(
        functools.partial(up_kernel, hb, rows, width, experts, shares),
        [
            jax.ShapeDtypeStruct((tokens_all, hid), BF16),
            jax.ShapeDtypeStruct((tokens_all, LANES), F32),
        ],
        (gathered, w_gate, w_up),
        (vmem, hbm, hbm),
        [
            pltpu.VMEM((n_blk, tokens_all, width), BF16),
            pltpu.VMEM((hb, tokens_all), F32),
            pltpu.VMEM((SLOTS, n_blk, hb, width), BF16),
            pltpu.VMEM((SLOTS, n_blk, hb, width), BF16),
            pltpu.SemaphoreType.DMA((2, SLOTS, n_blk)),
        ],
        40,
        4 * tokens_all * hid * model,
        4 * hid * model,
    )

    fb = largest_step(width, (512, 384, 256, 128))

    def down(parts, kind):
        return call(
            functools.partial(down_kernel, fb, parts),
            [jax.ShapeDtypeStruct((tokens_all, width), kind) for unused in parts],
            (hidden, coef, w_down),
            (vmem, vmem, hbm),
            [pltpu.VMEM((SLOTS, hid, fb), BF16), pltpu.SemaphoreType.DMA((SLOTS,))],
            20,
            2 * tokens_all * hid * width * len(parts),
            2 * hid * width * len(parts),
        )

    def along(k):
        return [(s, ((s // PAIR + k) % places) * PAIR + s % PAIR) for s in range(n_expert)]

    away = down(tuple(range(1, n_blk)), BF16)
    came = [
        lax.ppermute(part, "blk", [(s, (s + j) % n_blk) for s in range(n_blk)])
        for j, part in enumerate(away, 1)
    ]
    (summed,) = down((0,), F32)
    for part in came:
        summed = summed + part.astype(F32)
    given = lax.ppermute(
        summed[half:].astype(BF16), "expert", [(s, s ^ 1) for s in range(n_expert)]
    )
    summed = summed[:half] + given.astype(F32)
    mixed = summed[:rows]
    for k in range(1, places):
        piece = summed[k * rows : (k + 1) * rows].astype(BF16)
        mixed = mixed + lax.ppermute(piece, "expert", along(-k)).astype(F32)
    return mixed.astype(BF16)


def solution(mesh):
    placed = (
        P(("groups", "expert"), "blk"),
        P(("groups", "expert"), None),
        P(("groups", "expert"), None),
        P("expert", "blk", None),
        P("expert", "blk", None),
        P("expert", "blk", None),
    )
    return jax.shard_map(
        body, mesh=mesh, in_specs=placed, out_specs=P(("groups", "expert"), "blk"), check_vma=False
    )
```

time: 74.6 us -> 105 us (1.41)
  blocking collectives: 0 us -> 38.6 us
  starting transfers between devices: 14 us -> 2.22 us
  Pallas kernels: 45.9 us -> 52.7 us
  local copies, waits for them, and re-layouts: 2.19 us -> 0.03 us
  waiting for transfers between devices: 11.4 us -> 10.3 us
    all_gather x0 -> x1, blocking collectives: none -> 38.6 us  [body(): gathered = lax.all_gather(packed, ('expert', 'blk'), axis=1, tiled=True)]
    ppermute x9 -> x2, starting transfers between devices: 10.6 us -> 0.14 us  [the longest x1 0.07 us: body(): lax.ppermute(summed[half:].astype(BF16), 'expert', [(s, s ^ 1) for s in r...]
    pallas_call x5 -> x4, Pallas kernels: 45.9 us -> 52.7 us  [call(): pl.pallas_call(kernel, out_shape=outs, in_specs=[pl.BlockSpec(memory_spac...]
    unnamed x6 -> x0, local copies, waits for them, and re-layouts: 2.16 us -> none
    ppermute x9 -> x2, waiting for transfers between devices: 5.98 us -> 4.53 us  [the longest x1 3.1 us: body(): lax.ppermute(part, 'blk', [(s, (s + j) % n_blk) for s in range(n_blk)])]
    ppermute x3, starting transfers between devices: 3.34 us -> 2.07 us  [body(): mixed = mixed + lax.ppermute(piece, 'expert', along(-k)).astype(F32)]
  transfers between devices with their start and end apart: 12 -> 5, of which waited for: 8 -> 5; matrix products, arithmetic and copies ran while one was open for 0% -> 0% of each run, Pallas kernels for 31% -> 6%
where the time goes in v1:
time: 105 us
  Pallas kernels  52.7 us (50%)
  blocking collectives  38.6 us (37%)
  waiting for transfers between devices  10.3 us (10%)
  starting transfers between devices  2.22 us (2%)
    pallas_call x4, Pallas kernels, call(): pl.pallas_call(kernel, out_shape=outs, in_specs=[pl.BlockSpec(memory_spac...  52.7 us
    all_gather x1, blocking collectives, body(): gathered = lax.all_gather(packed, ('expert', 'blk'), axis=1, tiled=True)  38.6 us
    ppermute x3, waiting for transfers between devices, body(): mixed = mixed + lax.ppermute(piece, 'expert', along(-k)).astype(F32)  5.72 us
    ppermute x1, waiting for transfers between devices, body(): lax.ppermute(part, 'blk', [(s, (s + j) % n_blk) for s in range(n_blk)])  3.1 us
  transfers between devices with their start and end apart: 5, of which 5 were waited for; matrix products, arithmetic and copies ran while one was open for 0% of the time, Pallas kernels for 6%

profile of v1, /device:TPU:0, one launch (start us, length us, event | category | flops | bytes accessed | tf_op | source)
XLA Modules:
  0.0 104.6 jit_solution(12785005389410372756)
XLA Ops:
  0.0 0.9 shard_map.64
  0.9 38.6 %all_gather.3.gathered = bf16[8,51200]{1,0:T(8,128)(2,1)S(1)} all-gather(bf16[8,3200]{1,0:T(8,128)(2,1)S(1)} %shard_map.64), channel_id=1, replica_groups=mesh['groups'=2,'expert'=8,'blk'=2] {'expert','blk'}, dimensions={1}, use_global_device_ids=true | all-gather | bytes 870400 | tf_op jit(solution)/shard_map/all_gather | solution.py:199
  39.4 38.4 %shard_map.65 = (bf16[64,2688]{1,0:T(8,128)(2,1)S(1)}, f32[64,128]{1,0:T(8,128)S(1)}) custom-call(bf16[8,51200]{1,0:T(8,128)(2,1)S(1)} %all_gather.3.gathered, bf16[1,2688,6144]{2,1,0:T(8,128)(2,1)} %w_gate.1, bf16[1,2688,6144]{2,1,0:T(8,128)(2,1)} %w_up.1), custom_call_target="tpu_custom_call" | custom-call | flops 4227858432 | bytes 66060288 | tf_op jit(solution)/shard_map/pallas_call | solution.py:31
  77.8 6.7 %shard_map.67 = bf16[64,3072]{1,0:T(8,128)(2,1)S(1)} custom-call(bf16[64,2688]{1,0:T(8,128)(2,1)S(1)} %get-tuple-element.7.hidden, f32[64,128]{1,0:T(8,128)S(1)} %get-tuple-element.8.coef, bf16[1,2688,6144]{2,1,0:T(8,128)(2,1)} %w_down.3), custom_call_target="tpu_custom_call" | custom-call | flops 1056964608 | bytes 16515072 | tf_op jit(solution)/shard_map/pallas_call | solution.py:31
  84.6 0.1 collective-permute-start
  84.6 6.7 %shard_map.66 = f32[64,3072]{1,0:T(8,128)S(1)} custom-call(bf16[64,2688]{1,0:T(8,128)(2,1)S(1)} %get-tuple-element.7.hidden, f32[64,128]{1,0:T(8,128)S(1)} %get-tuple-element.8.coef, bf16[1,2688,6144]{2,1,0:T(8,128)(2,1)} %w_down.3), custom_call_target="tpu_custom_call" | custom-call | flops 1056964608 | bytes 16515072 | tf_op jit(solution)/shard_map/pallas_call | solution.py:31
  91.4 3.1 %collective-permute-done = bf16[64,3072]{1,0:T(8,128)(2,1)S(1)} collective-permute-done((bf16[64,3072]{1,0:T(8,128)(2,1)S(1)}, bf16[64,3072]{1,0:T(8,128)(2,1)S(1)}, u32[]{:S(2)}, u32[]{:S(2)}) %collective-permute-start) | collective-permute-done | bytes 393248 | tf_op jit(solution)/shard_map/ppermute | solution.py:241
  94.5 0.1 convert_add_fusion
  94.6 0.1 collective-permute-start.1
  94.7 1.4 %collective-permute-done.1 = bf16[32,3072]{1,0:T(8,128)(2,1)S(1)} collective-permute-done((bf16[32,3072]{1,0:T(8,128)(2,1)S(1)}, bf16[32,3072]{1,0:T(8,128)(2,1)S(1)}, u32[]{:S(2)}, u32[]{:S(2)}) %collective-permute-start.1) | collective-permute-done | bytes 196640 | tf_op jit(solution)/shard_map/ppermute | solution.py:247
  96.1 0.1 fusion.3
  96.2 0.1 collective-permute-start.2
  96.2 2.0 %collective-permute-start.4 = (bf16[8,3072]{1,0:T(8,128)(2,1)S(1)}, bf16[8,3072]{1,0:T(8,128)(2,1)S(1)}, u32[]{:S(2)}, u32[]{:S(2)}) collective-permute-start(bf16[8,3072]{1,0:T(8,128)(2,1)S(1)} %get-tuple-element.12), channel_id=1, source_target_pairs={{0,4},{2,6},{4,8},{6,10},{8,12},{10,14},{12,0},{14,2},{1,5},{3,7},... | collective-permute-start | bytes 147464 | tf_op jit(solution)/shard_map/ppermute | solution.py:254
  98.2 0.0 collective-permute-start.3
  98.2 2.1 %collective-permute-done.2 = bf16[8,3072]{1,0:T(8,128)(2,1)S(1)} collective-permute-done((bf16[8,3072]{1,0:T(8,128)(2,1)S(1)}, bf16[8,3072]{1,0:T(8,128)(2,1)S(1)}, u32[]{:S(2)}, u32[]{:S(2)}) %collective-permute-start.2) | collective-permute-done | bytes 49184 | tf_op jit(solution)/shard_map/ppermute | solution.py:254
  100.3 2.2 %collective-permute-done.4 = bf16[8,3072]{1,0:T(8,128)(2,1)S(1)} collective-permute-done((bf16[8,3072]{1,0:T(8,128)(2,1)S(1)}, bf16[8,3072]{1,0:T(8,128)(2,1)S(1)}, u32[]{:S(2)}, u32[]{:S(2)}) %collective-permute-start.4) | collective-permute-done | bytes 49184 | tf_op jit(solution)/shard_map/ppermute | solution.py:254
  102.5 1.5 %collective-permute-done.3 = bf16[8,3072]{1,0:T(8,128)(2,1)S(1)} collective-permute-done((bf16[8,3072]{1,0:T(8,128)(2,1)S(1)}, bf16[8,3072]{1,0:T(8,128)(2,1)S(1)}, u32[]{:S(2)}, u32[]{:S(2)}) %collective-permute-start.3) | collective-permute-done | bytes 49184 | tf_op jit(solution)/shard_map/ppermute | solution.py:254
  104.0 0.6 fusion.2
  (2 shorter events, 0.0 us)
Async XLA Ops:
  84.6 9.9 %collective-permute-start = (bf16[64,3072]{1,0:T(8,128)(2,1)S(1)}, bf16[64,3072]{1,0:T(8,128)(2,1)S(1)}, u32[]{:S(2)}, u32[]{:S(2)}) collective-permute-start(bf16[64,3072]{1,0:T(8,128)(2,1)S(1)} %shard_map.67), channel_id=1, source_target_pairs={{0,1},{1,0},{2,3},{3,2},{4,5},{5,4},{6,7},{7,6},{8,9},{9,8},{10,11... | collective-permute-start | bytes 1179656 | tf_op jit(solution)/shard_map/ppermute | solution.py:241
  94.6 1.5 %collective-permute-start.1 = (bf16[32,3072]{1,0:T(8,128)(2,1)S(1)}, bf16[32,3072]{1,0:T(8,128)(2,1)S(1)}, u32[]{:S(2)}, u32[]{:S(2)}) collective-permute-start(bf16[32,3072]{1,0:T(8,128)(2,1)S(1)} %slice.43), channel_id=1, source_target_pairs={{0,2},{2,0},{4,6},{6,4},{8,10},{10,8},{12,14},{14,12},{1,3},{3,1},... | collective-permute-start | bytes 589832 | tf_op jit(solution)/shard_map/ppermute | solution.py:247
  96.2 4.1 %collective-permute-start.2 = (bf16[8,3072]{1,0:T(8,128)(2,1)S(1)}, bf16[8,3072]{1,0:T(8,128)(2,1)S(1)}, u32[]{:S(2)}, u32[]{:S(2)}) collective-permute-start(bf16[8,3072]{1,0:T(8,128)(2,1)S(1)} %get-tuple-element.11), channel_id=1, source_target_pairs={{0,12},{2,14},{4,0},{6,2},{8,4},{10,6},{12,8},{14,10},{1,13},{3,15... | collective-permute-start | bytes 147464 | tf_op jit(solution)/shard_map/ppermute | solution.py:254
  96.2 6.3 %collective-permute-start.4 = (bf16[8,3072]{1,0:T(8,128)(2,1)S(1)}, bf16[8,3072]{1,0:T(8,128)(2,1)S(1)}, u32[]{:S(2)}, u32[]{:S(2)}) collective-permute-start(bf16[8,3072]{1,0:T(8,128)(2,1)S(1)} %get-tuple-element.12), channel_id=1, source_target_pairs={{0,4},{2,6},{4,8},{6,10},{8,12},{10,14},{12,0},{14,2},{1,5},{3,7},... | collective-permute-start | bytes 147464 | tf_op jit(solution)/shard_map/ppermute | solution.py:254
  98.2 5.7 %collective-permute-start.3 = (bf16[8,3072]{1,0:T(8,128)(2,1)S(1)}, bf16[8,3072]{1,0:T(8,128)(2,1)S(1)}, u32[]{:S(2)}, u32[]{:S(2)}) collective-permute-start(bf16[8,3072]{1,0:T(8,128)(2,1)S(1)} %get-tuple-element.13), channel_id=1, source_target_pairs={{0,8},{2,10},{4,12},{6,14},{8,0},{10,2},{12,4},{14,6},{1,9},{3,11}... | collective-permute-start | bytes 147464 | tf_op jit(solution)/shard_map/ppermute | solution.py:254

commit v2 on v1

v2 whole, which is shorter than its diff:
```python
import functools

import jax
import jax.numpy as jnp
from jax import lax
from jax.experimental import pallas as pl
from jax.experimental.pallas import tpu as pltpu
from jax.sharding import PartitionSpec as P

FFW = 5376
PAIR = 2
LANES = 128
SLOTS = 3
MIB = 1024 * 1024
F32 = jnp.float32
BF16 = jnp.bfloat16


def largest_step(total, choices):
    for step in choices:
        if total % step == 0:
            return step
    return total


def call(kernel, outs, operands, spaces, scratch, limit, flops, moved):
    return pl.pallas_call(
        kernel,
        out_shape=outs,
        in_specs=[pl.BlockSpec(memory_space=space) for space in spaces],
        out_specs=jax.tree.map(lambda unused: pl.BlockSpec(memory_space=pltpu.VMEM), outs),
        scratch_shapes=scratch,
        compiler_params=pltpu.CompilerParams(vmem_limit_bytes=limit * MIB),
        cost_estimate=pl.CostEstimate(flops=flops, bytes_accessed=moved, transcendentals=0),
    )(*operands)


def in_hbm(*arrays):
    return [pltpu.with_memory_space_constraint(array, pltpu.HBM) for array in arrays]


def stream(count, copies, begin, work):
    for step in range(min(SLOTS - 1, count)):
        for copy in copies(step, step):
            copy.start()
    begin()

    def one(step, carry):
        slot = lax.rem(step, SLOTS)
        later = step + SLOTS - 1

        @pl.when(later < count)
        def _():
            for copy in copies(later, lax.rem(later, SLOTS)):
                copy.start()

        work(step, slot, copies(step, slot))
        return carry

    lax.fori_loop(0, count, one, 0)


def pack_kernel(experts, tokens, ids, weights, out, held, named, weighed, sems):
    moves = [
        pltpu.make_async_copy(source, target, sems.at[at])
        for at, (source, target) in enumerate(((ids, named), (weights, weighed), (tokens, held)))
    ]
    for move in moves:
        move.start()
    rows, width = tokens.shape
    shape = (rows, out.shape[1] - width)
    lane = lax.broadcasted_iota(jnp.int32, shape, 1)
    diagonal = lax.broadcasted_iota(jnp.int32, (rows, rows), 0) == lax.broadcasted_iota(
        jnp.int32, (rows, rows), 1
    )
    coef = jnp.zeros(shape, F32)
    moves[0].wait()
    moves[1].wait()
    for k in range(ids.shape[0]):
        name = jnp.sum(jnp.where(diagonal, named[k : k + 1], 0), axis=1, keepdims=True)
        weight = jnp.sum(jnp.where(diagonal, weighed[k : k + 1], 0.0), axis=1, keepdims=True)
        coef += jnp.where(lax.rem(lane, experts) == name, weight, 0.0)
    high = coef.astype(BF16).astype(F32)
    middle = (coef - high).astype(BF16).astype(F32)
    low = coef - high - middle
    part = jnp.where(lane < experts, high, jnp.where(lane < 2 * experts, middle, low))
    out[:, width:] = jnp.where(lane < 3 * experts, part, 0.0).astype(BF16)
    moves[2].wait()
    out[:, :width] = held[...]


def up_kernel(kb, parts, last, *refs):
    sent, refs = refs[: 2 * len(parts)], refs[2 * len(parts) :]
    held, refs = (refs[:2], refs[2:]) if last else ((), refs)
    w_gate, w_up = refs[:2]
    outs, (x, gate_buf, up_buf, sems, *sums) = (refs[2:3], refs[3:]) if last else (refs[2:4], refs[4:])
    gate_sum, up_sum = sums if last else outs
    half, hid = sent[0].shape[0], w_gate.shape[1]
    width = x.shape[0] // len(parts)
    per = width // kb
    here, cycle = lax.axis_index("blk"), lax.axis_size("blk")

    def copies(step, slot):
        owner = lax.rem(here + parts[0] + step // per, cycle)
        columns = pl.ds(pl.multiple_of(owner * width + lax.rem(step, per) * kb, LANES), kb)
        return [
            pltpu.make_async_copy(w_gate.at[0, :, columns], gate_buf.at[slot], sems.at[0, slot]),
            pltpu.make_async_copy(w_up.at[0, :, columns], up_buf.at[slot], sems.at[1, slot]),
        ]

    def begin():
        for j in range(len(parts)):
            rows = [sent[2 * j + at][:, :width].astype(F32) for at in range(2)]
            x[j * width : (j + 1) * width] = jnp.concatenate(rows, axis=0).T.astype(BF16)
        gate_sum[...] = held[0][...] if last else jnp.zeros_like(gate_sum)
        up_sum[...] = held[1][...] if last else jnp.zeros_like(up_sum)

    def work(step, slot, waits):
        right = x[pl.ds(pl.multiple_of(step * kb, LANES), kb)]
        waits[0].wait()
        gate_sum[...] += jnp.dot(gate_buf[slot], right, preferred_element_type=F32)
        waits[1].wait()
        up_sum[...] += jnp.dot(up_buf[slot], right, preferred_element_type=F32)

    stream(len(parts) * per, copies, begin, work)
    if last:
        unit = largest_step(hid, (384,))
        for first in range(0, hid, unit):
            units = pl.ds(first, unit)
            gate = gate_sum[units]
            value = gate / (1.0 + jnp.exp(-gate)) * up_sum[units]
            outs[0][:, units] = value.T.astype(BF16)


def down_kernel(fb, parts, experts, shares, hidden, own, other, w_down, *refs):
    outs, (buf, sems) = refs[: 2 * len(parts)], refs[2 * len(parts) :]
    half, width = outs[0].shape
    here, cycle = lax.axis_index("blk"), lax.axis_size("blk")
    expert = lax.axis_index("expert") // shares
    packed = jnp.concatenate([own[:, width:], other[:, width:]], axis=0).astype(F32)
    lane = lax.broadcasted_iota(jnp.int32, packed.shape, 1)
    mine = (lax.rem(lane, experts) == expert) & (lane < 3 * experts)
    coef = jnp.sum(jnp.where(mine, packed, 0.0), axis=1, keepdims=True)
    for place, part in enumerate(parts):
        first = lax.rem(here + part, cycle) * width

        def copies(step, slot):
            columns = pl.ds(pl.multiple_of(first + step * fb, LANES), fb)
            return [pltpu.make_async_copy(w_down.at[0, :, columns], buf.at[slot], sems.at[slot])]

        def work(step, slot, waits):
            waits[0].wait()
            value = jnp.dot(hidden[...], buf[slot], preferred_element_type=F32) * coef
            columns = pl.ds(pl.multiple_of(step * fb, LANES), fb)
            for at in range(2):
                out = outs[2 * place + at]
                out[:, columns] = value[at * half : (at + 1) * half].astype(out.dtype)

        stream(width // fb, copies, lambda: None, work)


def body(tokens, expert_ids, route_weight, w_gate, w_up, w_down):
    n_expert = lax.axis_size("expert")
    n_blk = lax.axis_size("blk")
    rows, width = tokens.shape
    top = expert_ids.shape[1]
    hid = w_gate.shape[1]
    shares = FFW // (hid * n_blk)
    experts = n_expert // shares
    places = n_expert // PAIR
    half = places * rows
    tokens_all = PAIR * half
    room = -(-3 * experts // LANES) * LANES
    vmem, hbm = pltpu.VMEM, pl.ANY
    w_gate, w_up, w_down = in_hbm(w_gate, w_up, w_down)

    packed = call(
        functools.partial(pack_kernel, experts),
        jax.ShapeDtypeStruct((rows, width + room), BF16),
        in_hbm(tokens, expert_ids.T, route_weight.T),
        (hbm,) * 3,
        [
            pltpu.VMEM((rows, width), BF16),
            pltpu.VMEM((top, rows), jnp.int32),
            pltpu.VMEM((top, rows), F32),
            pltpu.SemaphoreType.DMA((3,)),
        ],
        8,
        rows * room,
        4 * rows * width,
    )

    def along(k):
        return [(s, ((s // PAIR + k) % places) * PAIR + s % PAIR) for s in range(n_expert)]

    def across(k):
        return [(s, (s + k) % n_blk) for s in range(n_blk)]

    def across_other(k):
        return [
            (s * n_blk + b, (s ^ 1) * n_blk + (b + k) % n_blk)
            for s in range(n_expert)
            for b in range(n_blk)
        ]

    swap = [(s, s ^ 1) for s in range(n_expert)]

    pieces = [packed] + [lax.ppermute(packed, "expert", along(k)) for k in range(1, places)]
    own = jnp.concatenate(pieces, axis=0)
    other = lax.ppermute(own, "expert", swap)
    bare = own[:, :width]
    sent = []
    for j in range(1, n_blk):
        sent.append(lax.ppermute(bare, "blk", across(-j)))
        sent.append(lax.ppermute(bare, ("expert", "blk"), across_other(-j)))

    kb = largest_step(width, (512, 384, 256, 128))
    sums = [jax.ShapeDtypeStruct((hid, tokens_all), F32)] * 2

    def up(parts, last, outs, operands):
        return call(
            functools.partial(up_kernel, kb, parts, last),
            outs,
            (*operands, w_gate, w_up),
            (vmem,) * len(operands) + (hbm, hbm),
            [
                pltpu.VMEM((width * len(parts), tokens_all), BF16),
                pltpu.VMEM((SLOTS, hid, kb), BF16),
                pltpu.VMEM((SLOTS, hid, kb), BF16),
                pltpu.SemaphoreType.DMA((2, SLOTS)),
            ]
            + [pltpu.VMEM(each.shape, F32) for each in sums if last],
            32,
            4 * tokens_all * hid * width * len(parts),
            4 * hid * width * len(parts),
        )

    partial_sums = up((0,), False, sums, (own, other))
    hidden = up(
        tuple(range(1, n_blk)),
        True,
        jax.ShapeDtypeStruct((tokens_all, hid), BF16),
        (*sent, *partial_sums),
    )

    fb = largest_step(width, (512, 384, 256, 128))

    def down(parts, kinds):
        return call(
            functools.partial(down_kernel, fb, parts, experts, shares),
            [jax.ShapeDtypeStruct((half, width), kind) for unused in parts for kind in kinds],
            (hidden, own, other, w_down),
            (vmem, vmem, vmem, hbm),
            [pltpu.VMEM((SLOTS, hid, fb), BF16), pltpu.SemaphoreType.DMA((SLOTS,))],
            20,
            2 * tokens_all * hid * width * len(parts),
            2 * hid * width * len(parts),
        )

    away = down(tuple(range(1, n_blk)), (BF16, BF16))
    total = []
    for j in range(1, n_blk):
        total.append(lax.ppermute(away[2 * j - 2], "blk", across(j)))
        total.append(lax.ppermute(away[2 * j - 1], ("expert", "blk"), across_other(j)))
    kept, given = down((0,), (F32, BF16))
    total.append(lax.ppermute(given, "expert", swap))
    summed = kept
    for term in total:
        summed = summed + term.astype(F32)
    mixed = summed[:rows]
    for k in range(1, places):
        piece = summed[k * rows : (k + 1) * rows].astype(BF16)
        mixed = mixed + lax.ppermute(piece, "expert", along(-k)).astype(F32)
    return mixed.astype(BF16)


def solution(mesh):
    placed = (
        P(("groups", "expert"), "blk"),
        P(("groups", "expert"), None),
        P(("groups", "expert"), None),
        P("expert", "blk", None),
        P("expert", "blk", None),
        P("expert", "blk", None),
    )
    return jax.shard_map(
        body, mesh=mesh, in_specs=placed, out_specs=P(("groups", "expert"), "blk"), check_vma=False
    )
```

time: 105 us -> 66.5 us (0.63)
  blocking collectives: 38.6 us -> 0 us
  Pallas kernels: 52.7 us -> 40 us
  starting transfers between devices: 2.22 us -> 14 us
  waiting for transfers between devices: 10.3 us -> 11.4 us
    all_gather x1 -> x0, blocking collectives: 38.6 us -> none  [body(): gathered = lax.all_gather(packed, ('expert', 'blk'), axis=1, tiled=True)]
    pallas_call x4 -> x5, Pallas kernels: 52.7 us -> 40 us  [call(): pl.pallas_call(kernel, out_shape=outs, in_specs=[pl.BlockSpec(memory_spac...]
    ppermute x2 -> x9, starting transfers between devices: 0.14 us -> 10.6 us  [the longest x3 6.11 us: body(): lax.ppermute(packed, 'expert', along(k))]
    ppermute x2 -> x9, waiting for transfers between devices: 4.53 us -> 5.98 us  [the longest x3 4.9 us: body(): lax.ppermute(packed, 'expert', along(k))]
    ppermute x3, starting transfers between devices: 2.07 us -> 3.32 us  [body(): mixed = mixed + lax.ppermute(piece, 'expert', along(-k)).astype(F32)]
  transfers between devices with their start and end apart: 5 -> 12, of which waited for: 5 -> 8; matrix products, arithmetic and copies ran while one was open for 0% -> 0% of each run, Pallas kernels for 6% -> 29%
where the time goes in v2:
time: 66.5 us; the launch traced here: 66.3 us
  Pallas kernels  40 us (60%)
  starting transfers between devices  14 us (21%)
  waiting for transfers between devices  11.4 us (17%)
  other arithmetic  0.76 us (1%)
    pallas_call x5, Pallas kernels, call(): pl.pallas_call(kernel, out_shape=outs, in_specs=[pl.BlockSpec(memory_spac...  40 us
    ppermute x3, starting transfers between devices, body(): lax.ppermute(packed, 'expert', along(k))  6.11 us
    ppermute x3, waiting for transfers between devices, body(): mixed = mixed + lax.ppermute(piece, 'expert', along(-k)).astype(F32)  5.44 us
    ppermute x3, waiting for transfers between devices, body(): lax.ppermute(packed, 'expert', along(k))  4.9 us
    ppermute x3, starting transfers between devices, body(): mixed = mixed + lax.ppermute(piece, 'expert', along(-k)).astype(F32)  3.32 us
    ppermute x1, starting transfers between devices, body(): sent.append(lax.ppermute(bare, ('expert', 'blk'), across_other(-j)))  1.65 us
    ppermute x1, starting transfers between devices, body(): total.append(lax.ppermute(away[2 * j - 2], 'blk', across(j)))  1.55 us
  transfers between devices with their start and end apart: 12, of which 8 were waited for; matrix products, arithmetic and copies ran while one was open for 0% of the time, Pallas kernels for 29%

profile of v2, /device:TPU:0, one launch (start us, length us, event | category | flops | bytes accessed | tf_op | source)
XLA Modules:
  0.0 66.3 jit_solution(13800001316847288224)
XLA Ops:
  0.0 0.9 %shard_map.64 = bf16[8,3200]{1,0:T(8,128)(2,1)S(1)} custom-call(bf16[8,3072]{1,0:T(8,128)(2,1)} %tokens.1, s32[4,8]{1,0:T(4,128)} %bitcast.2, f32[4,8]{1,0:T(4,128)} %bitcast.3), custom_call_target="tpu_custom_call" | custom-call | flops 1024 | bytes 98304 | tf_op jit(solution)/shard_map/pallas_call | solution.py:27
  0.9 5.1 %collective-permute-start.2 = (bf16[8,3200]{1,0:T(8,128)(2,1)S(1)}, bf16[8,3200]{1,0:T(8,128)(2,1)S(1)}, u32[]{:S(2)}, u32[]{:S(2)}) collective-permute-start(bf16[8,3200]{1,0:T(8,128)(2,1)S(1)} %shard_map.64), channel_id=1, source_target_pairs={{0,12},{2,14},{4,0},{6,2},{8,4},{10,6},{12,8},{14,10},{1,13},{3,15... | collective-permute-start | bytes 153608 | tf_op jit(solution)/shard_map/ppermute | solution.py:208
  6.0 0.0 collective-permute-start.1
  6.0 1.0 %collective-permute-start = (bf16[8,3200]{1,0:T(8,128)(2,1)S(1)}, bf16[8,3200]{1,0:T(8,128)(2,1)S(1)}, u32[]{:S(2)}, u32[]{:S(2)}) collective-permute-start(bf16[8,3200]{1,0:T(8,128)(2,1)S(1)} %shard_map.64), channel_id=1, source_target_pairs={{0,4},{2,6},{4,8},{6,10},{8,12},{10,14},{12,0},{14,2},{1,5},{3,7},... | collective-permute-start | bytes 153608 | tf_op jit(solution)/shard_map/ppermute | solution.py:208
  7.0 1.2 %collective-permute-done.2 = bf16[8,3200]{1,0:T(8,128)(2,1)S(1)} collective-permute-done((bf16[8,3200]{1,0:T(8,128)(2,1)S(1)}, bf16[8,3200]{1,0:T(8,128)(2,1)S(1)}, u32[]{:S(2)}, u32[]{:S(2)}) %collective-permute-start.2) | collective-permute-done | bytes 51232 | tf_op jit(solution)/shard_map/ppermute | solution.py:208
  8.1 2.9 %collective-permute-done.1 = bf16[8,3200]{1,0:T(8,128)(2,1)S(1)} collective-permute-done((bf16[8,3200]{1,0:T(8,128)(2,1)S(1)}, bf16[8,3200]{1,0:T(8,128)(2,1)S(1)}, u32[]{:S(2)}, u32[]{:S(2)}) %collective-permute-start.1) | collective-permute-done | bytes 51232 | tf_op jit(solution)/shard_map/ppermute | solution.py:208
  11.0 0.9 %collective-permute-done = bf16[8,3200]{1,0:T(8,128)(2,1)S(1)} collective-permute-done((bf16[8,3200]{1,0:T(8,128)(2,1)S(1)}, bf16[8,3200]{1,0:T(8,128)(2,1)S(1)}, u32[]{:S(2)}, u32[]{:S(2)}) %collective-permute-start) | collective-permute-done | bytes 51232 | tf_op jit(solution)/shard_map/ppermute | solution.py:208
  11.9 0.1 collective-permute-start.5
  12.0 1.7 %collective-permute-start.4 = (bf16[32,3072]{1,0:T(8,128)(2,1)S(1)}, bf16[32,3072]{1,0:T(8,128)(2,1)S(1)}, u32[]{:S(2)}, u32[]{:S(2)}) collective-permute-start(bf16[32,3072]{1,0:T(8,128)(2,1)S(1)} %slice.23), channel_id=1, source_target_pairs={{0,3},{1,2},{2,1},{3,0},{4,7},{5,6},{6,5},{7,4},{8,11},{9,10},{10,... | collective-permute-start | bytes 589832 | tf_op jit(solution)/shard_map/ppermute | solution.py:215
  13.7 0.5 collective-permute-start.3
  14.2 0.0 collective-permute-done.5.refs_1_.other
  14.2 12.6 %shard_map.65 = (f32[2688,64]{1,0:T(8,128)S(1)}, f32[2688,64]{1,0:T(8,128)S(1)}) custom-call(bf16[32,3200]{1,0:T(8,128)(2,1)S(1)} %pad_maximum_fusion.refs_0_.own, bf16[32,3200]{1,0:T(8,128)(2,1)S(1)} %collective-permute-done.5.refs_1_.other, bf16[1,2688,6144]{2,1,0:T(8,128)(2,1)} %refs_4_.1, bf16[1,2688,6144]{2,1,0:T(8,128)(2,1)} %refs_5_.1), custom_call_target="tpu_custom_call" | custom-call | flops 2113929216 | bytes 33030144 | tf_op jit(solution)/shard_map/pallas_call | solution.py:27
  26.8 0.0 collective-permute-done.4.refs_1_
  26.9 0.0 collective-permute-done.3.refs_0_
  26.9 13.1 %shard_map.66.hidden = bf16[64,2688]{1,0:T(8,128)(2,1)S(1)} custom-call(bf16[32,3072]{1,0:T(8,128)(2,1)S(1)} %collective-permute-done.3.refs_0_, bf16[32,3072]{1,0:T(8,128)(2,1)S(1)} %collective-permute-done.4.refs_1_, f32[2688,64]{1,0:T(8,128)S(1)} %get-tuple-element.11.refs_2_, f32[2688,64]{1,0:T(8,128)S(1)} %get-tuple-element.12.refs_3_, ...), custom_call_target="tpu_custom_call" | custom-call | flops 2113929216 | bytes 33030144 | tf_op jit(solution)/shard_map/pallas_call | solution.py:27
  40.0 6.7 %shard_map.68 = (bf16[32,3072]{1,0:T(8,128)(2,1)S(1)}, bf16[32,3072]{1,0:T(8,128)(2,1)S(1)}) custom-call(bf16[64,2688]{1,0:T(8,128)(2,1)S(1)} %shard_map.66.hidden, bf16[32,3200]{1,0:T(8,128)(2,1)S(1)} %pad_maximum_fusion.refs_0_.own, bf16[32,3200]{1,0:T(8,128)(2,1)S(1)} %collective-permute-done.5.refs_1_.other, bf16[1,2688,6144]{2,1,0:T(8,128)(2,1)} %w_down.3), custom_call_target="tpu_custom_call" | custom-call | flops 1056964608 | bytes 16515072 | tf_op jit(solution)/shard_map/pallas_call | solution.py:27
  46.7 1.6 %collective-permute-start.6 = (bf16[32,3072]{1,0:T(8,128)(2,1)S(1)}, bf16[32,3072]{1,0:T(8,128)(2,1)S(1)}, u32[]{:S(2)}, u32[]{:S(2)}) collective-permute-start(bf16[32,3072]{1,0:T(8,128)(2,1)S(1)} %get-tuple-element.14), channel_id=1, source_target_pairs={{0,1},{1,0},{2,3},{3,2},{4,5},{5,4},{6,7},{7,6},{8,9},{9,8},{10,11... | collective-permute-start | bytes 589832 | tf_op jit(solution)/shard_map/ppermute | solution.py:263
  48.3 0.0 collective-permute-start.7
  48.3 6.7 %shard_map.67 = (f32[32,3072]{1,0:T(8,128)S(1)}, bf16[32,3072]{1,0:T(8,128)(2,1)S(1)}) custom-call(bf16[64,2688]{1,0:T(8,128)(2,1)S(1)} %shard_map.66.hidden, bf16[32,3200]{1,0:T(8,128)(2,1)S(1)} %pad_maximum_fusion.refs_0_.own, bf16[32,3200]{1,0:T(8,128)(2,1)S(1)} %collective-permute-done.5.refs_1_.other, bf16[1,2688,6144]{2,1,0:T(8,128)(2,1)} %w_down.3), custom_call_target="tpu_custom_call" | custom-call | flops 1056964608 | bytes 16515072 | tf_op jit(solution)/shard_map/pallas_call | solution.py:27
  55.0 0.7 %collective-permute-start.8 = (bf16[32,3072]{1,0:T(8,128)(2,1)S(1)}, bf16[32,3072]{1,0:T(8,128)(2,1)S(1)}, u32[]{:S(2)}, u32[]{:S(2)}) collective-permute-start(bf16[32,3072]{1,0:T(8,128)(2,1)S(1)} %get-tuple-element.16), channel_id=1, source_target_pairs={{0,2},{2,0},{4,6},{6,4},{8,10},{10,8},{12,14},{14,12},{1,3},{3,1},... | collective-permute-start | bytes 589832 | tf_op jit(solution)/shard_map/ppermute | solution.py:266
  55.7 0.0 collective-permute-done.6
  55.7 0.8 %collective-permute-done.7 = bf16[32,3072]{1,0:T(8,128)(2,1)S(1)} collective-permute-done((bf16[32,3072]{1,0:T(8,128)(2,1)S(1)}, bf16[32,3072]{1,0:T(8,128)(2,1)S(1)}, u32[]{:S(2)}, u32[]{:S(2)}) %collective-permute-start.7) | collective-permute-done | bytes 196640 | tf_op jit(solution)/shard_map/ppermute | solution.py:264
  56.5 0.2 collective-permute-done.8
  56.8 0.1 fusion.3
  56.9 1.5 %collective-permute-start.9 = (bf16[8,3072]{1,0:T(8,128)(2,1)S(1)}, bf16[8,3072]{1,0:T(8,128)(2,1)S(1)}, u32[]{:S(2)}, u32[]{:S(2)}) collective-permute-start(bf16[8,3072]{1,0:T(8,128)(2,1)S(1)} %get-tuple-element.19), channel_id=1, source_target_pairs={{0,12},{2,14},{4,0},{6,2},{8,4},{10,6},{12,8},{14,10},{1,13},{3,15... | collective-permute-start | bytes 147464 | tf_op jit(solution)/shard_map/ppermute | solution.py:273
  58.3 0.6 collective-permute-start.11
  59.0 1.2 %collective-permute-start.10 = (bf16[8,3072]{1,0:T(8,128)(2,1)S(1)}, bf16[8,3072]{1,0:T(8,128)(2,1)S(1)}, u32[]{:S(2)}, u32[]{:S(2)}) collective-permute-start(bf16[8,3072]{1,0:T(8,128)(2,1)S(1)} %get-tuple-element.21), channel_id=1, source_target_pairs={{0,8},{2,10},{4,12},{6,14},{8,0},{10,2},{12,4},{14,6},{1,9},{3,11}... | collective-permute-start | bytes 147464 | tf_op jit(solution)/shard_map/ppermute | solution.py:273
  60.2 1.0 %collective-permute-done.9 = bf16[8,3072]{1,0:T(8,128)(2,1)S(1)} collective-permute-done((bf16[8,3072]{1,0:T(8,128)(2,1)S(1)}, bf16[8,3072]{1,0:T(8,128)(2,1)S(1)}, u32[]{:S(2)}, u32[]{:S(2)}) %collective-permute-start.9) | collective-permute-done | bytes 49184 | tf_op jit(solution)/shard_map/ppermute | solution.py:273
  61.2 3.5 %collective-permute-done.11 = bf16[8,3072]{1,0:T(8,128)(2,1)S(1)} collective-permute-done((bf16[8,3072]{1,0:T(8,128)(2,1)S(1)}, bf16[8,3072]{1,0:T(8,128)(2,1)S(1)}, u32[]{:S(2)}, u32[]{:S(2)}) %collective-permute-start.11) | collective-permute-done | bytes 49184 | tf_op jit(solution)/shard_map/ppermute | solution.py:273
  64.7 1.0 %collective-permute-done.10 = bf16[8,3072]{1,0:T(8,128)(2,1)S(1)} collective-permute-done((bf16[8,3072]{1,0:T(8,128)(2,1)S(1)}, bf16[8,3072]{1,0:T(8,128)(2,1)S(1)}, u32[]{:S(2)}, u32[]{:S(2)}) %collective-permute-start.10) | collective-permute-done | bytes 49184 | tf_op jit(solution)/shard_map/ppermute | solution.py:273
  65.7 0.6 fusion.2
  (3 shorter events, 0.0 us)
Async XLA Ops:
  0.9 7.3 %collective-permute-start.2 = (bf16[8,3200]{1,0:T(8,128)(2,1)S(1)}, bf16[8,3200]{1,0:T(8,128)(2,1)S(1)}, u32[]{:S(2)}, u32[]{:S(2)}) collective-permute-start(bf16[8,3200]{1,0:T(8,128)(2,1)S(1)} %shard_map.64), channel_id=1, source_target_pairs={{0,12},{2,14},{4,0},{6,2},{8,4},{10,6},{12,8},{14,10},{1,13},{3,15... | collective-permute-start | bytes 153608 | tf_op jit(solution)/shard_map/ppermute | solution.py:208
  6.0 5.0 %collective-permute-start.1 = (bf16[8,3200]{1,0:T(8,128)(2,1)S(1)}, bf16[8,3200]{1,0:T(8,128)(2,1)S(1)}, u32[]{:S(2)}, u32[]{:S(2)}) collective-permute-start(bf16[8,3200]{1,0:T(8,128)(2,1)S(1)} %shard_map.64), channel_id=1, source_target_pairs={{0,8},{2,10},{4,12},{6,14},{8,0},{10,2},{12,4},{14,6},{1,9},{3,11}... | collective-permute-start | bytes 153608 | tf_op jit(solution)/shard_map/ppermute | solution.py:208
  6.0 5.9 %collective-permute-start = (bf16[8,3200]{1,0:T(8,128)(2,1)S(1)}, bf16[8,3200]{1,0:T(8,128)(2,1)S(1)}, u32[]{:S(2)}, u32[]{:S(2)}) collective-permute-start(bf16[8,3200]{1,0:T(8,128)(2,1)S(1)} %shard_map.64), channel_id=1, source_target_pairs={{0,4},{2,6},{4,8},{6,10},{8,12},{10,14},{12,0},{14,2},{1,5},{3,7},... | collective-permute-start | bytes 153608 | tf_op jit(solution)/shard_map/ppermute | solution.py:208
  11.9 2.3 %collective-permute-start.5 = (bf16[32,3200]{1,0:T(8,128)(2,1)S(1)}, bf16[32,3200]{1,0:T(8,128)(2,1)S(1)}, u32[]{:S(2)}, u32[]{:S(2)}) collective-permute-start(bf16[32,3200]{1,0:T(8,128)(2,1)S(1)} %pad_maximum_fusion.refs_0_.own), channel_id=1, source_target_pairs={{0,2},{2,0},{4,6},{6,4},{8,10},{10,8},{12,14},{14,12},{1,3},{3,1},... | collective-permute-start | bytes 614408 | tf_op jit(solution)/shard_map/ppermute | solution.py:210
  12.0 14.8 %collective-permute-start.4 = (bf16[32,3072]{1,0:T(8,128)(2,1)S(1)}, bf16[32,3072]{1,0:T(8,128)(2,1)S(1)}, u32[]{:S(2)}, u32[]{:S(2)}) collective-permute-start(bf16[32,3072]{1,0:T(8,128)(2,1)S(1)} %slice.23), channel_id=1, source_target_pairs={{0,3},{1,2},{2,1},{3,0},{4,7},{5,6},{6,5},{7,4},{8,11},{9,10},{10,... | collective-permute-start | bytes 589832 | tf_op jit(solution)/shard_map/ppermute | solution.py:215
  13.7 13.2 %collective-permute-start.3 = (bf16[32,3072]{1,0:T(8,128)(2,1)S(1)}, bf16[32,3072]{1,0:T(8,128)(2,1)S(1)}, u32[]{:S(2)}, u32[]{:S(2)}) collective-permute-start(bf16[32,3072]{1,0:T(8,128)(2,1)S(1)} %slice.23), channel_id=1, source_target_pairs={{0,1},{1,0},{2,3},{3,2},{4,5},{5,4},{6,7},{7,6},{8,9},{9,8},{10,11... | collective-permute-start | bytes 589832 | tf_op jit(solution)/shard_map/ppermute | solution.py:214
  46.7 9.0 %collective-permute-start.6 = (bf16[32,3072]{1,0:T(8,128)(2,1)S(1)}, bf16[32,3072]{1,0:T(8,128)(2,1)S(1)}, u32[]{:S(2)}, u32[]{:S(2)}) collective-permute-start(bf16[32,3072]{1,0:T(8,128)(2,1)S(1)} %get-tuple-element.14), channel_id=1, source_target_pairs={{0,1},{1,0},{2,3},{3,2},{4,5},{5,4},{6,7},{7,6},{8,9},{9,8},{10,11... | collective-permute-start | bytes 589832 | tf_op jit(solution)/shard_map/ppermute | solution.py:263
  48.3 8.3 %collective-permute-start.7 = (bf16[32,3072]{1,0:T(8,128)(2,1)S(1)}, bf16[32,3072]{1,0:T(8,128)(2,1)S(1)}, u32[]{:S(2)}, u32[]{:S(2)}) collective-permute-start(bf16[32,3072]{1,0:T(8,128)(2,1)S(1)} %get-tuple-element.15), channel_id=1, source_target_pairs={{0,3},{1,2},{2,1},{3,0},{4,7},{5,6},{6,5},{7,4},{8,11},{9,10},{10,... | collective-permute-start | bytes 589832 | tf_op jit(solution)/shard_map/ppermute | solution.py:264
  55.0 1.8 %collective-permute-start.8 = (bf16[32,3072]{1,0:T(8,128)(2,1)S(1)}, bf16[32,3072]{1,0:T(8,128)(2,1)S(1)}, u32[]{:S(2)}, u32[]{:S(2)}) collective-permute-start(bf16[32,3072]{1,0:T(8,128)(2,1)S(1)} %get-tuple-element.16), channel_id=1, source_target_pairs={{0,2},{2,0},{4,6},{6,4},{8,10},{10,8},{12,14},{14,12},{1,3},{3,1},... | collective-permute-start | bytes 589832 | tf_op jit(solution)/shard_map/ppermute | solution.py:266
  56.9 4.3 %collective-permute-start.9 = (bf16[8,3072]{1,0:T(8,128)(2,1)S(1)}, bf16[8,3072]{1,0:T(8,128)(2,1)S(1)}, u32[]{:S(2)}, u32[]{:S(2)}) collective-permute-start(bf16[8,3072]{1,0:T(8,128)(2,1)S(1)} %get-tuple-element.19), channel_id=1, source_target_pairs={{0,12},{2,14},{4,0},{6,2},{8,4},{10,6},{12,8},{14,10},{1,13},{3,15... | collective-permute-start | bytes 147464 | tf_op jit(solution)/shard_map/ppermute | solution.py:273
  58.3 6.4 %collective-permute-start.11 = (bf16[8,3072]{1,0:T(8,128)(2,1)S(1)}, bf16[8,3072]{1,0:T(8,128)(2,1)S(1)}, u32[]{:S(2)}, u32[]{:S(2)}) collective-permute-start(bf16[8,3072]{1,0:T(8,128)(2,1)S(1)} %get-tuple-element.20), channel_id=1, source_target_pairs={{0,4},{2,6},{4,8},{6,10},{8,12},{10,14},{12,0},{14,2},{1,5},{3,7},... | collective-permute-start | bytes 147464 | tf_op jit(solution)/shard_map/ppermute | solution.py:273
  59.0 6.7 %collective-permute-start.10 = (bf16[8,3072]{1,0:T(8,128)(2,1)S(1)}, bf16[8,3072]{1,0:T(8,128)(2,1)S(1)}, u32[]{:S(2)}, u32[]{:S(2)}) collective-permute-start(bf16[8,3072]{1,0:T(8,128)(2,1)S(1)} %get-tuple-element.21), channel_id=1, source_target_pairs={{0,8},{2,10},{4,12},{6,14},{8,0},{10,2},{12,4},{14,6},{1,9},{3,11}... | collective-permute-start | bytes 147464 | tf_op jit(solution)/shard_map/ppermute | solution.py:273

commit v3 on v2

v3 whole, which is shorter than its diff:
```python
import functools

import jax
import jax.numpy as jnp
from jax import lax
from jax.experimental import pallas as pl
from jax.experimental.pallas import tpu as pltpu
from jax.sharding import PartitionSpec as P

FFW = 5376
PAIR = 2
LANES = 128
SLOTS = 3
MIB = 1024 * 1024
F32 = jnp.float32
BF16 = jnp.bfloat16


def largest_step(total, choices):
    for step in choices:
        if total % step == 0:
            return step
    return total


def call(kernel, outs, operands, spaces, scratch, limit, flops, moved):
    return pl.pallas_call(
        kernel,
        out_shape=outs,
        in_specs=[pl.BlockSpec(memory_space=space) for space in spaces],
        out_specs=[pl.BlockSpec(memory_space=pltpu.VMEM) for unused in outs],
        scratch_shapes=scratch,
        compiler_params=pltpu.CompilerParams(vmem_limit_bytes=limit * MIB),
        cost_estimate=pl.CostEstimate(flops=flops, bytes_accessed=moved, transcendentals=0),
    )(*operands)


def in_hbm(*arrays):
    return [pltpu.with_memory_space_constraint(array, pltpu.HBM) for array in arrays]


def columns_of(step, per, block):
    owner = lax.rem(lax.axis_index("blk") + step // per, lax.axis_size("blk"))
    return pl.ds(pl.multiple_of((owner * per + lax.rem(step, per)) * block, LANES), block)


def moves(weights, step, per, targets, sems):
    return [
        pltpu.make_async_copy(weight.at[0, :, columns_of(step, per, target.shape[-1])], target, sem)
        for weight, target, sem in zip(weights, targets, sems)
    ]


def stream(held, count, fetch, ahead, begin, from_held, from_ring):
    rest = count - held
    for at in range(min(SLOTS, rest)):
        for copy in fetch(held + at, at):
            copy.start()
    if rest == 0:
        for copy in ahead:
            copy.start()
    begin()

    def first(step, carry):
        from_held(step)
        return carry

    if held:
        lax.fori_loop(0, held, first, 0)

    def then(at, carry):
        later = at + SLOTS - 1

        @pl.when((at > 0) & (later < rest))
        def _():
            for copy in fetch(held + later, lax.rem(later, SLOTS)):
                copy.start()

        @pl.when(at == max(rest - SLOTS, 0))
        def _():
            for copy in ahead:
                copy.start()

        slot = lax.rem(at, SLOTS)
        from_ring(held + at, slot, fetch(held + at, slot))
        return carry

    if rest:
        lax.fori_loop(0, rest, then, 0)


def finish(copies):
    for copy in copies:
        copy.wait()


def head_kernel(count, per, after, w_gate, w_up, gate, up, sems):
    copies = []
    for step in range(count):
        at = (sems.at[0, step], sems.at[1, step])
        copies += moves((w_gate, w_up), step, per, (gate.at[step], up.at[step]), at)
    for copy in copies:
        copy.start()
    finish(copies)


def pack_kernel(experts, tokens, ids, weights, out, held, named, weighed, sems):
    copies = [
        pltpu.make_async_copy(source, target, sems.at[at])
        for at, (source, target) in enumerate(((ids, named), (weights, weighed), (tokens, held)))
    ]
    for copy in copies:
        copy.start()
    rows, width = tokens.shape
    shape = (rows, out.shape[1] - width)
    lane = lax.broadcasted_iota(jnp.int32, shape, 1)
    diagonal = lax.broadcasted_iota(jnp.int32, (rows, rows), 0) == lax.broadcasted_iota(
        jnp.int32, (rows, rows), 1
    )
    coef = jnp.zeros(shape, F32)
    copies[0].wait()
    copies[1].wait()
    for k in range(ids.shape[0]):
        name = jnp.sum(jnp.where(diagonal, named[k : k + 1], 0), axis=1, keepdims=True)
        weight = jnp.sum(jnp.where(diagonal, weighed[k : k + 1], 0.0), axis=1, keepdims=True)
        coef += jnp.where(lax.rem(lane, experts) == name, weight, 0.0)
    high = coef.astype(BF16).astype(F32)
    middle = (coef - high).astype(BF16).astype(F32)
    low = coef - high - middle
    part = jnp.where(lane < experts, high, jnp.where(lane < 2 * experts, middle, low))
    out[:, width:] = jnp.where(lane < 3 * experts, part, 0.0).astype(BF16)
    copies[2].wait()
    out[:, :width] = held[...]


def up_kernel(kb, parts, held, more, last, *refs):
    sent, refs = refs[: 2 * len(parts)], refs[2 * len(parts) :]
    earlier, refs = (refs[:2], refs[2:]) if last else ((), refs)
    (gate_held, up_held, w_gate, w_up), refs = refs[:4], refs[4:]
    if last:
        w_down, hidden, down_next, x, gate_ring, up_ring, sems, next_sems, gate_sum, up_sum = refs
    else:
        gate_sum, up_sum, gate_next, up_next, x, gate_ring, up_ring, sems, next_sems = refs
    hid = w_gate.shape[1]
    width = x.shape[0] // len(parts)
    per = width // kb
    start = parts[0] * per
    weights = (w_gate, w_up)

    def fetch(step, slot):
        places = (gate_ring.at[slot], up_ring.at[slot])
        return moves(weights, start + step, per, places, (sems.at[0, slot], sems.at[1, slot]))

    ahead = []
    for k in range(more):
        if last:
            down_per = width // down_next.shape[-1]
            ahead += moves((w_down,), down_per + k, down_per, (down_next.at[k],), (next_sems.at[0, k],))
        else:
            places = (gate_next.at[k], up_next.at[k])
            at = (next_sems.at[0, k], next_sems.at[1, k])
            ahead += moves(weights, start + per + k, per, places, at)

    def begin():
        for j in range(len(parts)):
            rows = [sent[2 * j + at][:, :width].astype(F32) for at in range(2)]
            x[j * width : (j + 1) * width] = jnp.concatenate(rows, axis=0).T.astype(BF16)
        gate_sum[...] = earlier[0][...] if last else jnp.zeros_like(gate_sum)
        up_sum[...] = earlier[1][...] if last else jnp.zeros_like(up_sum)

    def right(step):
        return x[pl.ds(pl.multiple_of(step * kb, LANES), kb)]

    def from_held(step):
        gate_sum[...] += jnp.dot(gate_held[step], right(step), preferred_element_type=F32)
        up_sum[...] += jnp.dot(up_held[step], right(step), preferred_element_type=F32)

    def from_ring(step, slot, waits):
        waits[0].wait()
        gate_sum[...] += jnp.dot(gate_ring[slot], right(step), preferred_element_type=F32)
        waits[1].wait()
        up_sum[...] += jnp.dot(up_ring[slot], right(step), preferred_element_type=F32)

    stream(held, len(parts) * per, fetch, ahead, begin, from_held, from_ring)
    if last:
        unit = largest_step(hid, (384,))
        for first in range(0, hid, unit):
            units = pl.ds(first, unit)
            gate = gate_sum[units]
            value = gate / (1.0 + jnp.exp(-gate)) * up_sum[units]
            hidden[:, units] = value.T.astype(BF16)
    finish(ahead)


def down_kernel(start, count, held, experts, shares, hidden, own, other, *refs):
    down_held, refs = (refs[0], refs[1:]) if held else (None, refs)
    w_down, *outs, ring, sems = refs
    unused, half, width = outs[0].shape
    fb = ring.shape[-1]
    per = width // fb
    expert = lax.axis_index("expert") // shares
    packed = jnp.concatenate([own[:, width:], other[:, width:]], axis=0).astype(F32)
    lane = lax.broadcasted_iota(jnp.int32, packed.shape, 1)
    mine = (lax.rem(lane, experts) == expert) & (lane < 3 * experts)
    coef = jnp.sum(jnp.where(mine, packed, 0.0), axis=1, keepdims=True)

    def fetch(step, slot):
        return moves((w_down,), start + step, per, (ring.at[slot],), (sems.at[slot],))

    def put(step, block):
        value = jnp.dot(hidden[...], block, preferred_element_type=F32) * coef
        columns = pl.ds(pl.multiple_of(lax.rem(step, per) * fb, LANES), fb)
        for at, out in enumerate(outs):
            out[step // per, :, columns] = value[at * half : (at + 1) * half].astype(out.dtype)

    def from_held(step):
        put(step, down_held[step])

    def from_ring(step, slot, waits):
        waits[0].wait()
        put(step, ring[slot])

    stream(held, count, fetch, (), lambda: None, from_held, from_ring)


def body(tokens, expert_ids, route_weight, w_gate, w_up, w_down):
    n_expert = lax.axis_size("expert")
    n_blk = lax.axis_size("blk")
    rows, width = tokens.shape
    top = expert_ids.shape[1]
    hid = w_gate.shape[1]
    shares = FFW // (hid * n_blk)
    experts = n_expert // shares
    places = n_expert // PAIR
    half = places * rows
    tokens_all = PAIR * half
    room = -(-3 * experts // LANES) * LANES
    vmem, hbm = pltpu.VMEM, pl.ANY
    w_gate, w_up, w_down = in_hbm(w_gate, w_up, w_down)

    (packed,) = call(
        functools.partial(pack_kernel, experts),
        [jax.ShapeDtypeStruct((rows, width + room), BF16)],
        in_hbm(tokens, expert_ids.T, route_weight.T),
        (hbm,) * 3,
        [
            pltpu.VMEM((rows, width), BF16),
            pltpu.VMEM((top, rows), jnp.int32),
            pltpu.VMEM((top, rows), F32),
            pltpu.SemaphoreType.DMA((3,)),
        ],
        8,
        rows * room,
        4 * rows * width,
    )

    def along(k):
        return [(s, ((s // PAIR + k) % places) * PAIR + s % PAIR) for s in range(n_expert)]

    def across(k):
        return [(s, (s + k) % n_blk) for s in range(n_blk)]

    def across_other(k):
        return [
            (s * n_blk + b, (s ^ 1) * n_blk + (b + k) % n_blk)
            for s in range(n_expert)
            for b in range(n_blk)
        ]

    swap = [(s, s ^ 1) for s in range(n_expert)]

    kb = largest_step(width, (512, 384, 256, 128))
    per = width // kb
    steps = per * (n_blk - 1)
    first_held, second_held, third_held = min(3, per), min(2, steps), min(3, steps)

    def blocks(count):
        return pltpu.VMEM((count, hid, kb), BF16)

    held = call(
        functools.partial(head_kernel, first_held, per),
        [blocks(first_held)] * 2,
        (packed, w_gate, w_up),
        (hbm,) * 3,
        [pltpu.SemaphoreType.DMA((2, first_held))],
        4,
        0,
        4 * hid * kb * first_held,
    )
    pieces = [packed] + [lax.ppermute(packed, "expert", along(k)) for k in range(1, places)]
    pieces, held = lax.optimization_barrier((pieces, held))
    own = jnp.concatenate(pieces, axis=0)
    other = lax.ppermute(own, "expert", swap)
    bare = own[:, :width]
    sent = []
    for j in range(1, n_blk):
        sent.append(lax.ppermute(bare, "blk", across(-j)))
        sent.append(lax.ppermute(bare, ("expert", "blk"), across_other(-j)))

    sums = [jax.ShapeDtypeStruct((hid, tokens_all), F32)] * 2

    def up(parts, held, more, last, outs, operands):
        weights = (w_gate, w_up, w_down) if last else (w_gate, w_up)
        return call(
            functools.partial(up_kernel, kb, parts, held, more, last),
            outs,
            (*operands, *weights),
            (vmem,) * len(operands) + (hbm,) * len(weights),
            [
                pltpu.VMEM((width * len(parts), tokens_all), BF16),
                blocks(SLOTS),
                blocks(SLOTS),
                pltpu.SemaphoreType.DMA((2, SLOTS)),
                pltpu.SemaphoreType.DMA((2, more)),
            ]
            + [pltpu.VMEM(each.shape, F32) for each in sums if last],
            23 if last else 20,
            4 * tokens_all * hid * width * len(parts),
            4 * hid * width * len(parts),
        )

    *partial_sums, gate_held, up_held = up(
        (0,), first_held, second_held, False, sums + [blocks(second_held)] * 2, (own, other, *held)
    )
    hidden, down_held = up(
        tuple(range(1, n_blk)),
        second_held,
        third_held,
        True,
        [jax.ShapeDtypeStruct((tokens_all, hid), BF16), blocks(third_held)],
        (*sent, *partial_sums, gate_held, up_held),
    )

    def down(first, count, kinds, *down_held):
        held = third_held if down_held else 0
        return call(
            functools.partial(down_kernel, first, count, held, experts, shares),
            [jax.ShapeDtypeStruct((count // per, half, width), kind) for kind in kinds],
            (hidden, own, other, *down_held, w_down),
            (vmem,) * (3 + len(down_held)) + (hbm,),
            [blocks(SLOTS), pltpu.SemaphoreType.DMA((SLOTS,))],
            14,
            2 * tokens_all * hid * kb * count,
            2 * hid * kb * count,
        )

    away = down(per, steps, (BF16, BF16), down_held)
    total = []
    for j in range(1, n_blk):
        total.append(lax.ppermute(away[0][j - 1], "blk", across(j)))
        total.append(lax.ppermute(away[1][j - 1], ("expert", "blk"), across_other(j)))
    kept, given = down(0, per, (F32, BF16))
    total.append(lax.ppermute(given[0], "expert", swap))
    summed = kept[0]
    for term in total:
        summed = summed + term.astype(F32)
    mixed = summed[:rows]
    for k in range(1, places):
        piece = summed[k * rows : (k + 1) * rows].astype(BF16)
        mixed = mixed + lax.ppermute(piece, "expert", along(-k)).astype(F32)
    return mixed.astype(BF16)


def solution(mesh):
    placed = (
        P(("groups", "expert"), "blk"),
        P(("groups", "expert"), None),
        P(("groups", "expert"), None),
        P("expert", "blk", None),
        P("expert", "blk", None),
        P("expert", "blk", None),
    )
    return jax.shard_map(
        body, mesh=mesh, in_specs=placed, out_specs=P(("groups", "expert"), "blk"), check_vma=False
    )
```

time: 66.5 us -> 61.2 us (0.920)
  waiting for transfers between devices: 11.4 us -> 5.17 us
  starting transfers between devices: 14 us -> 15.4 us
    ppermute x3, waiting for transfers between devices: 4.9 us -> 0.01 us  [body(): lax.ppermute(packed, 'expert', along(k))]
    ppermute x3, waiting for transfers between devices: 5.44 us -> 3.4 us  [body(): mixed = mixed + lax.ppermute(piece, 'expert', along(-k)).astype(F32)]
    ppermute x1, starting transfers between devices: 1.65 us -> 0.35 us  [body(): sent.append(lax.ppermute(bare, ('expert', 'blk'), across_other(-j)))]
    ppermute x1, starting transfers between devices: 0.53 us -> 1.56 us  [body(): sent.append(lax.ppermute(bare, 'blk', across(-j)))]
    ppermute x3, starting transfers between devices: 6.11 us -> 7.01 us  [body(): lax.ppermute(packed, 'expert', along(k))]
    ppermute x3, starting transfers between devices: 3.32 us -> 4.09 us  [body(): mixed = mixed + lax.ppermute(piece, 'expert', along(-k)).astype(F32)]
    ppermute x3, waiting for transfers between devices: 1.07 us -> 1.75 us  [the longest x1 1.75 us: body(): lax.ppermute(away[1][j - 1], ('expert', 'blk'), across_other(j))]
    pallas_call x5 -> x6, Pallas kernels: 40 us -> 39.5 us  [call(): pl.pallas_call(kernel, out_shape=outs, in_specs=[pl.BlockSpec(memory_spac...]
  transfers between devices with their start and end apart: 12 -> 12, of which waited for: 8 -> 3; matrix products, arithmetic and copies ran while one was open for 0% -> 0% of each run, Pallas kernels for 29% -> 38%
where the time goes in v3:
time: 61.2 us; the launch traced here: 61 us
  Pallas kernels  39.5 us (65%)
  starting transfers between devices  15.4 us (25%)
  waiting for transfers between devices  5.17 us (8%)
  other arithmetic  0.74 us (1%)
    pallas_call x6, Pallas kernels, call(): pl.pallas_call(kernel, out_shape=outs, in_specs=[pl.BlockSpec(memory_spac...  39.5 us
    ppermute x3, starting transfers between devices, body(): lax.ppermute(packed, 'expert', along(k))  7.01 us
    ppermute x3, starting transfers between devices, body(): mixed = mixed + lax.ppermute(piece, 'expert', along(-k)).astype(F32)  4.09 us
    ppermute x3, waiting for transfers between devices, body(): mixed = mixed + lax.ppermute(piece, 'expert', along(-k)).astype(F32)  3.4 us
    ppermute x1, waiting for transfers between devices, body(): lax.ppermute(away[1][j - 1], ('expert', 'blk'), across_other(j))  1.75 us
    ppermute x1, starting transfers between devices, body(): total.append(lax.ppermute(away[0][j - 1], 'blk', across(j)))  1.56 us
    ppermute x1, starting transfers between devices, body(): sent.append(lax.ppermute(bare, 'blk', across(-j)))  1.56 us
  transfers between devices with their start and end apart: 12, of which 3 were waited for; matrix products, arithmetic and copies ran while one was open for 0% of the time, Pallas kernels for 38%

profile of v3, /device:TPU:0, one launch (start us, length us, event | category | flops | bytes accessed | tf_op | source)
XLA Modules:
  0.0 61.0 jit_solution(17204603872398788900)
XLA Ops:
  0.0 0.9 %shard_map.64.after = bf16[8,3200]{1,0:T(8,128)(2,1)S(1)} custom-call(bf16[8,3072]{1,0:T(8,128)(2,1)} %tokens.1, s32[4,8]{1,0:T(4,128)} %bitcast.15, f32[4,8]{1,0:T(4,128)} %bitcast.16), custom_call_target="tpu_custom_call" | custom-call | flops 1024 | bytes 98304 | tf_op jit(solution)/shard_map/pallas_call | solution.py:27
  0.9 3.1 %collective-permute-start = (bf16[8,3200]{1,0:T(8,128)(2,1)S(1)}, bf16[8,3200]{1,0:T(8,128)(2,1)S(1)}, u32[]{:S(2)}, u32[]{:S(2)}) collective-permute-start(bf16[8,3200]{1,0:T(8,128)(2,1)S(1)} %shard_map.64.after), channel_id=1, source_target_pairs={{0,4},{2,6},{4,8},{6,10},{8,12},{10,14},{12,0},{14,2},{1,5},{3,7},... | collective-permute-start | bytes 153608 | tf_op jit(solution)/shard_map/ppermute | solution.py:290
  3.9 2.6 %collective-permute-start.1 = (bf16[8,3200]{1,0:T(8,128)(2,1)S(1)}, bf16[8,3200]{1,0:T(8,128)(2,1)S(1)}, u32[]{:S(2)}, u32[]{:S(2)}) collective-permute-start(bf16[8,3200]{1,0:T(8,128)(2,1)S(1)} %shard_map.64.after), channel_id=1, source_target_pairs={{0,8},{2,10},{4,12},{6,14},{8,0},{10,2},{12,4},{14,6},{1,9},{3,11}... | collective-permute-start | bytes 153608 | tf_op jit(solution)/shard_map/ppermute | solution.py:290
  6.5 1.3 %collective-permute-start.2 = (bf16[8,3200]{1,0:T(8,128)(2,1)S(1)}, bf16[8,3200]{1,0:T(8,128)(2,1)S(1)}, u32[]{:S(2)}, u32[]{:S(2)}) collective-permute-start(bf16[8,3200]{1,0:T(8,128)(2,1)S(1)} %shard_map.64.after), channel_id=1, source_target_pairs={{0,12},{2,14},{4,0},{6,2},{8,4},{10,6},{12,8},{14,10},{1,13},{3,15... | collective-permute-start | bytes 153608 | tf_op jit(solution)/shard_map/ppermute | solution.py:290
  7.9 5.9 %shard_map.65 = (bf16[3,2688,512]{2,1,0:T(8,128)(2,1)S(1)}, bf16[3,2688,512]{2,1,0:T(8,128)(2,1)S(1)}) custom-call(bf16[8,3200]{1,0:T(8,128)(2,1)S(1)} %shard_map.64.after, bf16[1,2688,6144]{2,1,0:T(8,128)(2,1)} %refs_6_.1, bf16[1,2688,6144]{2,1,0:T(8,128)(2,1)} %refs_7_.1), custom_call_target="tpu_custom_call" | custom-call | bytes 16515072 | tf_op jit(solution)/shard_map/pallas_call | solution.py:27
  13.8 0.0 collective-permute-done
  13.8 0.0 collective-permute-done.1
  13.8 0.0 collective-permute-done.2
  13.9 0.1 collective-permute-start.5
  14.0 1.6 %collective-permute-start.3 = (bf16[32,3072]{1,0:T(8,128)(2,1)S(1)}, bf16[32,3072]{1,0:T(8,128)(2,1)S(1)}, u32[]{:S(2)}, u32[]{:S(2)}) collective-permute-start(bf16[32,3072]{1,0:T(8,128)(2,1)S(1)} %slice.23), channel_id=1, source_target_pairs={{0,1},{1,0},{2,3},{3,2},{4,5},{5,4},{6,7},{7,6},{8,9},{9,8},{10,11... | collective-permute-start | bytes 589832 | tf_op jit(solution)/shard_map/ppermute | solution.py:297
  15.5 0.4 collective-permute-start.4
  15.9 0.0 collective-permute-done.5.refs_1_.other
  15.9 10.7 %shard_map.66 = (f32[2688,64]{1,0:T(8,128)S(1)}, f32[2688,64]{1,0:T(8,128)S(1)}, bf16[2,2688,512]{2,1,0:T(8,128)(2,1)S(1)}, bf16[2,2688,512]{2,1,0:T(8,128)(2,1)S(1)}) custom-call(bf16[32,3200]{1,0:T(8,128)(2,1)S(1)} %constant_dynamic-update-slice_fusion.refs_0_.own, bf16[32,3200]{1,0:T(8,128)(2,1)S(1)} %collective-permute-done.5.refs_1_.other, ...), custom_call_target="tpu_custom_call" | custom-call | flops 2113929216 | bytes 33030144 | tf_op jit(solution)/shard_map/pallas_call | solution.py:27
  26.6 0.0 collective-permute-done.3.refs_0_
  26.6 0.0 collective-permute-done.4.refs_1_
  26.6 11.3 %shard_map.67 = (bf16[64,2688]{1,0:T(8,128)(2,1)S(1)}, bf16[3,2688,512]{2,1,0:T(8,128)(2,1)S(1)}) custom-call(bf16[32,3072]{1,0:T(8,128)(2,1)S(1)} %collective-permute-done.3.refs_0_, bf16[32,3072]{1,0:T(8,128)(2,1)S(1)} %collective-permute-done.4.refs_1_, f32[2688,64]{1,0:T(8,128)S(1)} %get-tuple-element.31.refs_2_, ...), custom_call_target="tpu_custom_call" | custom-call | flops 2113929216 | bytes 33030144 | tf_op jit(solution)/shard_map/pallas_call | solution.py:27
  37.9 4.1 %shard_map.69 = (bf16[1,32,3072]{2,1,0:T(8,128)(2,1)S(1)}, bf16[1,32,3072]{2,1,0:T(8,128)(2,1)S(1)}) custom-call(bf16[64,2688]{1,0:T(8,128)(2,1)S(1)} %get-tuple-element.35.hidden, bf16[32,3200]{1,0:T(8,128)(2,1)S(1)} %constant_dynamic-update-slice_fusion.refs_0_.own, bf16[32,3200]{1,0:T(8,128)(2,1)S(1)} %collective-permute-done.5.refs_1_.other, ...), custom_call_target="tpu_custom_call" | custom-call | flops 1056964608 | bytes 16515072 | tf_op jit(solution)/shard_map/pallas_call | solution.py:27
  42.0 1.6 %collective-permute-start.6 = (bf16[32,3072]{1,0:T(8,128)(2,1)S(1)}, bf16[32,3072]{1,0:T(8,128)(2,1)S(1)}, u32[]{:S(2)}, u32[]{:S(2)}) collective-permute-start(bf16[32,3072]{1,0:T(8,128)(2,1)S(1)} %bitcast.13), channel_id=1, source_target_pairs={{0,1},{1,0},{2,3},{3,2},{4,5},{5,4},{6,7},{7,6},{8,9},{9,8},{10,11... | collective-permute-start | bytes 589832 | tf_op jit(solution)/shard_map/ppermute | solution.py:350
  43.6 0.2 collective-permute-start.7
  43.7 6.7 %shard_map.68 = (f32[1,32,3072]{2,1,0:T(8,128)S(1)}, bf16[1,32,3072]{2,1,0:T(8,128)(2,1)S(1)}) custom-call(bf16[64,2688]{1,0:T(8,128)(2,1)S(1)} %get-tuple-element.35.hidden, bf16[32,3200]{1,0:T(8,128)(2,1)S(1)} %constant_dynamic-update-slice_fusion.refs_0_.own, bf16[32,3200]{1,0:T(8,128)(2,1)S(1)} %collective-permute-done.5.refs_1_.other, ...), custom_call_target="tpu_custom_call" | custom-call | flops 1056964608 | bytes 16515072 | tf_op jit(solution)/shard_map/pallas_call | solution.py:27
  50.4 0.6 collective-permute-start.8
  51.0 0.0 collective-permute-done.6
  51.0 1.7 %collective-permute-done.7 = bf16[32,3072]{1,0:T(8,128)(2,1)S(1)} collective-permute-done((bf16[32,3072]{1,0:T(8,128)(2,1)S(1)}, bf16[32,3072]{1,0:T(8,128)(2,1)S(1)}, u32[]{:S(2)}, u32[]{:S(2)}) %collective-permute-start.7) | collective-permute-done | bytes 196640 | tf_op jit(solution)/shard_map/ppermute | solution.py:351
  52.8 0.0 collective-permute-done.8
  52.8 0.1 fusion.5
  52.9 0.3 collective-permute-start.10
  53.1 0.8 %collective-permute-start.11 = (bf16[8,3072]{1,0:T(8,128)(2,1)S(1)}, bf16[8,3072]{1,0:T(8,128)(2,1)S(1)}, u32[]{:S(2)}, u32[]{:S(2)}) collective-permute-start(bf16[8,3072]{1,0:T(8,128)(2,1)S(1)} %get-tuple-element.44), channel_id=1, source_target_pairs={{0,4},{2,6},{4,8},{6,10},{8,12},{10,14},{12,0},{14,2},{1,5},{3,7},... | collective-permute-start | bytes 147464 | tf_op jit(solution)/shard_map/ppermute | solution.py:360
  54.0 3.0 %collective-permute-start.9 = (bf16[8,3072]{1,0:T(8,128)(2,1)S(1)}, bf16[8,3072]{1,0:T(8,128)(2,1)S(1)}, u32[]{:S(2)}, u32[]{:S(2)}) collective-permute-start(bf16[8,3072]{1,0:T(8,128)(2,1)S(1)} %get-tuple-element.43), channel_id=1, source_target_pairs={{0,12},{2,14},{4,0},{6,2},{8,4},{10,6},{12,8},{14,10},{1,13},{3,15... | collective-permute-start | bytes 147464 | tf_op jit(solution)/shard_map/ppermute | solution.py:360
  57.0 3.3 %collective-permute-done.10 = bf16[8,3072]{1,0:T(8,128)(2,1)S(1)} collective-permute-done((bf16[8,3072]{1,0:T(8,128)(2,1)S(1)}, bf16[8,3072]{1,0:T(8,128)(2,1)S(1)}, u32[]{:S(2)}, u32[]{:S(2)}) %collective-permute-start.10) | collective-permute-done | bytes 49184 | tf_op jit(solution)/shard_map/ppermute | solution.py:360
  60.3 0.0 collective-permute-done.11
  60.3 0.1 collective-permute-done.9
  60.4 0.6 %fusion.4 = bf16[8,3072]{1,0:T(8,128)(2,1)} fusion(f32[32,3072]{1,0:T(8,128)S(1)} %get-tuple-element.42, bf16[8,3072]{1,0:T(8,128)(2,1)S(1)} %collective-permute-done.11, bf16[8,3072]{1,0:T(8,128)(2,1)S(1)} %collective-permute-done.10, bf16[8,3072]{1,0:T(8,128)(2,1)S(1)} %collective-permute-done.9), kind=kLoop, calls=%fused_computation.6 | loop fusion | flops 172032 | bytes 294912 | tf_op jit(solution)/shard_map/convert_element_type | solution.py:361
  (6 shorter events, 0.1 us)
Async XLA Ops:
  0.9 12.9 %collective-permute-start = (bf16[8,3200]{1,0:T(8,128)(2,1)S(1)}, bf16[8,3200]{1,0:T(8,128)(2,1)S(1)}, u32[]{:S(2)}, u32[]{:S(2)}) collective-permute-start(bf16[8,3200]{1,0:T(8,128)(2,1)S(1)} %shard_map.64.after), channel_id=1, source_target_pairs={{0,4},{2,6},{4,8},{6,10},{8,12},{10,14},{12,0},{14,2},{1,5},{3,7},... | collective-permute-start | bytes 153608 | tf_op jit(solution)/shard_map/ppermute | solution.py:290
  3.9 9.9 %collective-permute-start.1 = (bf16[8,3200]{1,0:T(8,128)(2,1)S(1)}, bf16[8,3200]{1,0:T(8,128)(2,1)S(1)}, u32[]{:S(2)}, u32[]{:S(2)}) collective-permute-start(bf16[8,3200]{1,0:T(8,128)(2,1)S(1)} %shard_map.64.after), channel_id=1, source_target_pairs={{0,8},{2,10},{4,12},{6,14},{8,0},{10,2},{12,4},{14,6},{1,9},{3,11}... | collective-permute-start | bytes 153608 | tf_op jit(solution)/shard_map/ppermute | solution.py:290
  6.5 7.3 %collective-permute-start.2 = (bf16[8,3200]{1,0:T(8,128)(2,1)S(1)}, bf16[8,3200]{1,0:T(8,128)(2,1)S(1)}, u32[]{:S(2)}, u32[]{:S(2)}) collective-permute-start(bf16[8,3200]{1,0:T(8,128)(2,1)S(1)} %shard_map.64.after), channel_id=1, source_target_pairs={{0,12},{2,14},{4,0},{6,2},{8,4},{10,6},{12,8},{14,10},{1,13},{3,15... | collective-permute-start | bytes 153608 | tf_op jit(solution)/shard_map/ppermute | solution.py:290
  13.9 2.0 %collective-permute-start.5 = (bf16[32,3200]{1,0:T(8,128)(2,1)S(1)}, bf16[32,3200]{1,0:T(8,128)(2,1)S(1)}, u32[]{:S(2)}, u32[]{:S(2)}) collective-permute-start(bf16[32,3200]{1,0:T(8,128)(2,1)S(1)} %constant_dynamic-update-slice_fusion.refs_0_.own), channel_id=1, source_target_pairs={{0,2},{2,0},{4,6},{6,4},{8,10},{10,8},{12,14},{14,12},{1,3},{3,1},... | collective-permute-start | bytes 614408 | tf_op jit(solution)/shard_map/ppermute | solution.py:293
  14.0 12.6 %collective-permute-start.3 = (bf16[32,3072]{1,0:T(8,128)(2,1)S(1)}, bf16[32,3072]{1,0:T(8,128)(2,1)S(1)}, u32[]{:S(2)}, u32[]{:S(2)}) collective-permute-start(bf16[32,3072]{1,0:T(8,128)(2,1)S(1)} %slice.23), channel_id=1, source_target_pairs={{0,1},{1,0},{2,3},{3,2},{4,5},{5,4},{6,7},{7,6},{8,9},{9,8},{10,11... | collective-permute-start | bytes 589832 | tf_op jit(solution)/shard_map/ppermute | solution.py:297
  15.5 11.0 %collective-permute-start.4 = (bf16[32,3072]{1,0:T(8,128)(2,1)S(1)}, bf16[32,3072]{1,0:T(8,128)(2,1)S(1)}, u32[]{:S(2)}, u32[]{:S(2)}) collective-permute-start(bf16[32,3072]{1,0:T(8,128)(2,1)S(1)} %slice.23), channel_id=1, source_target_pairs={{0,3},{1,2},{2,1},{3,0},{4,7},{5,6},{6,5},{7,4},{8,11},{9,10},{10,... | collective-permute-start | bytes 589832 | tf_op jit(solution)/shard_map/ppermute | solution.py:298
  42.0 9.0 %collective-permute-start.6 = (bf16[32,3072]{1,0:T(8,128)(2,1)S(1)}, bf16[32,3072]{1,0:T(8,128)(2,1)S(1)}, u32[]{:S(2)}, u32[]{:S(2)}) collective-permute-start(bf16[32,3072]{1,0:T(8,128)(2,1)S(1)} %bitcast.13), channel_id=1, source_target_pairs={{0,1},{1,0},{2,3},{3,2},{4,5},{5,4},{6,7},{7,6},{8,9},{9,8},{10,11... | collective-permute-start | bytes 589832 | tf_op jit(solution)/shard_map/ppermute | solution.py:350
  43.6 9.2 %collective-permute-start.7 = (bf16[32,3072]{1,0:T(8,128)(2,1)S(1)}, bf16[32,3072]{1,0:T(8,128)(2,1)S(1)}, u32[]{:S(2)}, u32[]{:S(2)}) collective-permute-start(bf16[32,3072]{1,0:T(8,128)(2,1)S(1)} %bitcast.12), channel_id=1, source_target_pairs={{0,3},{1,2},{2,1},{3,0},{4,7},{5,6},{6,5},{7,4},{8,11},{9,10},{10,... | collective-permute-start | bytes 589832 | tf_op jit(solution)/shard_map/ppermute | solution.py:351
  50.4 2.3 %collective-permute-start.8 = (bf16[32,3072]{1,0:T(8,128)(2,1)S(1)}, bf16[32,3072]{1,0:T(8,128)(2,1)S(1)}, u32[]{:S(2)}, u32[]{:S(2)}) collective-permute-start(bf16[32,3072]{1,0:T(8,128)(2,1)S(1)} %bitcast.14), channel_id=1, source_target_pairs={{0,2},{2,0},{4,6},{6,4},{8,10},{10,8},{12,14},{14,12},{1,3},{3,1},... | collective-permute-start | bytes 589832 | tf_op jit(solution)/shard_map/ppermute | solution.py:353
  52.9 7.4 %collective-permute-start.10 = (bf16[8,3072]{1,0:T(8,128)(2,1)S(1)}, bf16[8,3072]{1,0:T(8,128)(2,1)S(1)}, u32[]{:S(2)}, u32[]{:S(2)}) collective-permute-start(bf16[8,3072]{1,0:T(8,128)(2,1)S(1)} %get-tuple-element.45), channel_id=1, source_target_pairs={{0,8},{2,10},{4,12},{6,14},{8,0},{10,2},{12,4},{14,6},{1,9},{3,11}... | collective-permute-start | bytes 147464 | tf_op jit(solution)/shard_map/ppermute | solution.py:360
  53.1 7.2 %collective-permute-start.11 = (bf16[8,3072]{1,0:T(8,128)(2,1)S(1)}, bf16[8,3072]{1,0:T(8,128)(2,1)S(1)}, u32[]{:S(2)}, u32[]{:S(2)}) collective-permute-start(bf16[8,3072]{1,0:T(8,128)(2,1)S(1)} %get-tuple-element.44), channel_id=1, source_target_pairs={{0,4},{2,6},{4,8},{6,10},{8,12},{10,14},{12,0},{14,2},{1,5},{3,7},... | collective-permute-start | bytes 147464 | tf_op jit(solution)/shard_map/ppermute | solution.py:360
  54.0 6.4 %collective-permute-start.9 = (bf16[8,3072]{1,0:T(8,128)(2,1)S(1)}, bf16[8,3072]{1,0:T(8,128)(2,1)S(1)}, u32[]{:S(2)}, u32[]{:S(2)}) collective-permute-start(bf16[8,3072]{1,0:T(8,128)(2,1)S(1)} %get-tuple-element.43), channel_id=1, source_target_pairs={{0,12},{2,14},{4,0},{6,2},{8,4},{10,6},{12,8},{14,10},{1,13},{3,15... | collective-permute-start | bytes 147464 | tf_op jit(solution)/shard_map/ppermute | solution.py:360

commit v4 on v3

--- a/solution.py
+++ b/solution.py
@@ -10,7 +10,8 @@
 FFW = 5376
 PAIR = 2
 LANES = 128
-SLOTS = 3
+UP_SLOTS = 2
+DOWN_SLOTS = 3
 MIB = 1024 * 1024
 F32 = jnp.float32
 BF16 = jnp.bfloat16
@@ -51,9 +52,9 @@
     ]
 
 
-def stream(held, count, fetch, ahead, begin, from_held, from_ring):
+def stream(held, count, slots, fetch, ahead, begin, from_held, from_ring):
     rest = count - held
-    for at in range(min(SLOTS, rest)):
+    for at in range(min(slots, rest)):
         for copy in fetch(held + at, at):
             copy.start()
     if rest == 0:
@@ -69,19 +70,19 @@
         lax.fori_loop(0, held, first, 0)
 
     def then(at, carry):
-        later = at + SLOTS - 1
+        later = at + slots - 1
 
         @pl.when((at > 0) & (later < rest))
         def _():
-            for copy in fetch(held + later, lax.rem(later, SLOTS)):
+            for copy in fetch(held + later, lax.rem(later, slots)):
                 copy.start()
 
-        @pl.when(at == max(rest - SLOTS, 0))
+        @pl.when(at == max(rest - slots, 0))
         def _():
             for copy in ahead:
                 copy.start()
 
-        slot = lax.rem(at, SLOTS)
+        slot = lax.rem(at, slots)
         from_ring(held + at, slot, fetch(held + at, slot))
         return carry
 
@@ -181,7 +182,7 @@
         waits[1].wait()
         up_sum[...] += jnp.dot(up_ring[slot], right(step), preferred_element_type=F32)
 
-    stream(held, len(parts) * per, fetch, ahead, begin, from_held, from_ring)
+    stream(held, len(parts) * per, gate_ring.shape[0], fetch, ahead, begin, from_held, from_ring)
     if last:
         unit = largest_step(hid, (384,))
         for first in range(0, hid, unit):
@@ -220,7 +221,7 @@
         waits[0].wait()
         put(step, ring[slot])
 
-    stream(held, count, fetch, (), lambda: None, from_held, from_ring)
+    stream(held, count, ring.shape[0], fetch, (), lambda: None, from_held, from_ring)
 
 
 def body(tokens, expert_ids, route_weight, w_gate, w_up, w_down):
@@ -255,7 +256,7 @@
     )
 
     def along(k):
-        return [(s, ((s // PAIR + k) % places) * PAIR + s % PAIR) for s in range(n_expert)]
+        return [(s, (s // PAIR ^ k) * PAIR + s % PAIR) for s in range(n_expert)]
 
     def across(k):
         return [(s, (s + k) % n_blk) for s in range(n_blk)]
@@ -269,23 +270,23 @@
 
     swap = [(s, s ^ 1) for s in range(n_expert)]
 
-    kb = largest_step(width, (512, 384, 256, 128))
-    per = width // kb
-    steps = per * (n_blk - 1)
-    first_held, second_held, third_held = min(3, per), min(2, steps), min(3, steps)
-
-    def blocks(count):
-        return pltpu.VMEM((count, hid, kb), BF16)
+    kb = largest_step(width, (1024, 768, 512, 384, 256, 128))
+    fb = largest_step(width, (512, 384, 256, 128))
+    per, down_per = width // kb, width // fb
+    up_held, down_held = 1, min(3, down_per)
+
+    def blocks(count, block):
+        return pltpu.VMEM((count, hid, block), BF16)
 
     held = call(
-        functools.partial(head_kernel, first_held, per),
-        [blocks(first_held)] * 2,
+        functools.partial(head_kernel, up_held, per),
+        [blocks(up_held, kb)] * 2,
         (packed, w_gate, w_up),
         (hbm,) * 3,
-        [pltpu.SemaphoreType.DMA((2, first_held))],
+        [pltpu.SemaphoreType.DMA((2, up_held))],
         4,
         0,
-        4 * hid * kb * first_held,
+        4 * hid * kb * up_held,
     )
     pieces = [packed] + [lax.ppermute(packed, "expert", along(k)) for k in range(1, places)]
     pieces, held = lax.optimization_barrier((pieces, held))
@@ -299,66 +300,66 @@
 
     sums = [jax.ShapeDtypeStruct((hid, tokens_all), F32)] * 2
 
-    def up(parts, held, more, last, outs, operands):
+    def up(parts, more, outs, operands):
+        last = parts[0] > 0
         weights = (w_gate, w_up, w_down) if last else (w_gate, w_up)
         return call(
-            functools.partial(up_kernel, kb, parts, held, more, last),
+            functools.partial(up_kernel, kb, parts, up_held, more, last),
             outs,
             (*operands, *weights),
             (vmem,) * len(operands) + (hbm,) * len(weights),
             [
                 pltpu.VMEM((width * len(parts), tokens_all), BF16),
-                blocks(SLOTS),
-                blocks(SLOTS),
-                pltpu.SemaphoreType.DMA((2, SLOTS)),
+                blocks(UP_SLOTS, kb),
+                blocks(UP_SLOTS, kb),
+                pltpu.SemaphoreType.DMA((2, UP_SLOTS)),
                 pltpu.SemaphoreType.DMA((2, more)),
             ]
             + [pltpu.VMEM(each.shape, F32) for each in sums if last],
-            23 if last else 20,
+            35 if last else 33,
             4 * tokens_all * hid * width * len(parts),
             4 * hid * width * len(parts),
         )
 
-    *partial_sums, gate_held, up_held = up(
-        (0,), first_held, second_held, False, sums + [blocks(second_held)] * 2, (own, other, *held)
-    )
-    hidden, down_held = up(
+    begun = up((0,), up_held, sums + [blocks(up_held, kb)] * 2, (own, other, *held))
+    hidden, first_blocks = up(
         tuple(range(1, n_blk)),
-        second_held,
-        third_held,
-        True,
-        [jax.ShapeDtypeStruct((tokens_all, hid), BF16), blocks(third_held)],
-        (*sent, *partial_sums, gate_held, up_held),
-    )
-
-    def down(first, count, kinds, *down_held):
-        held = third_held if down_held else 0
+        down_held,
+        [jax.ShapeDtypeStruct((tokens_all, hid), BF16), blocks(down_held, fb)],
+        (*sent, *begun),
+    )
+
+    def down(first, count, kinds, *held):
         return call(
-            functools.partial(down_kernel, first, count, held, experts, shares),
-            [jax.ShapeDtypeStruct((count // per, half, width), kind) for kind in kinds],
-            (hidden, own, other, *down_held, w_down),
-            (vmem,) * (3 + len(down_held)) + (hbm,),
-            [blocks(SLOTS), pltpu.SemaphoreType.DMA((SLOTS,))],
-            14,
-            2 * tokens_all * hid * kb * count,
-            2 * hid * kb * count,
+            functools.partial(down_kernel, first, count, down_held * len(held), experts, shares),
+            [jax.ShapeDtypeStruct((count // down_per, half, width), kind) for kind in kinds],
+            (hidden, own, other, *held, w_down),
+            (vmem,) * (3 + len(held)) + (hbm,),
+            [blocks(DOWN_SLOTS, fb), pltpu.SemaphoreType.DMA((DOWN_SLOTS,))],
+            20,
+            2 * tokens_all * hid * fb * count,
+            2 * hid * fb * count,
         )
 
-    away = down(per, steps, (BF16, BF16), down_held)
+    away = down(down_per, down_per * (n_blk - 1), (BF16, BF16), first_blocks)
     total = []
     for j in range(1, n_blk):
         total.append(lax.ppermute(away[0][j - 1], "blk", across(j)))
         total.append(lax.ppermute(away[1][j - 1], ("expert", "blk"), across_other(j)))
-    kept, given = down(0, per, (F32, BF16))
+    kept, given = down(0, down_per, (F32, BF16))
     total.append(lax.ppermute(given[0], "expert", swap))
     summed = kept[0]
     for term in total:
         summed = summed + term.astype(F32)
-    mixed = summed[:rows]
-    for k in range(1, places):
-        piece = summed[k * rows : (k + 1) * rows].astype(BF16)
-        mixed = mixed + lax.ppermute(piece, "expert", along(-k)).astype(F32)
-    return mixed.astype(BF16)
+    pieces = {k: summed[k * rows : (k + 1) * rows] for k in range(places)}
+    bit = 1
+    while bit < places:
+        leaving = [k for k in pieces if k & bit]
+        piece = jnp.concatenate([pieces[k] for k in leaving], axis=0).astype(BF16)
+        piece = lax.ppermute(piece, "expert", along(bit)).astype(F32)
+        pieces = {k ^ bit: pieces[k ^ bit] + piece[at * rows : (at + 1) * rows] for at, k in enumerate(leaving)}
+        bit *= 2
+    return pieces[0].astype(BF16)
 
 
 def solution(mesh):

time: 61.2 us -> 76.4 us (1.25)
  Pallas kernels: 39.5 us -> 48 us
  local copies, waits for them, and re-layouts: 0.07 us -> 4.88 us
  waiting for transfers between devices: 5.17 us -> 8.69 us
  starting transfers between devices: 15.4 us -> 13.7 us
    pallas_call x6, Pallas kernels: 39.5 us -> 48 us  [call(): pl.pallas_call(kernel, out_shape=outs, in_specs=[pl.BlockSpec(memory_spac...]
    unnamed x3 -> x7, local copies, waits for them, and re-layouts: 0.03 us -> 4.85 us
    ppermute x3 -> x2, waiting for transfers between devices: 3.4 us -> 7 us  [body(): piece = lax.ppermute(piece, 'expert', along(bit)).astype(F32)]
    ppermute x3, starting transfers between devices: 7.01 us -> 5.68 us  [body(): lax.ppermute(packed, 'expert', along(k))]
    ppermute x3 -> x2, starting transfers between devices: 4.09 us -> 3.72 us  [body(): piece = lax.ppermute(piece, 'expert', along(bit)).astype(F32)]
  transfers between devices with their start and end apart: 12 -> 11, of which waited for: 3 -> 3; matrix products, arithmetic and copies ran while one was open for 0% -> 0% of each run, Pallas kernels for 38% -> 36%
where the time goes in v4:
time: 76.4 us; the launch traced here: 76.2 us
  Pallas kernels  48 us (63%)
  starting transfers between devices  13.7 us (18%)
  waiting for transfers between devices  8.69 us (11%)
  local copies, waits for them, and re-layouts  4.88 us (6%)
  other arithmetic  0.77 us (1%)
    pallas_call x6, Pallas kernels, call(): pl.pallas_call(kernel, out_shape=outs, in_specs=[pl.BlockSpec(memory_spac...  48 us
    ppermute x2, waiting for transfers between devices, body(): piece = lax.ppermute(piece, 'expert', along(bit)).astype(F32)  7 us
    ppermute x3, starting transfers between devices, body(): lax.ppermute(packed, 'expert', along(k))  5.68 us
    unnamed x7, local copies, waits for them, and re-layouts  4.85 us
    ppermute x2, starting transfers between devices, body(): piece = lax.ppermute(piece, 'expert', along(bit)).astype(F32)  3.72 us
    ppermute x1, starting transfers between devices, body(): sent.append(lax.ppermute(bare, 'blk', across(-j)))  1.77 us
    ppermute x1, starting transfers between devices, body(): total.append(lax.ppermute(away[0][j - 1], 'blk', across(j)))  1.76 us
    ppermute x1, waiting for transfers between devices, body(): lax.ppermute(away[1][j - 1], ('expert', 'blk'), across_other(j))  1.66 us
  transfers between devices with their start and end apart: 11, of which 3 were waited for; matrix products, arithmetic and copies ran while one was open for 0% of the time, Pallas kernels for 36%

profile of v4, /device:TPU:0, one launch (start us, length us, event | category | flops | bytes accessed | tf_op | source)
XLA Modules:
  0.0 76.2 jit_solution(16495718409816480118)
XLA Ops:
  0.0 0.9 %shard_map.64.after = bf16[8,3200]{1,0:T(8,128)(2,1)S(1)} custom-call(bf16[8,3072]{1,0:T(8,128)(2,1)} %tokens.1, s32[4,8]{1,0:T(4,128)} %bitcast.15, f32[4,8]{1,0:T(4,128)} %bitcast.16), custom_call_target="tpu_custom_call" | custom-call | flops 1024 | bytes 98304 | tf_op jit(solution)/shard_map/pallas_call | solution.py:28
  0.9 3.1 %collective-permute-start = (bf16[8,3200]{1,0:T(8,128)(2,1)S(1)}, bf16[8,3200]{1,0:T(8,128)(2,1)S(1)}, u32[]{:S(2)}, u32[]{:S(2)}) collective-permute-start(bf16[8,3200]{1,0:T(8,128)(2,1)S(1)} %shard_map.64.after), channel_id=1, source_target_pairs={{0,4},{2,6},{4,0},{6,2},{8,12},{10,14},{12,8},{14,10},{1,5},{3,7},... | collective-permute-start | bytes 153608 | tf_op jit(solution)/shard_map/ppermute | solution.py:291
  4.0 2.6 %collective-permute-start.1 = (bf16[8,3200]{1,0:T(8,128)(2,1)S(1)}, bf16[8,3200]{1,0:T(8,128)(2,1)S(1)}, u32[]{:S(2)}, u32[]{:S(2)}) collective-permute-start(bf16[8,3200]{1,0:T(8,128)(2,1)S(1)} %shard_map.64.after), channel_id=1, source_target_pairs={{0,8},{2,10},{4,12},{6,14},{8,0},{10,2},{12,4},{14,6},{1,9},{3,11}... | collective-permute-start | bytes 153608 | tf_op jit(solution)/shard_map/ppermute | solution.py:291
  6.5 0.0 collective-permute-start.2
  6.5 4.2 %shard_map.65 = (bf16[1,2688,1024]{2,1,0:T(8,128)(2,1)S(1)}, bf16[1,2688,1024]{2,1,0:T(8,128)(2,1)S(1)}) custom-call(bf16[8,3200]{1,0:T(8,128)(2,1)S(1)} %shard_map.64.after, bf16[1,2688,6144]{2,1,0:T(8,128)(2,1)} %refs_6_.1, bf16[1,2688,6144]{2,1,0:T(8,128)(2,1)} %refs_7_.1), custom_call_target="tpu_custom_call" | custom-call | bytes 11010048 | tf_op jit(solution)/shard_map/pallas_call | solution.py:28
  10.8 2.4 %copy-done.1 = bf16[1,2688,1024]{2,1,0:T(8,128)(2,1)} copy-done((bf16[1,2688,1024]{2,1,0:T(8,128)(2,1)}, bf16[1,2688,1024]{2,1,0:T(8,128)(2,1)S(1)}, u32[]{:S(2)}) %copy-start.1) | copy-done | bytes 5505048
  13.2 0.0 collective-permute-done
  13.2 0.0 collective-permute-done.1
  13.2 0.0 collective-permute-done.2
  13.3 0.1 collective-permute-start.5
  13.4 1.8 %collective-permute-start.3 = (bf16[32,3072]{1,0:T(8,128)(2,1)S(1)}, bf16[32,3072]{1,0:T(8,128)(2,1)S(1)}, u32[]{:S(2)}, u32[]{:S(2)}) collective-permute-start(bf16[32,3072]{1,0:T(8,128)(2,1)S(1)} %slice.30), channel_id=1, source_target_pairs={{0,1},{1,0},{2,3},{3,2},{4,5},{5,4},{6,7},{7,6},{8,9},{9,8},{10,11... | collective-permute-start | bytes 589832 | tf_op jit(solution)/shard_map/ppermute | solution.py:298
  15.1 0.2 collective-permute-start.4
  15.3 0.0 collective-permute-done.5.refs_1_.other
  15.3 16.5 %shard_map.66 = (f32[2688,64]{1,0:T(8,128)S(1)}, f32[2688,64]{1,0:T(8,128)S(1)}, bf16[1,2688,1024]{2,1,0:T(8,128)(2,1)S(1)}, bf16[1,2688,1024]{2,1,0:T(8,128)(2,1)S(1)}) custom-call(bf16[32,3200]{1,0:T(8,128)(2,1)S(1)} %constant_dynamic-update-slice_fusion.refs_0_.own, bf16[32,3200]{1,0:T(8,128)(2,1)S(1)} %collective-permute-done.5.refs_1_.other, ...), custom_call_target="tpu_custom_call" | custom-call | flops 2113929216 | bytes 33030144 | tf_op jit(solution)/shard_map/pallas_call | solution.py:28
  31.8 2.4 %copy-done = bf16[1,2688,1024]{2,1,0:T(8,128)(2,1)} copy-done((bf16[1,2688,1024]{2,1,0:T(8,128)(2,1)}, bf16[1,2688,1024]{2,1,0:T(8,128)(2,1)S(1)}, u32[]{:S(2)}) %copy-start) | copy-done | bytes 5505048
  34.2 0.0 collective-permute-done.3.refs_0_
  34.2 0.0 collective-permute-done.4.refs_1_
  34.2 15.6 %shard_map.67 = (bf16[64,2688]{1,0:T(8,128)(2,1)S(1)}, bf16[3,2688,512]{2,1,0:T(8,128)(2,1)S(1)}) custom-call(bf16[32,3072]{1,0:T(8,128)(2,1)S(1)} %collective-permute-done.3.refs_0_, bf16[32,3072]{1,0:T(8,128)(2,1)S(1)} %collective-permute-done.4.refs_1_, f32[2688,64]{1,0:T(8,128)S(1)} %get-tuple-element.31.refs_2_, ...), custom_call_target="tpu_custom_call" | custom-call | flops 2113929216 | bytes 33030144 | tf_op jit(solution)/shard_map/pallas_call | solution.py:28
  49.8 4.1 %shard_map.69 = (bf16[1,32,3072]{2,1,0:T(8,128)(2,1)S(1)}, bf16[1,32,3072]{2,1,0:T(8,128)(2,1)S(1)}) custom-call(bf16[64,2688]{1,0:T(8,128)(2,1)S(1)} %get-tuple-element.35.hidden, bf16[32,3200]{1,0:T(8,128)(2,1)S(1)} %constant_dynamic-update-slice_fusion.refs_0_.own, bf16[32,3200]{1,0:T(8,128)(2,1)S(1)} %collective-permute-done.5.refs_1_.other, ...), custom_call_target="tpu_custom_call" | custom-call | flops 1056964608 | bytes 16515072 | tf_op jit(solution)/shard_map/pallas_call | solution.py:28
  53.9 1.8 %collective-permute-start.6 = (bf16[32,3072]{1,0:T(8,128)(2,1)S(1)}, bf16[32,3072]{1,0:T(8,128)(2,1)S(1)}, u32[]{:S(2)}, u32[]{:S(2)}) collective-permute-start(bf16[32,3072]{1,0:T(8,128)(2,1)S(1)} %bitcast.13), channel_id=1, source_target_pairs={{0,1},{1,0},{2,3},{3,2},{4,5},{5,4},{6,7},{7,6},{8,9},{9,8},{10,11... | collective-permute-start | bytes 589832 | tf_op jit(solution)/shard_map/ppermute | solution.py:347
  55.7 0.0 collective-permute-start.7
  55.7 6.7 %shard_map.68 = (f32[1,32,3072]{2,1,0:T(8,128)S(1)}, bf16[1,32,3072]{2,1,0:T(8,128)(2,1)S(1)}) custom-call(bf16[64,2688]{1,0:T(8,128)(2,1)S(1)} %get-tuple-element.35.hidden, bf16[32,3200]{1,0:T(8,128)(2,1)S(1)} %constant_dynamic-update-slice_fusion.refs_0_.own, bf16[32,3200]{1,0:T(8,128)(2,1)S(1)} %collective-permute-done.5.refs_1_.other, ...), custom_call_target="tpu_custom_call" | custom-call | flops 1056964608 | bytes 16515072 | tf_op jit(solution)/shard_map/pallas_call | solution.py:28
  62.4 0.5 collective-permute-start.8
  62.9 0.0 collective-permute-done.6
  62.9 1.7 %collective-permute-done.7 = bf16[32,3072]{1,0:T(8,128)(2,1)S(1)} collective-permute-done((bf16[32,3072]{1,0:T(8,128)(2,1)S(1)}, bf16[32,3072]{1,0:T(8,128)(2,1)S(1)}, u32[]{:S(2)}, u32[]{:S(2)}) %collective-permute-start.7) | collective-permute-done | bytes 196640 | tf_op jit(solution)/shard_map/ppermute | solution.py:348
  64.6 0.0 collective-permute-done.8
  64.6 0.1 fusion.5
  64.8 1.0 %collective-permute-start.9 = (bf16[16,3072]{1,0:T(8,128)(2,1)S(1)}, bf16[16,3072]{1,0:T(8,128)(2,1)S(1)}, u32[]{:S(2)}, u32[]{:S(2)}) collective-permute-start(bf16[16,3072]{1,0:T(8,128)(2,1)S(1)} %pad_maximum_fusion), channel_id=1, source_target_pairs={{0,4},{2,6},{4,0},{6,2},{8,12},{10,14},{12,8},{14,10},{1,5},{3,7},... | collective-permute-start | bytes 294920 | tf_op jit(solution)/shard_map/ppermute | solution.py:359
  65.8 4.2 %collective-permute-done.9 = bf16[16,3072]{1,0:T(8,128)(2,1)S(1)} collective-permute-done((bf16[16,3072]{1,0:T(8,128)(2,1)S(1)}, bf16[16,3072]{1,0:T(8,128)(2,1)S(1)}, u32[]{:S(2)}, u32[]{:S(2)}) %collective-permute-start.9) | collective-permute-done | bytes 98336 | tf_op jit(solution)/shard_map/ppermute | solution.py:359
  70.1 2.7 %collective-permute-start.10 = (bf16[8,3072]{1,0:T(8,128)(2,1)S(1)}, bf16[8,3072]{1,0:T(8,128)(2,1)S(1)}, u32[]{:S(2)}, u32[]{:S(2)}) collective-permute-start(bf16[8,3072]{1,0:T(8,128)(2,1)S(1)} %fusion.2), channel_id=1, source_target_pairs={{0,8},{2,10},{4,12},{6,14},{8,0},{10,2},{12,4},{14,6},{1,9},{3,11}... | collective-permute-start | bytes 147464 | tf_op jit(solution)/shard_map/ppermute | solution.py:359
  72.8 2.8 %collective-permute-done.10 = bf16[8,3072]{1,0:T(8,128)(2,1)S(1)} collective-permute-done((bf16[8,3072]{1,0:T(8,128)(2,1)S(1)}, bf16[8,3072]{1,0:T(8,128)(2,1)S(1)}, u32[]{:S(2)}, u32[]{:S(2)}) %collective-permute-start.10) | collective-permute-done | bytes 49184 | tf_op jit(solution)/shard_map/ppermute | solution.py:359
  75.5 0.6 fusion.4
  (11 shorter events, 0.1 us)
Async XLA Ops:
  0.9 12.3 %collective-permute-start = (bf16[8,3200]{1,0:T(8,128)(2,1)S(1)}, bf16[8,3200]{1,0:T(8,128)(2,1)S(1)}, u32[]{:S(2)}, u32[]{:S(2)}) collective-permute-start(bf16[8,3200]{1,0:T(8,128)(2,1)S(1)} %shard_map.64.after), channel_id=1, source_target_pairs={{0,4},{2,6},{4,0},{6,2},{8,12},{10,14},{12,8},{14,10},{1,5},{3,7},... | collective-permute-start | bytes 153608 | tf_op jit(solution)/shard_map/ppermute | solution.py:291
  4.0 9.2 %collective-permute-start.1 = (bf16[8,3200]{1,0:T(8,128)(2,1)S(1)}, bf16[8,3200]{1,0:T(8,128)(2,1)S(1)}, u32[]{:S(2)}, u32[]{:S(2)}) collective-permute-start(bf16[8,3200]{1,0:T(8,128)(2,1)S(1)} %shard_map.64.after), channel_id=1, source_target_pairs={{0,8},{2,10},{4,12},{6,14},{8,0},{10,2},{12,4},{14,6},{1,9},{3,11}... | collective-permute-start | bytes 153608 | tf_op jit(solution)/shard_map/ppermute | solution.py:291
  6.5 6.7 %collective-permute-start.2 = (bf16[8,3200]{1,0:T(8,128)(2,1)S(1)}, bf16[8,3200]{1,0:T(8,128)(2,1)S(1)}, u32[]{:S(2)}, u32[]{:S(2)}) collective-permute-start(bf16[8,3200]{1,0:T(8,128)(2,1)S(1)} %shard_map.64.after), channel_id=1, source_target_pairs={{0,12},{2,14},{4,8},{6,10},{8,4},{10,6},{12,0},{14,2},{1,13},{3,15... | collective-permute-start | bytes 153608 | tf_op jit(solution)/shard_map/ppermute | solution.py:291
  10.8 2.4 %copy-start.1 = (bf16[1,2688,1024]{2,1,0:T(8,128)(2,1)}, bf16[1,2688,1024]{2,1,0:T(8,128)(2,1)S(1)}, u32[]{:S(2)}) copy-start(bf16[1,2688,1024]{2,1,0:T(8,128)(2,1)S(1)} %get-tuple-element.30.refs_3_) | copy-start | bytes 16515076
  13.3 2.1 %collective-permute-start.5 = (bf16[32,3200]{1,0:T(8,128)(2,1)S(1)}, bf16[32,3200]{1,0:T(8,128)(2,1)S(1)}, u32[]{:S(2)}, u32[]{:S(2)}) collective-permute-start(bf16[32,3200]{1,0:T(8,128)(2,1)S(1)} %constant_dynamic-update-slice_fusion.refs_0_.own), channel_id=1, source_target_pairs={{0,2},{2,0},{4,6},{6,4},{8,10},{10,8},{12,14},{14,12},{1,3},{3,1},... | collective-permute-start | bytes 614408 | tf_op jit(solution)/shard_map/ppermute | solution.py:294
  13.4 20.8 %collective-permute-start.3 = (bf16[32,3072]{1,0:T(8,128)(2,1)S(1)}, bf16[32,3072]{1,0:T(8,128)(2,1)S(1)}, u32[]{:S(2)}, u32[]{:S(2)}) collective-permute-start(bf16[32,3072]{1,0:T(8,128)(2,1)S(1)} %slice.30), channel_id=1, source_target_pairs={{0,1},{1,0},{2,3},{3,2},{4,5},{5,4},{6,7},{7,6},{8,9},{9,8},{10,11... | collective-permute-start | bytes 589832 | tf_op jit(solution)/shard_map/ppermute | solution.py:298
  15.1 19.1 %collective-permute-start.4 = (bf16[32,3072]{1,0:T(8,128)(2,1)S(1)}, bf16[32,3072]{1,0:T(8,128)(2,1)S(1)}, u32[]{:S(2)}, u32[]{:S(2)}) collective-permute-start(bf16[32,3072]{1,0:T(8,128)(2,1)S(1)} %slice.30), channel_id=1, source_target_pairs={{0,3},{1,2},{2,1},{3,0},{4,7},{5,6},{6,5},{7,4},{8,11},{9,10},{10,... | collective-permute-start | bytes 589832 | tf_op jit(solution)/shard_map/ppermute | solution.py:299
  31.8 2.4 %copy-start = (bf16[1,2688,1024]{2,1,0:T(8,128)(2,1)}, bf16[1,2688,1024]{2,1,0:T(8,128)(2,1)S(1)}, u32[]{:S(2)}) copy-start(bf16[1,2688,1024]{2,1,0:T(8,128)(2,1)S(1)} %get-tuple-element.34.refs_5_) | copy-start | bytes 16515076
  53.9 9.0 %collective-permute-start.6 = (bf16[32,3072]{1,0:T(8,128)(2,1)S(1)}, bf16[32,3072]{1,0:T(8,128)(2,1)S(1)}, u32[]{:S(2)}, u32[]{:S(2)}) collective-permute-start(bf16[32,3072]{1,0:T(8,128)(2,1)S(1)} %bitcast.13), channel_id=1, source_target_pairs={{0,1},{1,0},{2,3},{3,2},{4,5},{5,4},{6,7},{7,6},{8,9},{9,8},{10,11... | collective-permute-start | bytes 589832 | tf_op jit(solution)/shard_map/ppermute | solution.py:347
  55.7 8.9 %collective-permute-start.7 = (bf16[32,3072]{1,0:T(8,128)(2,1)S(1)}, bf16[32,3072]{1,0:T(8,128)(2,1)S(1)}, u32[]{:S(2)}, u32[]{:S(2)}) collective-permute-start(bf16[32,3072]{1,0:T(8,128)(2,1)S(1)} %bitcast.12), channel_id=1, source_target_pairs={{0,3},{1,2},{2,1},{3,0},{4,7},{5,6},{6,5},{7,4},{8,11},{9,10},{10,... | collective-permute-start | bytes 589832 | tf_op jit(solution)/shard_map/ppermute | solution.py:348
  62.4 2.2 %collective-permute-start.8 = (bf16[32,3072]{1,0:T(8,128)(2,1)S(1)}, bf16[32,3072]{1,0:T(8,128)(2,1)S(1)}, u32[]{:S(2)}, u32[]{:S(2)}) collective-permute-start(bf16[32,3072]{1,0:T(8,128)(2,1)S(1)} %bitcast.14), channel_id=1, source_target_pairs={{0,2},{2,0},{4,6},{6,4},{8,10},{10,8},{12,14},{14,12},{1,3},{3,1},... | collective-permute-start | bytes 589832 | tf_op jit(solution)/shard_map/ppermute | solution.py:350
  64.8 5.3 %collective-permute-start.9 = (bf16[16,3072]{1,0:T(8,128)(2,1)S(1)}, bf16[16,3072]{1,0:T(8,128)(2,1)S(1)}, u32[]{:S(2)}, u32[]{:S(2)}) collective-permute-start(bf16[16,3072]{1,0:T(8,128)(2,1)S(1)} %pad_maximum_fusion), channel_id=1, source_target_pairs={{0,4},{2,6},{4,0},{6,2},{8,12},{10,14},{12,8},{14,10},{1,5},{3,7},... | collective-permute-start | bytes 294920 | tf_op jit(solution)/shard_map/ppermute | solution.py:359
  70.1 5.5 %collective-permute-start.10 = (bf16[8,3072]{1,0:T(8,128)(2,1)S(1)}, bf16[8,3072]{1,0:T(8,128)(2,1)S(1)}, u32[]{:S(2)}, u32[]{:S(2)}) collective-permute-start(bf16[8,3072]{1,0:T(8,128)(2,1)S(1)} %fusion.2), channel_id=1, source_target_pairs={{0,8},{2,10},{4,12},{6,14},{8,0},{10,2},{12,4},{14,6},{1,9},{3,11}... | collective-permute-start | bytes 147464 | tf_op jit(solution)/shard_map/ppermute | solution.py:359

commit v5 on v3

--- a/solution.py
+++ b/solution.py
@@ -192,12 +192,13 @@
     finish(ahead)
 
 
-def down_kernel(start, count, held, experts, shares, hidden, own, other, *refs):
+def down_kernel(width, start, count, held, more, experts, shares, hidden, own, other, *refs):
     down_held, refs = (refs[0], refs[1:]) if held else (None, refs)
-    w_down, *outs, ring, sems = refs
-    unused, half, width = outs[0].shape
+    w_down, *outs, ring, sems, next_sems = refs
+    down_next = outs.pop() if more else None
+    unused, half, span = outs[0].shape
     fb = ring.shape[-1]
-    per = width // fb
+    per, inside = width // fb, span // fb
     expert = lax.axis_index("expert") // shares
     packed = jnp.concatenate([own[:, width:], other[:, width:]], axis=0).astype(F32)
     lane = lax.broadcasted_iota(jnp.int32, packed.shape, 1)
@@ -209,9 +210,9 @@
 
     def put(step, block):
         value = jnp.dot(hidden[...], block, preferred_element_type=F32) * coef
-        columns = pl.ds(pl.multiple_of(lax.rem(step, per) * fb, LANES), fb)
+        columns = pl.ds(pl.multiple_of(lax.rem(step, inside) * fb, LANES), fb)
         for at, out in enumerate(outs):
-            out[step // per, :, columns] = value[at * half : (at + 1) * half].astype(out.dtype)
+            out[step // inside, :, columns] = value[at * half : (at + 1) * half].astype(out.dtype)
 
     def from_held(step):
         put(step, down_held[step])
@@ -220,7 +221,11 @@
         waits[0].wait()
         put(step, ring[slot])
 
-    stream(held, count, fetch, (), lambda: None, from_held, from_ring)
+    ahead = []
+    for k in range(more):
+        ahead += moves((w_down,), k, per, (down_next.at[k],), (next_sems.at[k],))
+    stream(held, count, fetch, ahead, lambda: None, from_held, from_ring)
+    finish(ahead)
 
 
 def body(tokens, expert_ids, route_weight, w_gate, w_up, w_down):
@@ -272,7 +277,7 @@
     kb = largest_step(width, (512, 384, 256, 128))
     per = width // kb
     steps = per * (n_blk - 1)
-    first_held, second_held, third_held = min(3, per), min(2, steps), min(3, steps)
+    first_held, second_held, third_held = min(2, per), min(2, steps), min(3, steps)
 
     def blocks(count):
         return pltpu.VMEM((count, hid, kb), BF16)
@@ -331,27 +336,36 @@
         (*sent, *partial_sums, gate_held, up_held),
     )
 
-    def down(first, count, kinds, *down_held):
-        held = third_held if down_held else 0
+    def down(hidden, first, count, more, *down_held):
+        held = down_held[0].shape[0] if down_held else 0
+        span = min(count, per)
+        shape = (count // span, half, span * kb)
         return call(
-            functools.partial(down_kernel, first, count, held, experts, shares),
-            [jax.ShapeDtypeStruct((count // per, half, width), kind) for kind in kinds],
+            functools.partial(down_kernel, width, first, count, held, more, experts, shares),
+            [jax.ShapeDtypeStruct(shape, F32), jax.ShapeDtypeStruct(shape, BF16)] + [blocks(more)] * (more > 0),
             (hidden, own, other, *down_held, w_down),
             (vmem,) * (3 + len(down_held)) + (hbm,),
-            [blocks(SLOTS), pltpu.SemaphoreType.DMA((SLOTS,))],
+            [
+                blocks(min(SLOTS, max(count - held, 1))),
+                pltpu.SemaphoreType.DMA((SLOTS,)),
+                pltpu.SemaphoreType.DMA((max(more, 1),)),
+            ],
             14,
             2 * tokens_all * hid * kb * count,
             2 * hid * kb * count,
         )
 
-    away = down(per, steps, (BF16, BF16), down_held)
-    total = []
-    for j in range(1, n_blk):
-        total.append(lax.ppermute(away[0][j - 1], "blk", across(j)))
-        total.append(lax.ppermute(away[1][j - 1], ("expert", "blk"), across_other(j)))
-    kept, given = down(0, per, (F32, BF16))
-    total.append(lax.ppermute(given[0], "expert", swap))
-    summed = kept[0]
+    early = per // 3
+    away, given, *early_held = down(hidden, per, steps, early, down_held)
+    given = lax.ppermute(given, "expert", swap)
+    parts = [down(hidden, 0, early, 0, *early_held)] if early else []
+    away = (away + given.astype(F32)).astype(BF16)
+    away, hidden = lax.optimization_barrier((away, hidden))
+    away = jnp.pad(away, ((0, 0), (0, 0), (0, room)))
+    total = [lax.ppermute(away[j - 1], "blk", across(j))[:, :width] for j in range(1, n_blk)]
+    parts.append(down(hidden, early, per - early, 0))
+    kept, given = (jnp.concatenate([part[at][0] for part in parts], axis=1) for at in range(2))
+    summed = kept + lax.ppermute(given, "expert", swap).astype(F32)
     for term in total:
         summed = summed + term.astype(F32)
     mixed = summed[:rows]

time: 61.2 us -> 60.9 us (level)
    pallas_call x6 -> x7, Pallas kernels: 39.5 us -> 39.8 us  [call(): pl.pallas_call(kernel, out_shape=outs, in_specs=[pl.BlockSpec(memory_spac...]
  transfers between devices with their start and end apart: 12 -> 12, of which waited for: 3 -> 3; matrix products, arithmetic and copies ran while one was open for 0% -> 0% of each run, Pallas kernels for 38% -> 37%
where the time goes in v5:
time: 60.9 us; the launch traced here: 60.7 us
  Pallas kernels  39.8 us (65%)
  starting transfers between devices  15.2 us (25%)
  waiting for transfers between devices  4.61 us (8%)
  other arithmetic  0.78 us (1%)
    pallas_call x7, Pallas kernels, call(): pl.pallas_call(kernel, out_shape=outs, in_specs=[pl.BlockSpec(memory_spac...  39.8 us
    ppermute x3, starting transfers between devices, body(): lax.ppermute(packed, 'expert', along(k))  7.01 us
    ppermute x3, starting transfers between devices, body(): mixed = mixed + lax.ppermute(piece, 'expert', along(-k)).astype(F32)  4.22 us
    ppermute x3, waiting for transfers between devices, body(): mixed = mixed + lax.ppermute(piece, 'expert', along(-k)).astype(F32)  3.16 us
    ppermute x1, starting transfers between devices, body(): lax.ppermute(away[j - 1], 'blk', across(j))[:, :width]  1.56 us
    ppermute x1, starting transfers between devices, body(): sent.append(lax.ppermute(bare, 'blk', across(-j)))  1.56 us
    ppermute x1, waiting for transfers between devices, body(): summed = kept + lax.ppermute(given, 'expert', swap).astype(F32)  1.43 us
  transfers between devices with their start and end apart: 12, of which 3 were waited for; matrix products, arithmetic and copies ran while one was open for 0% of the time, Pallas kernels for 37%

profile of v5, /device:TPU:0, one launch (start us, length us, event | category | flops | bytes accessed | tf_op | source)
XLA Modules:
  0.0 60.7 jit_solution(18141528290944473400)
XLA Ops:
  0.0 0.9 %shard_map.64.after = bf16[8,3200]{1,0:T(8,128)(2,1)S(1)} custom-call(bf16[8,3072]{1,0:T(8,128)(2,1)} %tokens.1, s32[4,8]{1,0:T(4,128)} %bitcast.12, f32[4,8]{1,0:T(4,128)} %bitcast.13), custom_call_target="tpu_custom_call" | custom-call | flops 1024 | bytes 98304 | tf_op jit(solution)/shard_map/pallas_call | solution.py:27
  0.9 3.1 %collective-permute-start = (bf16[8,3200]{1,0:T(8,128)(2,1)S(1)}, bf16[8,3200]{1,0:T(8,128)(2,1)S(1)}, u32[]{:S(2)}, u32[]{:S(2)}) collective-permute-start(bf16[8,3200]{1,0:T(8,128)(2,1)S(1)} %shard_map.64.after), channel_id=1, source_target_pairs={{0,4},{2,6},{4,8},{6,10},{8,12},{10,14},{12,0},{14,2},{1,5},{3,7},... | collective-permute-start | bytes 153608 | tf_op jit(solution)/shard_map/ppermute | solution.py:295
  3.9 2.6 %collective-permute-start.1 = (bf16[8,3200]{1,0:T(8,128)(2,1)S(1)}, bf16[8,3200]{1,0:T(8,128)(2,1)S(1)}, u32[]{:S(2)}, u32[]{:S(2)}) collective-permute-start(bf16[8,3200]{1,0:T(8,128)(2,1)S(1)} %shard_map.64.after), channel_id=1, source_target_pairs={{0,8},{2,10},{4,12},{6,14},{8,0},{10,2},{12,4},{14,6},{1,9},{3,11}... | collective-permute-start | bytes 153608 | tf_op jit(solution)/shard_map/ppermute | solution.py:295
  6.5 1.3 %collective-permute-start.2 = (bf16[8,3200]{1,0:T(8,128)(2,1)S(1)}, bf16[8,3200]{1,0:T(8,128)(2,1)S(1)}, u32[]{:S(2)}, u32[]{:S(2)}) collective-permute-start(bf16[8,3200]{1,0:T(8,128)(2,1)S(1)} %shard_map.64.after), channel_id=1, source_target_pairs={{0,12},{2,14},{4,0},{6,2},{8,4},{10,6},{12,8},{14,10},{1,13},{3,15... | collective-permute-start | bytes 153608 | tf_op jit(solution)/shard_map/ppermute | solution.py:295
  7.9 4.3 %shard_map.65 = (bf16[2,2688,512]{2,1,0:T(8,128)(2,1)S(1)}, bf16[2,2688,512]{2,1,0:T(8,128)(2,1)S(1)}) custom-call(bf16[8,3200]{1,0:T(8,128)(2,1)S(1)} %shard_map.64.after, bf16[1,2688,6144]{2,1,0:T(8,128)(2,1)} %refs_6_.1, bf16[1,2688,6144]{2,1,0:T(8,128)(2,1)} %refs_7_.1), custom_call_target="tpu_custom_call" | custom-call | bytes 11010048 | tf_op jit(solution)/shard_map/pallas_call | solution.py:27
  12.2 0.0 collective-permute-done
  12.2 0.0 collective-permute-done.1
  12.2 0.0 collective-permute-done.2
  12.3 0.1 collective-permute-start.5
  12.4 1.6 %collective-permute-start.3 = (bf16[32,3072]{1,0:T(8,128)(2,1)S(1)}, bf16[32,3072]{1,0:T(8,128)(2,1)S(1)}, u32[]{:S(2)}, u32[]{:S(2)}) collective-permute-start(bf16[32,3072]{1,0:T(8,128)(2,1)S(1)} %slice.27), channel_id=1, source_target_pairs={{0,1},{1,0},{2,3},{3,2},{4,5},{5,4},{6,7},{7,6},{8,9},{9,8},{10,11... | collective-permute-start | bytes 589832 | tf_op jit(solution)/shard_map/ppermute | solution.py:302
  13.9 0.4 collective-permute-start.4
  14.3 0.0 collective-permute-done.5.refs_1_.other
  14.3 11.6 %shard_map.66 = (f32[2688,64]{1,0:T(8,128)S(1)}, f32[2688,64]{1,0:T(8,128)S(1)}, bf16[2,2688,512]{2,1,0:T(8,128)(2,1)S(1)}, bf16[2,2688,512]{2,1,0:T(8,128)(2,1)S(1)}) custom-call(bf16[32,3200]{1,0:T(8,128)(2,1)S(1)} %constant_dynamic-update-slice_fusion.refs_0_.own, bf16[32,3200]{1,0:T(8,128)(2,1)S(1)} %collective-permute-done.5.refs_1_.other, ...), custom_call_target="tpu_custom_call" | custom-call | flops 2113929216 | bytes 33030144 | tf_op jit(solution)/shard_map/pallas_call | solution.py:27
  25.9 0.0 collective-permute-done.3.refs_0_
  25.9 0.0 collective-permute-done.4.refs_1_
  25.9 11.3 %shard_map.67 = (bf16[64,2688]{1,0:T(8,128)(2,1)S(1)}, bf16[3,2688,512]{2,1,0:T(8,128)(2,1)S(1)}) custom-call(bf16[32,3072]{1,0:T(8,128)(2,1)S(1)} %collective-permute-done.3.refs_0_, bf16[32,3072]{1,0:T(8,128)(2,1)S(1)} %collective-permute-done.4.refs_1_, f32[2688,64]{1,0:T(8,128)S(1)} %get-tuple-element.36.refs_2_, ...), custom_call_target="tpu_custom_call" | custom-call | flops 2113929216 | bytes 33030144 | tf_op jit(solution)/shard_map/pallas_call | solution.py:27
  37.2 5.3 %shard_map.68 = (f32[1,32,3072]{2,1,0:T(8,128)S(1)}, bf16[1,32,3072]{2,1,0:T(8,128)(2,1)S(1)}, bf16[2,2688,512]{2,1,0:T(8,128)(2,1)S(1)}) custom-call(bf16[64,2688]{1,0:T(8,128)(2,1)S(1)} %get-tuple-element.46.hidden, bf16[32,3200]{1,0:T(8,128)(2,1)S(1)} %constant_dynamic-update-slice_fusion.refs_0_.own, ...), custom_call_target="tpu_custom_call" | custom-call | flops 1056964608 | bytes 16515072 | tf_op jit(solution)/shard_map/pallas_call | solution.py:27
  42.6 0.4 collective-permute-start.6
  42.9 1.3 %shard_map.69 = (f32[1,32,1024]{2,1,0:T(8,128)S(1)}, bf16[1,32,1024]{2,1,0:T(8,128)(2,1)S(1)}) custom-call(bf16[64,2688]{1,0:T(8,128)(2,1)S(1)} %get-tuple-element.46.hidden, bf16[32,3200]{1,0:T(8,128)(2,1)S(1)} %constant_dynamic-update-slice_fusion.refs_0_.own, bf16[32,3200]{1,0:T(8,128)(2,1)S(1)} %collective-permute-done.5.refs_1_.other, ...), custom_call_target="tpu_custom_call" | custom-call | flops 352321536 | bytes 5505024 | tf_op jit(solution)/shard_map/pallas_call | solution.py:27
  44.3 0.1 add_convert_fusion
  44.3 1.6 %collective-permute-start.8 = (bf16[32,3200]{1,0:T(8,128)(2,1)S(1)}, bf16[32,3200]{1,0:T(8,128)(2,1)S(1)}, u32[]{:S(2)}, u32[]{:S(2)}) collective-permute-start(bf16[32,3200]{1,0:T(8,128)(2,1)S(1)} %pad_bitcast_fusion), channel_id=1, source_target_pairs={{0,1},{1,0},{2,3},{3,2},{4,5},{5,4},{6,7},{7,6},{8,9},{9,8},{10,11... | collective-permute-start | bytes 614408 | tf_op jit(solution)/shard_map/ppermute | solution.py:365
  45.9 5.1 %shard_map.70 = (f32[1,32,2048]{2,1,0:T(8,128)S(1)}, bf16[1,32,2048]{2,1,0:T(8,128)(2,1)S(1)}) custom-call(bf16[64,2688]{1,0:T(8,128)(2,1)S(1)} %get-tuple-element.46.hidden, bf16[32,3200]{1,0:T(8,128)(2,1)S(1)} %constant_dynamic-update-slice_fusion.refs_0_.own, bf16[32,3200]{1,0:T(8,128)(2,1)S(1)} %collective-permute-done.5.refs_1_.other, ...), custom_call_target="tpu_custom_call" | custom-call | flops 704643072 | bytes 11010048 | tf_op jit(solution)/shard_map/pallas_call | solution.py:27
  51.1 0.1 collective-permute-start.7
  51.1 1.4 %collective-permute-done.7 = bf16[32,3072]{1,0:T(8,128)(2,1)S(1)} collective-permute-done((bf16[32,3072]{1,0:T(8,128)(2,1)S(1)}, bf16[32,3072]{1,0:T(8,128)(2,1)S(1)}, u32[]{:S(2)}, u32[]{:S(2)}) %collective-permute-start.7) | collective-permute-done | bytes 196640 | tf_op jit(solution)/shard_map/ppermute | solution.py:368
  52.6 0.1 fusion.4
  52.7 0.4 collective-permute-start.10
  53.1 1.8 %collective-permute-start.11 = (bf16[8,3072]{1,0:T(8,128)(2,1)S(1)}, bf16[8,3072]{1,0:T(8,128)(2,1)S(1)}, u32[]{:S(2)}, u32[]{:S(2)}) collective-permute-start(bf16[8,3072]{1,0:T(8,128)(2,1)S(1)} %get-tuple-element.54), channel_id=1, source_target_pairs={{0,4},{2,6},{4,8},{6,10},{8,12},{10,14},{12,0},{14,2},{1,5},{3,7},... | collective-permute-start | bytes 147464 | tf_op jit(solution)/shard_map/ppermute | solution.py:374
  54.9 2.0 %collective-permute-start.9 = (bf16[8,3072]{1,0:T(8,128)(2,1)S(1)}, bf16[8,3072]{1,0:T(8,128)(2,1)S(1)}, u32[]{:S(2)}, u32[]{:S(2)}) collective-permute-start(bf16[8,3072]{1,0:T(8,128)(2,1)S(1)} %get-tuple-element.53), channel_id=1, source_target_pairs={{0,12},{2,14},{4,0},{6,2},{8,4},{10,6},{12,8},{14,10},{1,13},{3,15... | collective-permute-start | bytes 147464 | tf_op jit(solution)/shard_map/ppermute | solution.py:374
  56.9 2.9 %collective-permute-done.10 = bf16[8,3072]{1,0:T(8,128)(2,1)S(1)} collective-permute-done((bf16[8,3072]{1,0:T(8,128)(2,1)S(1)}, bf16[8,3072]{1,0:T(8,128)(2,1)S(1)}, u32[]{:S(2)}, u32[]{:S(2)}) %collective-permute-start.10) | collective-permute-done | bytes 49184 | tf_op jit(solution)/shard_map/ppermute | solution.py:374
  59.8 0.0 collective-permute-done.11
  59.8 0.2 collective-permute-done.9
  60.1 0.6 %fusion.3 = bf16[8,3072]{1,0:T(8,128)(2,1)} fusion(f32[32,3072]{1,0:T(8,128)S(1)} %get-tuple-element.52, bf16[8,3072]{1,0:T(8,128)(2,1)S(1)} %collective-permute-done.11, bf16[8,3072]{1,0:T(8,128)(2,1)S(1)} %collective-permute-done.10, bf16[8,3072]{1,0:T(8,128)(2,1)S(1)} %collective-permute-done.9), kind=kLoop, calls=%fused_computation.8 | loop fusion | flops 172032 | bytes 294912 | tf_op jit(solution)/shard_map/convert_element_type | solution.py:375
  (10 shorter events, 0.1 us)
Async XLA Ops:
  0.9 11.3 %collective-permute-start = (bf16[8,3200]{1,0:T(8,128)(2,1)S(1)}, bf16[8,3200]{1,0:T(8,128)(2,1)S(1)}, u32[]{:S(2)}, u32[]{:S(2)}) collective-permute-start(bf16[8,3200]{1,0:T(8,128)(2,1)S(1)} %shard_map.64.after), channel_id=1, source_target_pairs={{0,4},{2,6},{4,8},{6,10},{8,12},{10,14},{12,0},{14,2},{1,5},{3,7},... | collective-permute-start | bytes 153608 | tf_op jit(solution)/shard_map/ppermute | solution.py:295
  3.9 8.2 %collective-permute-start.1 = (bf16[8,3200]{1,0:T(8,128)(2,1)S(1)}, bf16[8,3200]{1,0:T(8,128)(2,1)S(1)}, u32[]{:S(2)}, u32[]{:S(2)}) collective-permute-start(bf16[8,3200]{1,0:T(8,128)(2,1)S(1)} %shard_map.64.after), channel_id=1, source_target_pairs={{0,8},{2,10},{4,12},{6,14},{8,0},{10,2},{12,4},{14,6},{1,9},{3,11}... | collective-permute-start | bytes 153608 | tf_op jit(solution)/shard_map/ppermute | solution.py:295
  6.5 5.7 %collective-permute-start.2 = (bf16[8,3200]{1,0:T(8,128)(2,1)S(1)}, bf16[8,3200]{1,0:T(8,128)(2,1)S(1)}, u32[]{:S(2)}, u32[]{:S(2)}) collective-permute-start(bf16[8,3200]{1,0:T(8,128)(2,1)S(1)} %shard_map.64.after), channel_id=1, source_target_pairs={{0,12},{2,14},{4,0},{6,2},{8,4},{10,6},{12,8},{14,10},{1,13},{3,15... | collective-permute-start | bytes 153608 | tf_op jit(solution)/shard_map/ppermute | solution.py:295
  12.3 2.0 %collective-permute-start.5 = (bf16[32,3200]{1,0:T(8,128)(2,1)S(1)}, bf16[32,3200]{1,0:T(8,128)(2,1)S(1)}, u32[]{:S(2)}, u32[]{:S(2)}) collective-permute-start(bf16[32,3200]{1,0:T(8,128)(2,1)S(1)} %constant_dynamic-update-slice_fusion.refs_0_.own), channel_id=1, source_target_pairs={{0,2},{2,0},{4,6},{6,4},{8,10},{10,8},{12,14},{14,12},{1,3},{3,1},... | collective-permute-start | bytes 614408 | tf_op jit(solution)/shard_map/ppermute | solution.py:298
  12.4 13.5 %collective-permute-start.3 = (bf16[32,3072]{1,0:T(8,128)(2,1)S(1)}, bf16[32,3072]{1,0:T(8,128)(2,1)S(1)}, u32[]{:S(2)}, u32[]{:S(2)}) collective-permute-start(bf16[32,3072]{1,0:T(8,128)(2,1)S(1)} %slice.27), channel_id=1, source_target_pairs={{0,1},{1,0},{2,3},{3,2},{4,5},{5,4},{6,7},{7,6},{8,9},{9,8},{10,11... | collective-permute-start | bytes 589832 | tf_op jit(solution)/shard_map/ppermute | solution.py:302
  13.9 12.0 %collective-permute-start.4 = (bf16[32,3072]{1,0:T(8,128)(2,1)S(1)}, bf16[32,3072]{1,0:T(8,128)(2,1)S(1)}, u32[]{:S(2)}, u32[]{:S(2)}) collective-permute-start(bf16[32,3072]{1,0:T(8,128)(2,1)S(1)} %slice.27), channel_id=1, source_target_pairs={{0,3},{1,2},{2,1},{3,0},{4,7},{5,6},{6,5},{7,4},{8,11},{9,10},{10,... | collective-permute-start | bytes 589832 | tf_op jit(solution)/shard_map/ppermute | solution.py:303
  42.6 1.7 %collective-permute-start.6 = (bf16[1,32,3072]{2,1,0:T(8,128)(2,1)S(1)}, bf16[1,32,3072]{2,1,0:T(8,128)(2,1)S(1)}, u32[]{:S(2)}, u32[]{:S(2)}) collective-permute-start(bf16[1,32,3072]{2,1,0:T(8,128)(2,1)S(1)} %get-tuple-element.45), channel_id=1, source_target_pairs={{0,2},{2,0},{4,6},{6,4},{8,10},{10,8},{12,14},{14,12},{1,3},{3,1},... | collective-permute-start | bytes 589832 | tf_op jit(solution)/shard_map/ppermute | solution.py:360
  44.3 8.2 %collective-permute-start.8 = (bf16[32,3200]{1,0:T(8,128)(2,1)S(1)}, bf16[32,3200]{1,0:T(8,128)(2,1)S(1)}, u32[]{:S(2)}, u32[]{:S(2)}) collective-permute-start(bf16[32,3200]{1,0:T(8,128)(2,1)S(1)} %pad_bitcast_fusion), channel_id=1, source_target_pairs={{0,1},{1,0},{2,3},{3,2},{4,5},{5,4},{6,7},{7,6},{8,9},{9,8},{10,11... | collective-permute-start | bytes 614408 | tf_op jit(solution)/shard_map/ppermute | solution.py:365
  51.1 1.5 %collective-permute-start.7 = (bf16[32,3072]{1,0:T(8,128)(2,1)S(1)}, bf16[32,3072]{1,0:T(8,128)(2,1)S(1)}, u32[]{:S(2)}, u32[]{:S(2)}) collective-permute-start(bf16[32,3072]{1,0:T(8,128)(2,1)S(1)} %pad_maximum_fusion), channel_id=1, source_target_pairs={{0,2},{2,0},{4,6},{6,4},{8,10},{10,8},{12,14},{14,12},{1,3},{3,1},... | collective-permute-start | bytes 589832 | tf_op jit(solution)/shard_map/ppermute | solution.py:368
  52.7 7.2 %collective-permute-start.10 = (bf16[8,3072]{1,0:T(8,128)(2,1)S(1)}, bf16[8,3072]{1,0:T(8,128)(2,1)S(1)}, u32[]{:S(2)}, u32[]{:S(2)}) collective-permute-start(bf16[8,3072]{1,0:T(8,128)(2,1)S(1)} %get-tuple-element.55), channel_id=1, source_target_pairs={{0,8},{2,10},{4,12},{6,14},{8,0},{10,2},{12,4},{14,6},{1,9},{3,11}... | collective-permute-start | bytes 147464 | tf_op jit(solution)/shard_map/ppermute | solution.py:374
  53.1 6.8 %collective-permute-start.11 = (bf16[8,3072]{1,0:T(8,128)(2,1)S(1)}, bf16[8,3072]{1,0:T(8,128)(2,1)S(1)}, u32[]{:S(2)}, u32[]{:S(2)}) collective-permute-start(bf16[8,3072]{1,0:T(8,128)(2,1)S(1)} %get-tuple-element.54), channel_id=1, source_target_pairs={{0,4},{2,6},{4,8},{6,10},{8,12},{10,14},{12,0},{14,2},{1,5},{3,7},... | collective-permute-start | bytes 147464 | tf_op jit(solution)/shard_map/ppermute | solution.py:374
  54.9 5.2 %collective-permute-start.9 = (bf16[8,3072]{1,0:T(8,128)(2,1)S(1)}, bf16[8,3072]{1,0:T(8,128)(2,1)S(1)}, u32[]{:S(2)}, u32[]{:S(2)}) collective-permute-start(bf16[8,3072]{1,0:T(8,128)(2,1)S(1)} %get-tuple-element.53), channel_id=1, source_target_pairs={{0,12},{2,14},{4,0},{6,2},{8,4},{10,6},{12,8},{14,10},{1,13},{3,15... | collective-permute-start | bytes 147464 | tf_op jit(solution)/shard_map/ppermute | solution.py:374

commit v6 on v5

--- a/solution.py
+++ b/solution.py
@@ -168,18 +168,23 @@
         gate_sum[...] = earlier[0][...] if last else jnp.zeros_like(gate_sum)
         up_sum[...] = earlier[1][...] if last else jnp.zeros_like(up_sum)
 
-    def right(step):
-        return x[pl.ds(pl.multiple_of(step * kb, LANES), kb)]
+    pass_width = kb if last or kb % 256 else 256
+
+    def add(total, block, step):
+        for first in range(0, kb, pass_width):
+            right = x[pl.ds(pl.multiple_of(step * kb + first, LANES), pass_width)]
+            left = block[:, first : first + pass_width]
+            total[...] += jnp.dot(left, right, preferred_element_type=F32)
 
     def from_held(step):
-        gate_sum[...] += jnp.dot(gate_held[step], right(step), preferred_element_type=F32)
-        up_sum[...] += jnp.dot(up_held[step], right(step), preferred_element_type=F32)
+        add(gate_sum, gate_held.at[step], step)
+        add(up_sum, up_held.at[step], step)
 
     def from_ring(step, slot, waits):
         waits[0].wait()
-        gate_sum[...] += jnp.dot(gate_ring[slot], right(step), preferred_element_type=F32)
+        add(gate_sum, gate_ring.at[slot], step)
         waits[1].wait()
-        up_sum[...] += jnp.dot(up_ring[slot], right(step), preferred_element_type=F32)
+        add(up_sum, up_ring.at[slot], step)
 
     stream(held, len(parts) * per, fetch, ahead, begin, from_held, from_ring)
     if last:
@@ -260,7 +265,7 @@
     )
 
     def along(k):
-        return [(s, ((s // PAIR + k) % places) * PAIR + s % PAIR) for s in range(n_expert)]
+        return [(s, (s // PAIR ^ k) * PAIR + s % PAIR) for s in range(n_expert)]
 
     def across(k):
         return [(s, (s + k) % n_blk) for s in range(n_blk)]
@@ -277,7 +282,7 @@
     kb = largest_step(width, (512, 384, 256, 128))
     per = width // kb
     steps = per * (n_blk - 1)
-    first_held, second_held, third_held = min(2, per), min(2, steps), min(3, steps)
+    first_held, second_held, third_held = min(2, per), min(1, steps), min(3, steps)
 
     def blocks(count):
         return pltpu.VMEM((count, hid, kb), BF16)
@@ -371,7 +376,7 @@
     mixed = summed[:rows]
     for k in range(1, places):
         piece = summed[k * rows : (k + 1) * rows].astype(BF16)
-        mixed = mixed + lax.ppermute(piece, "expert", along(-k)).astype(F32)
+        mixed = mixed + lax.ppermute(piece, "expert", along(k)).astype(F32)
     return mixed.astype(BF16)
 
 

time: 60.9 us -> 67 us (1.10)
  Pallas kernels: 39.8 us -> 45.6 us
  waiting for transfers between devices: 4.61 us -> 7.01 us
  starting transfers between devices: 15.2 us -> 13.2 us
    pallas_call x7, Pallas kernels: 39.8 us -> 45.6 us  [call(): pl.pallas_call(kernel, out_shape=outs, in_specs=[pl.BlockSpec(memory_spac...]
    ppermute x3, waiting for transfers between devices: 0.01 us -> 1.59 us  [body(): lax.ppermute(packed, 'expert', along(k))]
    ppermute x3, starting transfers between devices: 7.01 us -> 5.68 us  [body(): lax.ppermute(packed, 'expert', along(k))]
    ppermute x3, waiting for transfers between devices: 3.16 us -> 3.97 us  [body(): mixed = mixed + lax.ppermute(piece, 'expert', along(k)).astype(F32)]
  transfers between devices with their start and end apart: 12 -> 12, of which waited for: 3 -> 5; matrix products, arithmetic and copies ran while one was open for 0% -> 0% of each run, Pallas kernels for 37% -> 37%
where the time goes in v6:
time: 67 us; the launch traced here: 66.8 us
  Pallas kernels  45.6 us (68%)
  starting transfers between devices  13.2 us (20%)
  waiting for transfers between devices  7.01 us (10%)
  other arithmetic  0.77 us (1%)
    pallas_call x7, Pallas kernels, call(): pl.pallas_call(kernel, out_shape=outs, in_specs=[pl.BlockSpec(memory_spac...  45.6 us
    ppermute x3, starting transfers between devices, body(): lax.ppermute(packed, 'expert', along(k))  5.68 us
    ppermute x3, waiting for transfers between devices, body(): mixed = mixed + lax.ppermute(piece, 'expert', along(k)).astype(F32)  3.97 us
    ppermute x3, starting transfers between devices, body(): mixed = mixed + lax.ppermute(piece, 'expert', along(k)).astype(F32)  3.55 us
    ppermute x3, waiting for transfers between devices, body(): lax.ppermute(packed, 'expert', along(k))  1.59 us
    ppermute x1, starting transfers between devices, body(): sent.append(lax.ppermute(bare, 'blk', across(-j)))  1.56 us
    ppermute x1, starting transfers between devices, body(): lax.ppermute(away[j - 1], 'blk', across(j))[:, :width]  1.55 us
    ppermute x1, waiting for transfers between devices, body(): summed = kept + lax.ppermute(given, 'expert', swap).astype(F32)  1.43 us
  transfers between devices with their start and end apart: 12, of which 5 were waited for; matrix products, arithmetic and copies ran while one was open for 0% of the time, Pallas kernels for 37%

profile of v6, /device:TPU:0, one launch (start us, length us, event | category | flops | bytes accessed | tf_op | source)
XLA Modules:
  0.0 66.8 jit_solution(15697985219931605799)
XLA Ops:
  0.0 0.9 %shard_map.64.after = bf16[8,3200]{1,0:T(8,128)(2,1)S(1)} custom-call(bf16[8,3072]{1,0:T(8,128)(2,1)} %tokens.1, s32[4,8]{1,0:T(4,128)} %bitcast.12, f32[4,8]{1,0:T(4,128)} %bitcast.13), custom_call_target="tpu_custom_call" | custom-call | flops 1024 | bytes 98304 | tf_op jit(solution)/shard_map/pallas_call | solution.py:27
  0.9 3.1 %collective-permute-start = (bf16[8,3200]{1,0:T(8,128)(2,1)S(1)}, bf16[8,3200]{1,0:T(8,128)(2,1)S(1)}, u32[]{:S(2)}, u32[]{:S(2)}) collective-permute-start(bf16[8,3200]{1,0:T(8,128)(2,1)S(1)} %shard_map.64.after), channel_id=1, source_target_pairs={{0,4},{2,6},{4,0},{6,2},{8,12},{10,14},{12,8},{14,10},{1,5},{3,7},... | collective-permute-start | bytes 153608 | tf_op jit(solution)/shard_map/ppermute | solution.py:300
  4.0 2.6 %collective-permute-start.1 = (bf16[8,3200]{1,0:T(8,128)(2,1)S(1)}, bf16[8,3200]{1,0:T(8,128)(2,1)S(1)}, u32[]{:S(2)}, u32[]{:S(2)}) collective-permute-start(bf16[8,3200]{1,0:T(8,128)(2,1)S(1)} %shard_map.64.after), channel_id=1, source_target_pairs={{0,8},{2,10},{4,12},{6,14},{8,0},{10,2},{12,4},{14,6},{1,9},{3,11}... | collective-permute-start | bytes 153608 | tf_op jit(solution)/shard_map/ppermute | solution.py:300
  6.5 0.0 collective-permute-start.2
  6.5 4.3 %shard_map.65 = (bf16[2,2688,512]{2,1,0:T(8,128)(2,1)S(1)}, bf16[2,2688,512]{2,1,0:T(8,128)(2,1)S(1)}) custom-call(bf16[8,3200]{1,0:T(8,128)(2,1)S(1)} %shard_map.64.after, bf16[1,2688,6144]{2,1,0:T(8,128)(2,1)} %refs_6_.1, bf16[1,2688,6144]{2,1,0:T(8,128)(2,1)} %refs_7_.1), custom_call_target="tpu_custom_call" | custom-call | bytes 11010048 | tf_op jit(solution)/shard_map/pallas_call | solution.py:27
  10.8 0.0 collective-permute-done
  10.9 0.0 collective-permute-done.1
  10.9 1.6 %collective-permute-done.2 = bf16[8,3200]{1,0:T(8,128)(2,1)S(1)} collective-permute-done((bf16[8,3200]{1,0:T(8,128)(2,1)S(1)}, bf16[8,3200]{1,0:T(8,128)(2,1)S(1)}, u32[]{:S(2)}, u32[]{:S(2)}) %collective-permute-start.2) | collective-permute-done | bytes 51232 | tf_op jit(solution)/shard_map/ppermute | solution.py:300
  12.5 0.1 collective-permute-start.5
  12.6 1.6 %collective-permute-start.3 = (bf16[32,3072]{1,0:T(8,128)(2,1)S(1)}, bf16[32,3072]{1,0:T(8,128)(2,1)S(1)}, u32[]{:S(2)}, u32[]{:S(2)}) collective-permute-start(bf16[32,3072]{1,0:T(8,128)(2,1)S(1)} %slice.27), channel_id=1, source_target_pairs={{0,1},{1,0},{2,3},{3,2},{4,5},{5,4},{6,7},{7,6},{8,9},{9,8},{10,11... | collective-permute-start | bytes 589832 | tf_op jit(solution)/shard_map/ppermute | solution.py:307
  14.2 0.4 collective-permute-start.4
  14.5 0.0 collective-permute-done.5.refs_1_.other
  14.5 13.9 %shard_map.66 = (f32[2688,64]{1,0:T(8,128)S(1)}, f32[2688,64]{1,0:T(8,128)S(1)}, bf16[1,2688,512]{2,1,0:T(8,128)(2,1)S(1)}, bf16[1,2688,512]{2,1,0:T(8,128)(2,1)S(1)}) custom-call(bf16[32,3200]{1,0:T(8,128)(2,1)S(1)} %constant_dynamic-update-slice_fusion.refs_0_.own, bf16[32,3200]{1,0:T(8,128)(2,1)S(1)} %collective-permute-done.5.refs_1_.other, ...), custom_call_target="tpu_custom_call" | custom-call | flops 2113929216 | bytes 33030144 | tf_op jit(solution)/shard_map/pallas_call | solution.py:27
  28.4 0.0 collective-permute-done.3.refs_0_
  28.4 0.0 collective-permute-done.4.refs_1_
  28.5 14.8 %shard_map.67 = (bf16[64,2688]{1,0:T(8,128)(2,1)S(1)}, bf16[3,2688,512]{2,1,0:T(8,128)(2,1)S(1)}) custom-call(bf16[32,3072]{1,0:T(8,128)(2,1)S(1)} %collective-permute-done.3.refs_0_, bf16[32,3072]{1,0:T(8,128)(2,1)S(1)} %collective-permute-done.4.refs_1_, f32[2688,64]{1,0:T(8,128)S(1)} %get-tuple-element.36.refs_2_, ...), custom_call_target="tpu_custom_call" | custom-call | flops 2113929216 | bytes 33030144 | tf_op jit(solution)/shard_map/pallas_call | solution.py:27
  43.2 5.3 %shard_map.68 = (f32[1,32,3072]{2,1,0:T(8,128)S(1)}, bf16[1,32,3072]{2,1,0:T(8,128)(2,1)S(1)}, bf16[2,2688,512]{2,1,0:T(8,128)(2,1)S(1)}) custom-call(bf16[64,2688]{1,0:T(8,128)(2,1)S(1)} %get-tuple-element.46.hidden, bf16[32,3200]{1,0:T(8,128)(2,1)S(1)} %constant_dynamic-update-slice_fusion.refs_0_.own, ...), custom_call_target="tpu_custom_call" | custom-call | flops 1056964608 | bytes 16515072 | tf_op jit(solution)/shard_map/pallas_call | solution.py:27
  48.6 0.4 collective-permute-start.6
  49.0 1.3 %shard_map.69 = (f32[1,32,1024]{2,1,0:T(8,128)S(1)}, bf16[1,32,1024]{2,1,0:T(8,128)(2,1)S(1)}) custom-call(bf16[64,2688]{1,0:T(8,128)(2,1)S(1)} %get-tuple-element.46.hidden, bf16[32,3200]{1,0:T(8,128)(2,1)S(1)} %constant_dynamic-update-slice_fusion.refs_0_.own, bf16[32,3200]{1,0:T(8,128)(2,1)S(1)} %collective-permute-done.5.refs_1_.other, ...), custom_call_target="tpu_custom_call" | custom-call | flops 352321536 | bytes 5505024 | tf_op jit(solution)/shard_map/pallas_call | solution.py:27
  50.4 1.6 %collective-permute-start.8 = (bf16[32,3200]{1,0:T(8,128)(2,1)S(1)}, bf16[32,3200]{1,0:T(8,128)(2,1)S(1)}, u32[]{:S(2)}, u32[]{:S(2)}) collective-permute-start(bf16[32,3200]{1,0:T(8,128)(2,1)S(1)} %pad_bitcast_fusion), channel_id=1, source_target_pairs={{0,1},{1,0},{2,3},{3,2},{4,5},{5,4},{6,7},{7,6},{8,9},{9,8},{10,11... | collective-permute-start | bytes 614408 | tf_op jit(solution)/shard_map/ppermute | solution.py:370
  51.9 5.1 %shard_map.70 = (f32[1,32,2048]{2,1,0:T(8,128)S(1)}, bf16[1,32,2048]{2,1,0:T(8,128)(2,1)S(1)}) custom-call(bf16[64,2688]{1,0:T(8,128)(2,1)S(1)} %get-tuple-element.46.hidden, bf16[32,3200]{1,0:T(8,128)(2,1)S(1)} %constant_dynamic-update-slice_fusion.refs_0_.own, bf16[32,3200]{1,0:T(8,128)(2,1)S(1)} %collective-permute-done.5.refs_1_.other, ...), custom_call_target="tpu_custom_call" | custom-call | flops 704643072 | bytes 11010048 | tf_op jit(solution)/shard_map/pallas_call | solution.py:27
  57.1 0.1 collective-permute-start.7
  57.1 1.4 %collective-permute-done.7 = bf16[32,3072]{1,0:T(8,128)(2,1)S(1)} collective-permute-done((bf16[32,3072]{1,0:T(8,128)(2,1)S(1)}, bf16[32,3072]{1,0:T(8,128)(2,1)S(1)}, u32[]{:S(2)}, u32[]{:S(2)}) %collective-permute-start.7) | collective-permute-done | bytes 196640 | tf_op jit(solution)/shard_map/ppermute | solution.py:373
  58.6 0.0 collective-permute-done.8
  58.6 0.1 fusion.4
  58.7 0.6 collective-permute-start.10
  59.2 1.8 %collective-permute-start.11 = (bf16[8,3072]{1,0:T(8,128)(2,1)S(1)}, bf16[8,3072]{1,0:T(8,128)(2,1)S(1)}, u32[]{:S(2)}, u32[]{:S(2)}) collective-permute-start(bf16[8,3072]{1,0:T(8,128)(2,1)S(1)} %get-tuple-element.54), channel_id=1, source_target_pairs={{0,12},{2,14},{4,8},{6,10},{8,4},{10,6},{12,0},{14,2},{1,13},{3,15... | collective-permute-start | bytes 147464 | tf_op jit(solution)/shard_map/ppermute | solution.py:379
  61.1 1.2 %collective-permute-start.9 = (bf16[8,3072]{1,0:T(8,128)(2,1)S(1)}, bf16[8,3072]{1,0:T(8,128)(2,1)S(1)}, u32[]{:S(2)}, u32[]{:S(2)}) collective-permute-start(bf16[8,3072]{1,0:T(8,128)(2,1)S(1)} %get-tuple-element.53), channel_id=1, source_target_pairs={{0,4},{2,6},{4,0},{6,2},{8,12},{10,14},{12,8},{14,10},{1,5},{3,7},... | collective-permute-start | bytes 147464 | tf_op jit(solution)/shard_map/ppermute | solution.py:379
  62.2 2.7 %collective-permute-done.10 = bf16[8,3072]{1,0:T(8,128)(2,1)S(1)} collective-permute-done((bf16[8,3072]{1,0:T(8,128)(2,1)S(1)}, bf16[8,3072]{1,0:T(8,128)(2,1)S(1)}, u32[]{:S(2)}, u32[]{:S(2)}) %collective-permute-start.10) | collective-permute-done | bytes 49184 | tf_op jit(solution)/shard_map/ppermute | solution.py:379
  65.0 0.7 %collective-permute-done.11 = bf16[8,3072]{1,0:T(8,128)(2,1)S(1)} collective-permute-done((bf16[8,3072]{1,0:T(8,128)(2,1)S(1)}, bf16[8,3072]{1,0:T(8,128)(2,1)S(1)}, u32[]{:S(2)}, u32[]{:S(2)}) %collective-permute-start.11) | collective-permute-done | bytes 49184 | tf_op jit(solution)/shard_map/ppermute | solution.py:379
  65.6 0.6 collective-permute-done.9
  66.2 0.6 fusion.3
  (10 shorter events, 0.1 us)
Async XLA Ops:
  0.9 10.0 %collective-permute-start = (bf16[8,3200]{1,0:T(8,128)(2,1)S(1)}, bf16[8,3200]{1,0:T(8,128)(2,1)S(1)}, u32[]{:S(2)}, u32[]{:S(2)}) collective-permute-start(bf16[8,3200]{1,0:T(8,128)(2,1)S(1)} %shard_map.64.after), channel_id=1, source_target_pairs={{0,4},{2,6},{4,0},{6,2},{8,12},{10,14},{12,8},{14,10},{1,5},{3,7},... | collective-permute-start | bytes 153608 | tf_op jit(solution)/shard_map/ppermute | solution.py:300
  4.0 6.9 %collective-permute-start.1 = (bf16[8,3200]{1,0:T(8,128)(2,1)S(1)}, bf16[8,3200]{1,0:T(8,128)(2,1)S(1)}, u32[]{:S(2)}, u32[]{:S(2)}) collective-permute-start(bf16[8,3200]{1,0:T(8,128)(2,1)S(1)} %shard_map.64.after), channel_id=1, source_target_pairs={{0,8},{2,10},{4,12},{6,14},{8,0},{10,2},{12,4},{14,6},{1,9},{3,11}... | collective-permute-start | bytes 153608 | tf_op jit(solution)/shard_map/ppermute | solution.py:300
  6.5 5.9 %collective-permute-start.2 = (bf16[8,3200]{1,0:T(8,128)(2,1)S(1)}, bf16[8,3200]{1,0:T(8,128)(2,1)S(1)}, u32[]{:S(2)}, u32[]{:S(2)}) collective-permute-start(bf16[8,3200]{1,0:T(8,128)(2,1)S(1)} %shard_map.64.after), channel_id=1, source_target_pairs={{0,12},{2,14},{4,8},{6,10},{8,4},{10,6},{12,0},{14,2},{1,13},{3,15... | collective-permute-start | bytes 153608 | tf_op jit(solution)/shard_map/ppermute | solution.py:300
  12.5 2.0 %collective-permute-start.5 = (bf16[32,3200]{1,0:T(8,128)(2,1)S(1)}, bf16[32,3200]{1,0:T(8,128)(2,1)S(1)}, u32[]{:S(2)}, u32[]{:S(2)}) collective-permute-start(bf16[32,3200]{1,0:T(8,128)(2,1)S(1)} %constant_dynamic-update-slice_fusion.refs_0_.own), channel_id=1, source_target_pairs={{0,2},{2,0},{4,6},{6,4},{8,10},{10,8},{12,14},{14,12},{1,3},{3,1},... | collective-permute-start | bytes 614408 | tf_op jit(solution)/shard_map/ppermute | solution.py:303
  12.6 15.8 %collective-permute-start.3 = (bf16[32,3072]{1,0:T(8,128)(2,1)S(1)}, bf16[32,3072]{1,0:T(8,128)(2,1)S(1)}, u32[]{:S(2)}, u32[]{:S(2)}) collective-permute-start(bf16[32,3072]{1,0:T(8,128)(2,1)S(1)} %slice.27), channel_id=1, source_target_pairs={{0,1},{1,0},{2,3},{3,2},{4,5},{5,4},{6,7},{7,6},{8,9},{9,8},{10,11... | collective-permute-start | bytes 589832 | tf_op jit(solution)/shard_map/ppermute | solution.py:307
  14.2 14.3 %collective-permute-start.4 = (bf16[32,3072]{1,0:T(8,128)(2,1)S(1)}, bf16[32,3072]{1,0:T(8,128)(2,1)S(1)}, u32[]{:S(2)}, u32[]{:S(2)}) collective-permute-start(bf16[32,3072]{1,0:T(8,128)(2,1)S(1)} %slice.27), channel_id=1, source_target_pairs={{0,3},{1,2},{2,1},{3,0},{4,7},{5,6},{6,5},{7,4},{8,11},{9,10},{10,... | collective-permute-start | bytes 589832 | tf_op jit(solution)/shard_map/ppermute | solution.py:308
  48.6 1.7 %collective-permute-start.6 = (bf16[1,32,3072]{2,1,0:T(8,128)(2,1)S(1)}, bf16[1,32,3072]{2,1,0:T(8,128)(2,1)S(1)}, u32[]{:S(2)}, u32[]{:S(2)}) collective-permute-start(bf16[1,32,3072]{2,1,0:T(8,128)(2,1)S(1)} %get-tuple-element.45), channel_id=1, source_target_pairs={{0,2},{2,0},{4,6},{6,4},{8,10},{10,8},{12,14},{14,12},{1,3},{3,1},... | collective-permute-start | bytes 589832 | tf_op jit(solution)/shard_map/ppermute | solution.py:365
  50.4 8.2 %collective-permute-start.8 = (bf16[32,3200]{1,0:T(8,128)(2,1)S(1)}, bf16[32,3200]{1,0:T(8,128)(2,1)S(1)}, u32[]{:S(2)}, u32[]{:S(2)}) collective-permute-start(bf16[32,3200]{1,0:T(8,128)(2,1)S(1)} %pad_bitcast_fusion), channel_id=1, source_target_pairs={{0,1},{1,0},{2,3},{3,2},{4,5},{5,4},{6,7},{7,6},{8,9},{9,8},{10,11... | collective-permute-start | bytes 614408 | tf_op jit(solution)/shard_map/ppermute | solution.py:370
  57.1 1.5 %collective-permute-start.7 = (bf16[32,3072]{1,0:T(8,128)(2,1)S(1)}, bf16[32,3072]{1,0:T(8,128)(2,1)S(1)}, u32[]{:S(2)}, u32[]{:S(2)}) collective-permute-start(bf16[32,3072]{1,0:T(8,128)(2,1)S(1)} %pad_maximum_fusion), channel_id=1, source_target_pairs={{0,2},{2,0},{4,6},{6,4},{8,10},{10,8},{12,14},{14,12},{1,3},{3,1},... | collective-permute-start | bytes 589832 | tf_op jit(solution)/shard_map/ppermute | solution.py:373
  58.7 6.3 %collective-permute-start.10 = (bf16[8,3072]{1,0:T(8,128)(2,1)S(1)}, bf16[8,3072]{1,0:T(8,128)(2,1)S(1)}, u32[]{:S(2)}, u32[]{:S(2)}) collective-permute-start(bf16[8,3072]{1,0:T(8,128)(2,1)S(1)} %get-tuple-element.55), channel_id=1, source_target_pairs={{0,8},{2,10},{4,12},{6,14},{8,0},{10,2},{12,4},{14,6},{1,9},{3,11}... | collective-permute-start | bytes 147464 | tf_op jit(solution)/shard_map/ppermute | solution.py:379
  59.2 6.4 %collective-permute-start.11 = (bf16[8,3072]{1,0:T(8,128)(2,1)S(1)}, bf16[8,3072]{1,0:T(8,128)(2,1)S(1)}, u32[]{:S(2)}, u32[]{:S(2)}) collective-permute-start(bf16[8,3072]{1,0:T(8,128)(2,1)S(1)} %get-tuple-element.54), channel_id=1, source_target_pairs={{0,12},{2,14},{4,8},{6,10},{8,4},{10,6},{12,0},{14,2},{1,13},{3,15... | collective-permute-start | bytes 147464 | tf_op jit(solution)/shard_map/ppermute | solution.py:379
  61.1 5.1 %collective-permute-start.9 = (bf16[8,3072]{1,0:T(8,128)(2,1)S(1)}, bf16[8,3072]{1,0:T(8,128)(2,1)S(1)}, u32[]{:S(2)}, u32[]{:S(2)}) collective-permute-start(bf16[8,3072]{1,0:T(8,128)(2,1)S(1)} %get-tuple-element.53), channel_id=1, source_target_pairs={{0,4},{2,6},{4,0},{6,2},{8,12},{10,14},{12,8},{14,10},{1,5},{3,7},... | collective-permute-start | bytes 147464 | tf_op jit(solution)/shard_map/ppermute | solution.py:379

commit v7 on v5

--- a/solution.py
+++ b/solution.py
@@ -53,15 +53,38 @@
 
 def stream(held, count, fetch, ahead, begin, from_held, from_ring):
     rest = count - held
-    for at in range(min(SLOTS, rest)):
+    lead = held if held and rest <= SLOTS else SLOTS - 1
+    first_ahead = min(max(count - lead, 0), count - 1)
+    second_ahead = min(first_ahead + 1, count - 1)
+    several = -(-len(ahead) // 2)
+    for at in range(min(lead - held + 1, rest)):
         for copy in fetch(held + at, at):
             copy.start()
-    if rest == 0:
-        for copy in ahead:
-            copy.start()
     begin()
 
+    def issue(step):
+        at = step + lead - held
+        if rest:
+
+            @pl.when((step > 0) & (at >= 0) & (at < rest))
+            def _():
+                for copy in fetch(held + at, lax.rem(at, SLOTS)):
+                    copy.start()
+
+        if ahead:
+
+            @pl.when(step == first_ahead)
+            def _():
+                for copy in ahead[:several]:
+                    copy.start()
+
+            @pl.when(step == second_ahead)
+            def _():
+                for copy in ahead[several:]:
+                    copy.start()
+
     def first(step, carry):
+        issue(step)
         from_held(step)
         return carry
 
@@ -69,18 +92,7 @@
         lax.fori_loop(0, held, first, 0)
 
     def then(at, carry):
-        later = at + SLOTS - 1
-
-        @pl.when((at > 0) & (later < rest))
-        def _():
-            for copy in fetch(held + later, lax.rem(later, SLOTS)):
-                copy.start()
-
-        @pl.when(at == max(rest - SLOTS, 0))
-        def _():
-            for copy in ahead:
-                copy.start()
-
+        issue(held + at)
         slot = lax.rem(at, SLOTS)
         from_ring(held + at, slot, fetch(held + at, slot))
         return carry

time: 60.9 us -> 63.2 us (1.038)
  Pallas kernels: 39.8 us -> 42.2 us
    pallas_call x7, Pallas kernels: 39.8 us -> 42.2 us  [call(): pl.pallas_call(kernel, out_shape=outs, in_specs=[pl.BlockSpec(memory_spac...]
where the time goes in v7:
time: 63.2 us; the launch traced here: 63.1 us
  Pallas kernels  42.2 us (67%)
  starting transfers between devices  15.2 us (24%)
  waiting for transfers between devices  4.61 us (7%)
  other arithmetic  0.78 us (1%)
    pallas_call x7, Pallas kernels, call(): pl.pallas_call(kernel, out_shape=outs, in_specs=[pl.BlockSpec(memory_spac...  42.2 us
    ppermute x3, starting transfers between devices, body(): lax.ppermute(packed, 'expert', along(k))  7.01 us
    ppermute x3, starting transfers between devices, body(): mixed = mixed + lax.ppermute(piece, 'expert', along(-k)).astype(F32)  4.22 us
    ppermute x3, waiting for transfers between devices, body(): mixed = mixed + lax.ppermute(piece, 'expert', along(-k)).astype(F32)  3.16 us
    ppermute x1, starting transfers between devices, body(): lax.ppermute(away[j - 1], 'blk', across(j))[:, :width]  1.56 us
    ppermute x1, starting transfers between devices, body(): sent.append(lax.ppermute(bare, 'blk', across(-j)))  1.56 us
    ppermute x1, waiting for transfers between devices, body(): summed = kept + lax.ppermute(given, 'expert', swap).astype(F32)  1.43 us
  transfers between devices with their start and end apart: 12, of which 3 were waited for; matrix products, arithmetic and copies ran while one was open for 0% of the time, Pallas kernels for 37%

profile of v7, /device:TPU:0, one launch (start us, length us, event | category | flops | bytes accessed | tf_op | source)
XLA Modules:
  0.0 63.1 jit_solution(3111949866740672106)
XLA Ops:
  0.0 0.9 %shard_map.64.after = bf16[8,3200]{1,0:T(8,128)(2,1)S(1)} custom-call(bf16[8,3072]{1,0:T(8,128)(2,1)} %tokens.1, s32[4,8]{1,0:T(4,128)} %bitcast.12, f32[4,8]{1,0:T(4,128)} %bitcast.13), custom_call_target="tpu_custom_call" | custom-call | flops 1024 | bytes 98304 | tf_op jit(solution)/shard_map/pallas_call | solution.py:27
  0.9 3.1 %collective-permute-start = (bf16[8,3200]{1,0:T(8,128)(2,1)S(1)}, bf16[8,3200]{1,0:T(8,128)(2,1)S(1)}, u32[]{:S(2)}, u32[]{:S(2)}) collective-permute-start(bf16[8,3200]{1,0:T(8,128)(2,1)S(1)} %shard_map.64.after), channel_id=1, source_target_pairs={{0,4},{2,6},{4,8},{6,10},{8,12},{10,14},{12,0},{14,2},{1,5},{3,7},... | collective-permute-start | bytes 153608 | tf_op jit(solution)/shard_map/ppermute | solution.py:307
  3.9 2.6 %collective-permute-start.1 = (bf16[8,3200]{1,0:T(8,128)(2,1)S(1)}, bf16[8,3200]{1,0:T(8,128)(2,1)S(1)}, u32[]{:S(2)}, u32[]{:S(2)}) collective-permute-start(bf16[8,3200]{1,0:T(8,128)(2,1)S(1)} %shard_map.64.after), channel_id=1, source_target_pairs={{0,8},{2,10},{4,12},{6,14},{8,0},{10,2},{12,4},{14,6},{1,9},{3,11}... | collective-permute-start | bytes 153608 | tf_op jit(solution)/shard_map/ppermute | solution.py:307
  6.5 1.3 %collective-permute-start.2 = (bf16[8,3200]{1,0:T(8,128)(2,1)S(1)}, bf16[8,3200]{1,0:T(8,128)(2,1)S(1)}, u32[]{:S(2)}, u32[]{:S(2)}) collective-permute-start(bf16[8,3200]{1,0:T(8,128)(2,1)S(1)} %shard_map.64.after), channel_id=1, source_target_pairs={{0,12},{2,14},{4,0},{6,2},{8,4},{10,6},{12,8},{14,10},{1,13},{3,15... | collective-permute-start | bytes 153608 | tf_op jit(solution)/shard_map/ppermute | solution.py:307
  7.9 4.3 %shard_map.65 = (bf16[2,2688,512]{2,1,0:T(8,128)(2,1)S(1)}, bf16[2,2688,512]{2,1,0:T(8,128)(2,1)S(1)}) custom-call(bf16[8,3200]{1,0:T(8,128)(2,1)S(1)} %shard_map.64.after, bf16[1,2688,6144]{2,1,0:T(8,128)(2,1)} %refs_6_.1, bf16[1,2688,6144]{2,1,0:T(8,128)(2,1)} %refs_7_.1), custom_call_target="tpu_custom_call" | custom-call | bytes 11010048 | tf_op jit(solution)/shard_map/pallas_call | solution.py:27
  12.2 0.0 collective-permute-done
  12.2 0.0 collective-permute-done.1
  12.2 0.0 collective-permute-done.2
  12.3 0.1 collective-permute-start.5
  12.4 1.6 %collective-permute-start.3 = (bf16[32,3072]{1,0:T(8,128)(2,1)S(1)}, bf16[32,3072]{1,0:T(8,128)(2,1)S(1)}, u32[]{:S(2)}, u32[]{:S(2)}) collective-permute-start(bf16[32,3072]{1,0:T(8,128)(2,1)S(1)} %slice.27), channel_id=1, source_target_pairs={{0,1},{1,0},{2,3},{3,2},{4,5},{5,4},{6,7},{7,6},{8,9},{9,8},{10,11... | collective-permute-start | bytes 589832 | tf_op jit(solution)/shard_map/ppermute | solution.py:314
  13.9 0.4 collective-permute-start.4
  14.3 0.0 collective-permute-done.5.refs_1_.other
  14.3 12.9 %shard_map.66 = (f32[2688,64]{1,0:T(8,128)S(1)}, f32[2688,64]{1,0:T(8,128)S(1)}, bf16[2,2688,512]{2,1,0:T(8,128)(2,1)S(1)}, bf16[2,2688,512]{2,1,0:T(8,128)(2,1)S(1)}) custom-call(bf16[32,3200]{1,0:T(8,128)(2,1)S(1)} %constant_dynamic-update-slice_fusion.refs_0_.own, bf16[32,3200]{1,0:T(8,128)(2,1)S(1)} %collective-permute-done.5.refs_1_.other, ...), custom_call_target="tpu_custom_call" | custom-call | flops 2113929216 | bytes 33030144 | tf_op jit(solution)/shard_map/pallas_call | solution.py:27
  27.2 0.0 collective-permute-done.3.refs_0_
  27.2 12.1 %shard_map.67 = (bf16[64,2688]{1,0:T(8,128)(2,1)S(1)}, bf16[3,2688,512]{2,1,0:T(8,128)(2,1)S(1)}) custom-call(bf16[32,3072]{1,0:T(8,128)(2,1)S(1)} %collective-permute-done.3.refs_0_, bf16[32,3072]{1,0:T(8,128)(2,1)S(1)} %collective-permute-done.4.refs_1_, f32[2688,64]{1,0:T(8,128)S(1)} %get-tuple-element.36.refs_2_, ...), custom_call_target="tpu_custom_call" | custom-call | flops 2113929216 | bytes 33030144 | tf_op jit(solution)/shard_map/pallas_call | solution.py:27
  39.3 5.6 %shard_map.68 = (f32[1,32,3072]{2,1,0:T(8,128)S(1)}, bf16[1,32,3072]{2,1,0:T(8,128)(2,1)S(1)}, bf16[2,2688,512]{2,1,0:T(8,128)(2,1)S(1)}) custom-call(bf16[64,2688]{1,0:T(8,128)(2,1)S(1)} %get-tuple-element.46.hidden, bf16[32,3200]{1,0:T(8,128)(2,1)S(1)} %constant_dynamic-update-slice_fusion.refs_0_.own, ...), custom_call_target="tpu_custom_call" | custom-call | flops 1056964608 | bytes 16515072 | tf_op jit(solution)/shard_map/pallas_call | solution.py:27
  44.9 0.4 collective-permute-start.6
  45.3 1.3 %shard_map.69 = (f32[1,32,1024]{2,1,0:T(8,128)S(1)}, bf16[1,32,1024]{2,1,0:T(8,128)(2,1)S(1)}) custom-call(bf16[64,2688]{1,0:T(8,128)(2,1)S(1)} %get-tuple-element.46.hidden, bf16[32,3200]{1,0:T(8,128)(2,1)S(1)} %constant_dynamic-update-slice_fusion.refs_0_.own, bf16[32,3200]{1,0:T(8,128)(2,1)S(1)} %collective-permute-done.5.refs_1_.other, ...), custom_call_target="tpu_custom_call" | custom-call | flops 352321536 | bytes 5505024 | tf_op jit(solution)/shard_map/pallas_call | solution.py:27
  46.6 0.1 add_convert_fusion
  46.7 1.6 %collective-permute-start.8 = (bf16[32,3200]{1,0:T(8,128)(2,1)S(1)}, bf16[32,3200]{1,0:T(8,128)(2,1)S(1)}, u32[]{:S(2)}, u32[]{:S(2)}) collective-permute-start(bf16[32,3200]{1,0:T(8,128)(2,1)S(1)} %pad_bitcast_fusion), channel_id=1, source_target_pairs={{0,1},{1,0},{2,3},{3,2},{4,5},{5,4},{6,7},{7,6},{8,9},{9,8},{10,11... | collective-permute-start | bytes 614408 | tf_op jit(solution)/shard_map/ppermute | solution.py:377
  48.3 5.1 %shard_map.70 = (f32[1,32,2048]{2,1,0:T(8,128)S(1)}, bf16[1,32,2048]{2,1,0:T(8,128)(2,1)S(1)}) custom-call(bf16[64,2688]{1,0:T(8,128)(2,1)S(1)} %get-tuple-element.46.hidden, bf16[32,3200]{1,0:T(8,128)(2,1)S(1)} %constant_dynamic-update-slice_fusion.refs_0_.own, bf16[32,3200]{1,0:T(8,128)(2,1)S(1)} %collective-permute-done.5.refs_1_.other, ...), custom_call_target="tpu_custom_call" | custom-call | flops 704643072 | bytes 11010048 | tf_op jit(solution)/shard_map/pallas_call | solution.py:27
  53.4 0.1 collective-permute-start.7
  53.5 1.4 %collective-permute-done.7 = bf16[32,3072]{1,0:T(8,128)(2,1)S(1)} collective-permute-done((bf16[32,3072]{1,0:T(8,128)(2,1)S(1)}, bf16[32,3072]{1,0:T(8,128)(2,1)S(1)}, u32[]{:S(2)}, u32[]{:S(2)}) %collective-permute-start.7) | collective-permute-done | bytes 196640 | tf_op jit(solution)/shard_map/ppermute | solution.py:380
  54.9 0.0 collective-permute-done.8
  54.9 0.1 fusion.4
  55.0 0.4 collective-permute-start.10
  55.4 1.8 %collective-permute-start.11 = (bf16[8,3072]{1,0:T(8,128)(2,1)S(1)}, bf16[8,3072]{1,0:T(8,128)(2,1)S(1)}, u32[]{:S(2)}, u32[]{:S(2)}) collective-permute-start(bf16[8,3072]{1,0:T(8,128)(2,1)S(1)} %get-tuple-element.54), channel_id=1, source_target_pairs={{0,4},{2,6},{4,8},{6,10},{8,12},{10,14},{12,0},{14,2},{1,5},{3,7},... | collective-permute-start | bytes 147464 | tf_op jit(solution)/shard_map/ppermute | solution.py:386
  57.2 2.0 %collective-permute-start.9 = (bf16[8,3072]{1,0:T(8,128)(2,1)S(1)}, bf16[8,3072]{1,0:T(8,128)(2,1)S(1)}, u32[]{:S(2)}, u32[]{:S(2)}) collective-permute-start(bf16[8,3072]{1,0:T(8,128)(2,1)S(1)} %get-tuple-element.53), channel_id=1, source_target_pairs={{0,12},{2,14},{4,0},{6,2},{8,4},{10,6},{12,8},{14,10},{1,13},{3,15... | collective-permute-start | bytes 147464 | tf_op jit(solution)/shard_map/ppermute | solution.py:386
  59.3 2.9 %collective-permute-done.10 = bf16[8,3072]{1,0:T(8,128)(2,1)S(1)} collective-permute-done((bf16[8,3072]{1,0:T(8,128)(2,1)S(1)}, bf16[8,3072]{1,0:T(8,128)(2,1)S(1)}, u32[]{:S(2)}, u32[]{:S(2)}) %collective-permute-start.10) | collective-permute-done | bytes 49184 | tf_op jit(solution)/shard_map/ppermute | solution.py:386
  62.2 0.0 collective-permute-done.11
  62.2 0.2 collective-permute-done.9
  62.4 0.6 %fusion.3 = bf16[8,3072]{1,0:T(8,128)(2,1)} fusion(f32[32,3072]{1,0:T(8,128)S(1)} %get-tuple-element.52, bf16[8,3072]{1,0:T(8,128)(2,1)S(1)} %collective-permute-done.11, bf16[8,3072]{1,0:T(8,128)(2,1)S(1)} %collective-permute-done.10, bf16[8,3072]{1,0:T(8,128)(2,1)S(1)} %collective-permute-done.9), kind=kLoop, calls=%fused_computation.8 | loop fusion | flops 172032 | bytes 294912 | tf_op jit(solution)/shard_map/convert_element_type | solution.py:387
  (10 shorter events, 0.1 us)
Async XLA Ops:
  0.9 11.3 %collective-permute-start = (bf16[8,3200]{1,0:T(8,128)(2,1)S(1)}, bf16[8,3200]{1,0:T(8,128)(2,1)S(1)}, u32[]{:S(2)}, u32[]{:S(2)}) collective-permute-start(bf16[8,3200]{1,0:T(8,128)(2,1)S(1)} %shard_map.64.after), channel_id=1, source_target_pairs={{0,4},{2,6},{4,8},{6,10},{8,12},{10,14},{12,0},{14,2},{1,5},{3,7},... | collective-permute-start | bytes 153608 | tf_op jit(solution)/shard_map/ppermute | solution.py:307
  3.9 8.2 %collective-permute-start.1 = (bf16[8,3200]{1,0:T(8,128)(2,1)S(1)}, bf16[8,3200]{1,0:T(8,128)(2,1)S(1)}, u32[]{:S(2)}, u32[]{:S(2)}) collective-permute-start(bf16[8,3200]{1,0:T(8,128)(2,1)S(1)} %shard_map.64.after), channel_id=1, source_target_pairs={{0,8},{2,10},{4,12},{6,14},{8,0},{10,2},{12,4},{14,6},{1,9},{3,11}... | collective-permute-start | bytes 153608 | tf_op jit(solution)/shard_map/ppermute | solution.py:307
  6.5 5.7 %collective-permute-start.2 = (bf16[8,3200]{1,0:T(8,128)(2,1)S(1)}, bf16[8,3200]{1,0:T(8,128)(2,1)S(1)}, u32[]{:S(2)}, u32[]{:S(2)}) collective-permute-start(bf16[8,3200]{1,0:T(8,128)(2,1)S(1)} %shard_map.64.after), channel_id=1, source_target_pairs={{0,12},{2,14},{4,0},{6,2},{8,4},{10,6},{12,8},{14,10},{1,13},{3,15... | collective-permute-start | bytes 153608 | tf_op jit(solution)/shard_map/ppermute | solution.py:307
  12.3 2.0 %collective-permute-start.5 = (bf16[32,3200]{1,0:T(8,128)(2,1)S(1)}, bf16[32,3200]{1,0:T(8,128)(2,1)S(1)}, u32[]{:S(2)}, u32[]{:S(2)}) collective-permute-start(bf16[32,3200]{1,0:T(8,128)(2,1)S(1)} %constant_dynamic-update-slice_fusion.refs_0_.own), channel_id=1, source_target_pairs={{0,2},{2,0},{4,6},{6,4},{8,10},{10,8},{12,14},{14,12},{1,3},{3,1},... | collective-permute-start | bytes 614408 | tf_op jit(solution)/shard_map/ppermute | solution.py:310
  12.4 14.8 %collective-permute-start.3 = (bf16[32,3072]{1,0:T(8,128)(2,1)S(1)}, bf16[32,3072]{1,0:T(8,128)(2,1)S(1)}, u32[]{:S(2)}, u32[]{:S(2)}) collective-permute-start(bf16[32,3072]{1,0:T(8,128)(2,1)S(1)} %slice.27), channel_id=1, source_target_pairs={{0,1},{1,0},{2,3},{3,2},{4,5},{5,4},{6,7},{7,6},{8,9},{9,8},{10,11... | collective-permute-start | bytes 589832 | tf_op jit(solution)/shard_map/ppermute | solution.py:314
  13.9 13.3 %collective-permute-start.4 = (bf16[32,3072]{1,0:T(8,128)(2,1)S(1)}, bf16[32,3072]{1,0:T(8,128)(2,1)S(1)}, u32[]{:S(2)}, u32[]{:S(2)}) collective-permute-start(bf16[32,3072]{1,0:T(8,128)(2,1)S(1)} %slice.27), channel_id=1, source_target_pairs={{0,3},{1,2},{2,1},{3,0},{4,7},{5,6},{6,5},{7,4},{8,11},{9,10},{10,... | collective-permute-start | bytes 589832 | tf_op jit(solution)/shard_map/ppermute | solution.py:315
  44.9 1.7 %collective-permute-start.6 = (bf16[1,32,3072]{2,1,0:T(8,128)(2,1)S(1)}, bf16[1,32,3072]{2,1,0:T(8,128)(2,1)S(1)}, u32[]{:S(2)}, u32[]{:S(2)}) collective-permute-start(bf16[1,32,3072]{2,1,0:T(8,128)(2,1)S(1)} %get-tuple-element.45), channel_id=1, source_target_pairs={{0,2},{2,0},{4,6},{6,4},{8,10},{10,8},{12,14},{14,12},{1,3},{3,1},... | collective-permute-start | bytes 589832 | tf_op jit(solution)/shard_map/ppermute | solution.py:372
  46.7 8.2 %collective-permute-start.8 = (bf16[32,3200]{1,0:T(8,128)(2,1)S(1)}, bf16[32,3200]{1,0:T(8,128)(2,1)S(1)}, u32[]{:S(2)}, u32[]{:S(2)}) collective-permute-start(bf16[32,3200]{1,0:T(8,128)(2,1)S(1)} %pad_bitcast_fusion), channel_id=1, source_target_pairs={{0,1},{1,0},{2,3},{3,2},{4,5},{5,4},{6,7},{7,6},{8,9},{9,8},{10,11... | collective-permute-start | bytes 614408 | tf_op jit(solution)/shard_map/ppermute | solution.py:377
  53.4 1.5 %collective-permute-start.7 = (bf16[32,3072]{1,0:T(8,128)(2,1)S(1)}, bf16[32,3072]{1,0:T(8,128)(2,1)S(1)}, u32[]{:S(2)}, u32[]{:S(2)}) collective-permute-start(bf16[32,3072]{1,0:T(8,128)(2,1)S(1)} %pad_maximum_fusion), channel_id=1, source_target_pairs={{0,2},{2,0},{4,6},{6,4},{8,10},{10,8},{12,14},{14,12},{1,3},{3,1},... | collective-permute-start | bytes 589832 | tf_op jit(solution)/shard_map/ppermute | solution.py:380
  55.0 7.2 %collective-permute-start.10 = (bf16[8,3072]{1,0:T(8,128)(2,1)S(1)}, bf16[8,3072]{1,0:T(8,128)(2,1)S(1)}, u32[]{:S(2)}, u32[]{:S(2)}) collective-permute-start(bf16[8,3072]{1,0:T(8,128)(2,1)S(1)} %get-tuple-element.55), channel_id=1, source_target_pairs={{0,8},{2,10},{4,12},{6,14},{8,0},{10,2},{12,4},{14,6},{1,9},{3,11}... | collective-permute-start | bytes 147464 | tf_op jit(solution)/shard_map/ppermute | solution.py:386
  55.4 6.8 %collective-permute-start.11 = (bf16[8,3072]{1,0:T(8,128)(2,1)S(1)}, bf16[8,3072]{1,0:T(8,128)(2,1)S(1)}, u32[]{:S(2)}, u32[]{:S(2)}) collective-permute-start(bf16[8,3072]{1,0:T(8,128)(2,1)S(1)} %get-tuple-element.54), channel_id=1, source_target_pairs={{0,4},{2,6},{4,8},{6,10},{8,12},{10,14},{12,0},{14,2},{1,5},{3,7},... | collective-permute-start | bytes 147464 | tf_op jit(solution)/shard_map/ppermute | solution.py:386
  57.2 5.2 %collective-permute-start.9 = (bf16[8,3072]{1,0:T(8,128)(2,1)S(1)}, bf16[8,3072]{1,0:T(8,128)(2,1)S(1)}, u32[]{:S(2)}, u32[]{:S(2)}) collective-permute-start(bf16[8,3072]{1,0:T(8,128)(2,1)S(1)} %get-tuple-element.53), channel_id=1, source_target_pairs={{0,12},{2,14},{4,0},{6,2},{8,4},{10,6},{12,8},{14,10},{1,13},{3,15... | collective-permute-start | bytes 147464 | tf_op jit(solution)/shard_map/ppermute | solution.py:386

commit v8 on v5

--- a/solution.py
+++ b/solution.py
@@ -76,13 +76,20 @@
             for copy in fetch(held + later, lax.rem(later, SLOTS)):
                 copy.start()
 
-        @pl.when(at == max(rest - SLOTS, 0))
-        def _():
-            for copy in ahead:
-                copy.start()
+        def start_ahead():
+            @pl.when(at == 0)
+            def _():
+                for copy in ahead:
+                    copy.start()
 
         slot = lax.rem(at, SLOTS)
-        from_ring(held + at, slot, fetch(held + at, slot))
+        waits = fetch(held + at, slot)
+        if rest <= SLOTS:
+            start_ahead()
+        waits[0].wait()
+        if rest > SLOTS:
+            start_ahead()
+        from_ring(held + at, slot, waits[1:])
         return carry
 
     if rest:
@@ -176,9 +183,8 @@
         up_sum[...] += jnp.dot(up_held[step], right(step), preferred_element_type=F32)
 
     def from_ring(step, slot, waits):
+        gate_sum[...] += jnp.dot(gate_ring[slot], right(step), preferred_element_type=F32)
         waits[0].wait()
-        gate_sum[...] += jnp.dot(gate_ring[slot], right(step), preferred_element_type=F32)
-        waits[1].wait()
         up_sum[...] += jnp.dot(up_ring[slot], right(step), preferred_element_type=F32)
 
     stream(held, len(parts) * per, fetch, ahead, begin, from_held, from_ring)
@@ -218,7 +224,6 @@
         put(step, down_held[step])
 
     def from_ring(step, slot, waits):
-        waits[0].wait()
         put(step, ring[slot])
 
     ahead = []

time: 60.9 us -> 61.8 us (1.015)
  Pallas kernels: 39.8 us -> 40.7 us
    pallas_call x7, Pallas kernels: 39.8 us -> 40.7 us  [call(): pl.pallas_call(kernel, out_shape=outs, in_specs=[pl.BlockSpec(memory_spac...]
where the time goes in v8:
time: 61.8 us; the launch traced here: 61.6 us
  Pallas kernels  40.7 us (66%)
  starting transfers between devices  15.2 us (25%)
  waiting for transfers between devices  4.6 us (7%)
  other arithmetic  0.78 us (1%)
    pallas_call x7, Pallas kernels, call(): pl.pallas_call(kernel, out_shape=outs, in_specs=[pl.BlockSpec(memory_spac...  40.7 us
    ppermute x3, starting transfers between devices, body(): lax.ppermute(packed, 'expert', along(k))  7.01 us
    ppermute x3, starting transfers between devices, body(): mixed = mixed + lax.ppermute(piece, 'expert', along(-k)).astype(F32)  4.23 us
    ppermute x3, waiting for transfers between devices, body(): mixed = mixed + lax.ppermute(piece, 'expert', along(-k)).astype(F32)  3.15 us
    ppermute x1, starting transfers between devices, body(): sent.append(lax.ppermute(bare, 'blk', across(-j)))  1.56 us
    ppermute x1, starting transfers between devices, body(): lax.ppermute(away[j - 1], 'blk', across(j))[:, :width]  1.55 us
    ppermute x1, waiting for transfers between devices, body(): summed = kept + lax.ppermute(given, 'expert', swap).astype(F32)  1.43 us
  transfers between devices with their start and end apart: 12, of which 3 were waited for; matrix products, arithmetic and copies ran while one was open for 0% of the time, Pallas kernels for 37%

profile of v8, /device:TPU:0, one launch (start us, length us, event | category | flops | bytes accessed | tf_op | source)
XLA Modules:
  0.0 61.6 jit_solution(10684515845726729770)
XLA Ops:
  0.0 0.9 %shard_map.64.after = bf16[8,3200]{1,0:T(8,128)(2,1)S(1)} custom-call(bf16[8,3072]{1,0:T(8,128)(2,1)} %tokens.1, s32[4,8]{1,0:T(4,128)} %bitcast.12, f32[4,8]{1,0:T(4,128)} %bitcast.13), custom_call_target="tpu_custom_call" | custom-call | flops 1024 | bytes 98304 | tf_op jit(solution)/shard_map/pallas_call | solution.py:27
  0.9 3.1 %collective-permute-start = (bf16[8,3200]{1,0:T(8,128)(2,1)S(1)}, bf16[8,3200]{1,0:T(8,128)(2,1)S(1)}, u32[]{:S(2)}, u32[]{:S(2)}) collective-permute-start(bf16[8,3200]{1,0:T(8,128)(2,1)S(1)} %shard_map.64.after), channel_id=1, source_target_pairs={{0,4},{2,6},{4,8},{6,10},{8,12},{10,14},{12,0},{14,2},{1,5},{3,7},... | collective-permute-start | bytes 153608 | tf_op jit(solution)/shard_map/ppermute | solution.py:300
  3.9 2.6 %collective-permute-start.1 = (bf16[8,3200]{1,0:T(8,128)(2,1)S(1)}, bf16[8,3200]{1,0:T(8,128)(2,1)S(1)}, u32[]{:S(2)}, u32[]{:S(2)}) collective-permute-start(bf16[8,3200]{1,0:T(8,128)(2,1)S(1)} %shard_map.64.after), channel_id=1, source_target_pairs={{0,8},{2,10},{4,12},{6,14},{8,0},{10,2},{12,4},{14,6},{1,9},{3,11}... | collective-permute-start | bytes 153608 | tf_op jit(solution)/shard_map/ppermute | solution.py:300
  6.5 1.3 %collective-permute-start.2 = (bf16[8,3200]{1,0:T(8,128)(2,1)S(1)}, bf16[8,3200]{1,0:T(8,128)(2,1)S(1)}, u32[]{:S(2)}, u32[]{:S(2)}) collective-permute-start(bf16[8,3200]{1,0:T(8,128)(2,1)S(1)} %shard_map.64.after), channel_id=1, source_target_pairs={{0,12},{2,14},{4,0},{6,2},{8,4},{10,6},{12,8},{14,10},{1,13},{3,15... | collective-permute-start | bytes 153608 | tf_op jit(solution)/shard_map/ppermute | solution.py:300
  7.9 4.3 %shard_map.65 = (bf16[2,2688,512]{2,1,0:T(8,128)(2,1)S(1)}, bf16[2,2688,512]{2,1,0:T(8,128)(2,1)S(1)}) custom-call(bf16[8,3200]{1,0:T(8,128)(2,1)S(1)} %shard_map.64.after, bf16[1,2688,6144]{2,1,0:T(8,128)(2,1)} %refs_6_.1, bf16[1,2688,6144]{2,1,0:T(8,128)(2,1)} %refs_7_.1), custom_call_target="tpu_custom_call" | custom-call | bytes 11010048 | tf_op jit(solution)/shard_map/pallas_call | solution.py:27
  12.2 0.0 collective-permute-done
  12.2 0.0 collective-permute-done.1
  12.2 0.0 collective-permute-done.2
  12.3 0.1 collective-permute-start.5
  12.4 1.6 %collective-permute-start.3 = (bf16[32,3072]{1,0:T(8,128)(2,1)S(1)}, bf16[32,3072]{1,0:T(8,128)(2,1)S(1)}, u32[]{:S(2)}, u32[]{:S(2)}) collective-permute-start(bf16[32,3072]{1,0:T(8,128)(2,1)S(1)} %slice.27), channel_id=1, source_target_pairs={{0,1},{1,0},{2,3},{3,2},{4,5},{5,4},{6,7},{7,6},{8,9},{9,8},{10,11... | collective-permute-start | bytes 589832 | tf_op jit(solution)/shard_map/ppermute | solution.py:307
  13.9 0.4 collective-permute-start.4
  14.3 0.0 collective-permute-done.5.refs_1_.other
  14.3 12.1 %shard_map.66 = (f32[2688,64]{1,0:T(8,128)S(1)}, f32[2688,64]{1,0:T(8,128)S(1)}, bf16[2,2688,512]{2,1,0:T(8,128)(2,1)S(1)}, bf16[2,2688,512]{2,1,0:T(8,128)(2,1)S(1)}) custom-call(bf16[32,3200]{1,0:T(8,128)(2,1)S(1)} %constant_dynamic-update-slice_fusion.refs_0_.own, bf16[32,3200]{1,0:T(8,128)(2,1)S(1)} %collective-permute-done.5.refs_1_.other, ...), custom_call_target="tpu_custom_call" | custom-call | flops 2113929216 | bytes 33030144 | tf_op jit(solution)/shard_map/pallas_call | solution.py:27
  26.4 0.0 collective-permute-done.3.refs_0_
  26.4 11.7 %shard_map.67 = (bf16[64,2688]{1,0:T(8,128)(2,1)S(1)}, bf16[3,2688,512]{2,1,0:T(8,128)(2,1)S(1)}) custom-call(bf16[32,3072]{1,0:T(8,128)(2,1)S(1)} %collective-permute-done.3.refs_0_, bf16[32,3072]{1,0:T(8,128)(2,1)S(1)} %collective-permute-done.4.refs_1_, f32[2688,64]{1,0:T(8,128)S(1)} %get-tuple-element.36.refs_2_, ...), custom_call_target="tpu_custom_call" | custom-call | flops 2113929216 | bytes 33030144 | tf_op jit(solution)/shard_map/pallas_call | solution.py:27
  38.1 5.3 %shard_map.68 = (f32[1,32,3072]{2,1,0:T(8,128)S(1)}, bf16[1,32,3072]{2,1,0:T(8,128)(2,1)S(1)}, bf16[2,2688,512]{2,1,0:T(8,128)(2,1)S(1)}) custom-call(bf16[64,2688]{1,0:T(8,128)(2,1)S(1)} %get-tuple-element.46.hidden, bf16[32,3200]{1,0:T(8,128)(2,1)S(1)} %constant_dynamic-update-slice_fusion.refs_0_.own, ...), custom_call_target="tpu_custom_call" | custom-call | flops 1056964608 | bytes 16515072 | tf_op jit(solution)/shard_map/pallas_call | solution.py:27
  43.5 0.4 collective-permute-start.6
  43.8 1.3 %shard_map.69 = (f32[1,32,1024]{2,1,0:T(8,128)S(1)}, bf16[1,32,1024]{2,1,0:T(8,128)(2,1)S(1)}) custom-call(bf16[64,2688]{1,0:T(8,128)(2,1)S(1)} %get-tuple-element.46.hidden, bf16[32,3200]{1,0:T(8,128)(2,1)S(1)} %constant_dynamic-update-slice_fusion.refs_0_.own, bf16[32,3200]{1,0:T(8,128)(2,1)S(1)} %collective-permute-done.5.refs_1_.other, ...), custom_call_target="tpu_custom_call" | custom-call | flops 352321536 | bytes 5505024 | tf_op jit(solution)/shard_map/pallas_call | solution.py:27
  45.2 0.1 add_convert_fusion
  45.2 1.6 %collective-permute-start.8 = (bf16[32,3200]{1,0:T(8,128)(2,1)S(1)}, bf16[32,3200]{1,0:T(8,128)(2,1)S(1)}, u32[]{:S(2)}, u32[]{:S(2)}) collective-permute-start(bf16[32,3200]{1,0:T(8,128)(2,1)S(1)} %pad_bitcast_fusion), channel_id=1, source_target_pairs={{0,1},{1,0},{2,3},{3,2},{4,5},{5,4},{6,7},{7,6},{8,9},{9,8},{10,11... | collective-permute-start | bytes 614408 | tf_op jit(solution)/shard_map/ppermute | solution.py:370
  46.8 5.1 %shard_map.70 = (f32[1,32,2048]{2,1,0:T(8,128)S(1)}, bf16[1,32,2048]{2,1,0:T(8,128)(2,1)S(1)}) custom-call(bf16[64,2688]{1,0:T(8,128)(2,1)S(1)} %get-tuple-element.46.hidden, bf16[32,3200]{1,0:T(8,128)(2,1)S(1)} %constant_dynamic-update-slice_fusion.refs_0_.own, bf16[32,3200]{1,0:T(8,128)(2,1)S(1)} %collective-permute-done.5.refs_1_.other, ...), custom_call_target="tpu_custom_call" | custom-call | flops 704643072 | bytes 11010048 | tf_op jit(solution)/shard_map/pallas_call | solution.py:27
  51.9 0.1 collective-permute-start.7
  52.0 1.4 %collective-permute-done.7 = bf16[32,3072]{1,0:T(8,128)(2,1)S(1)} collective-permute-done((bf16[32,3072]{1,0:T(8,128)(2,1)S(1)}, bf16[32,3072]{1,0:T(8,128)(2,1)S(1)}, u32[]{:S(2)}, u32[]{:S(2)}) %collective-permute-start.7) | collective-permute-done | bytes 196640 | tf_op jit(solution)/shard_map/ppermute | solution.py:373
  53.5 0.0 collective-permute-done.8
  53.5 0.1 fusion.4
  53.6 0.4 collective-permute-start.10
  54.0 1.8 %collective-permute-start.11 = (bf16[8,3072]{1,0:T(8,128)(2,1)S(1)}, bf16[8,3072]{1,0:T(8,128)(2,1)S(1)}, u32[]{:S(2)}, u32[]{:S(2)}) collective-permute-start(bf16[8,3072]{1,0:T(8,128)(2,1)S(1)} %get-tuple-element.54), channel_id=1, source_target_pairs={{0,4},{2,6},{4,8},{6,10},{8,12},{10,14},{12,0},{14,2},{1,5},{3,7},... | collective-permute-start | bytes 147464 | tf_op jit(solution)/shard_map/ppermute | solution.py:379
  55.7 2.0 %collective-permute-start.9 = (bf16[8,3072]{1,0:T(8,128)(2,1)S(1)}, bf16[8,3072]{1,0:T(8,128)(2,1)S(1)}, u32[]{:S(2)}, u32[]{:S(2)}) collective-permute-start(bf16[8,3072]{1,0:T(8,128)(2,1)S(1)} %get-tuple-element.53), channel_id=1, source_target_pairs={{0,12},{2,14},{4,0},{6,2},{8,4},{10,6},{12,8},{14,10},{1,13},{3,15... | collective-permute-start | bytes 147464 | tf_op jit(solution)/shard_map/ppermute | solution.py:379
  57.8 2.9 %collective-permute-done.10 = bf16[8,3072]{1,0:T(8,128)(2,1)S(1)} collective-permute-done((bf16[8,3072]{1,0:T(8,128)(2,1)S(1)}, bf16[8,3072]{1,0:T(8,128)(2,1)S(1)}, u32[]{:S(2)}, u32[]{:S(2)}) %collective-permute-start.10) | collective-permute-done | bytes 49184 | tf_op jit(solution)/shard_map/ppermute | solution.py:379
  60.7 0.0 collective-permute-done.11
  60.7 0.2 collective-permute-done.9
  60.9 0.6 %fusion.3 = bf16[8,3072]{1,0:T(8,128)(2,1)} fusion(f32[32,3072]{1,0:T(8,128)S(1)} %get-tuple-element.52, bf16[8,3072]{1,0:T(8,128)(2,1)S(1)} %collective-permute-done.11, bf16[8,3072]{1,0:T(8,128)(2,1)S(1)} %collective-permute-done.10, bf16[8,3072]{1,0:T(8,128)(2,1)S(1)} %collective-permute-done.9), kind=kLoop, calls=%fused_computation.8 | loop fusion | flops 172032 | bytes 294912 | tf_op jit(solution)/shard_map/convert_element_type | solution.py:380
  (10 shorter events, 0.1 us)
Async XLA Ops:
  0.9 11.3 %collective-permute-start = (bf16[8,3200]{1,0:T(8,128)(2,1)S(1)}, bf16[8,3200]{1,0:T(8,128)(2,1)S(1)}, u32[]{:S(2)}, u32[]{:S(2)}) collective-permute-start(bf16[8,3200]{1,0:T(8,128)(2,1)S(1)} %shard_map.64.after), channel_id=1, source_target_pairs={{0,4},{2,6},{4,8},{6,10},{8,12},{10,14},{12,0},{14,2},{1,5},{3,7},... | collective-permute-start | bytes 153608 | tf_op jit(solution)/shard_map/ppermute | solution.py:300
  3.9 8.2 %collective-permute-start.1 = (bf16[8,3200]{1,0:T(8,128)(2,1)S(1)}, bf16[8,3200]{1,0:T(8,128)(2,1)S(1)}, u32[]{:S(2)}, u32[]{:S(2)}) collective-permute-start(bf16[8,3200]{1,0:T(8,128)(2,1)S(1)} %shard_map.64.after), channel_id=1, source_target_pairs={{0,8},{2,10},{4,12},{6,14},{8,0},{10,2},{12,4},{14,6},{1,9},{3,11}... | collective-permute-start | bytes 153608 | tf_op jit(solution)/shard_map/ppermute | solution.py:300
  6.5 5.7 %collective-permute-start.2 = (bf16[8,3200]{1,0:T(8,128)(2,1)S(1)}, bf16[8,3200]{1,0:T(8,128)(2,1)S(1)}, u32[]{:S(2)}, u32[]{:S(2)}) collective-permute-start(bf16[8,3200]{1,0:T(8,128)(2,1)S(1)} %shard_map.64.after), channel_id=1, source_target_pairs={{0,12},{2,14},{4,0},{6,2},{8,4},{10,6},{12,8},{14,10},{1,13},{3,15... | collective-permute-start | bytes 153608 | tf_op jit(solution)/shard_map/ppermute | solution.py:300
  12.3 2.0 %collective-permute-start.5 = (bf16[32,3200]{1,0:T(8,128)(2,1)S(1)}, bf16[32,3200]{1,0:T(8,128)(2,1)S(1)}, u32[]{:S(2)}, u32[]{:S(2)}) collective-permute-start(bf16[32,3200]{1,0:T(8,128)(2,1)S(1)} %constant_dynamic-update-slice_fusion.refs_0_.own), channel_id=1, source_target_pairs={{0,2},{2,0},{4,6},{6,4},{8,10},{10,8},{12,14},{14,12},{1,3},{3,1},... | collective-permute-start | bytes 614408 | tf_op jit(solution)/shard_map/ppermute | solution.py:303
  12.4 14.0 %collective-permute-start.3 = (bf16[32,3072]{1,0:T(8,128)(2,1)S(1)}, bf16[32,3072]{1,0:T(8,128)(2,1)S(1)}, u32[]{:S(2)}, u32[]{:S(2)}) collective-permute-start(bf16[32,3072]{1,0:T(8,128)(2,1)S(1)} %slice.27), channel_id=1, source_target_pairs={{0,1},{1,0},{2,3},{3,2},{4,5},{5,4},{6,7},{7,6},{8,9},{9,8},{10,11... | collective-permute-start | bytes 589832 | tf_op jit(solution)/shard_map/ppermute | solution.py:307
  13.9 12.4 %collective-permute-start.4 = (bf16[32,3072]{1,0:T(8,128)(2,1)S(1)}, bf16[32,3072]{1,0:T(8,128)(2,1)S(1)}, u32[]{:S(2)}, u32[]{:S(2)}) collective-permute-start(bf16[32,3072]{1,0:T(8,128)(2,1)S(1)} %slice.27), channel_id=1, source_target_pairs={{0,3},{1,2},{2,1},{3,0},{4,7},{5,6},{6,5},{7,4},{8,11},{9,10},{10,... | collective-permute-start | bytes 589832 | tf_op jit(solution)/shard_map/ppermute | solution.py:308
  43.5 1.7 %collective-permute-start.6 = (bf16[1,32,3072]{2,1,0:T(8,128)(2,1)S(1)}, bf16[1,32,3072]{2,1,0:T(8,128)(2,1)S(1)}, u32[]{:S(2)}, u32[]{:S(2)}) collective-permute-start(bf16[1,32,3072]{2,1,0:T(8,128)(2,1)S(1)} %get-tuple-element.45), channel_id=1, source_target_pairs={{0,2},{2,0},{4,6},{6,4},{8,10},{10,8},{12,14},{14,12},{1,3},{3,1},... | collective-permute-start | bytes 589832 | tf_op jit(solution)/shard_map/ppermute | solution.py:365
  45.2 8.2 %collective-permute-start.8 = (bf16[32,3200]{1,0:T(8,128)(2,1)S(1)}, bf16[32,3200]{1,0:T(8,128)(2,1)S(1)}, u32[]{:S(2)}, u32[]{:S(2)}) collective-permute-start(bf16[32,3200]{1,0:T(8,128)(2,1)S(1)} %pad_bitcast_fusion), channel_id=1, source_target_pairs={{0,1},{1,0},{2,3},{3,2},{4,5},{5,4},{6,7},{7,6},{8,9},{9,8},{10,11... | collective-permute-start | bytes 614408 | tf_op jit(solution)/shard_map/ppermute | solution.py:370
  51.9 1.5 %collective-permute-start.7 = (bf16[32,3072]{1,0:T(8,128)(2,1)S(1)}, bf16[32,3072]{1,0:T(8,128)(2,1)S(1)}, u32[]{:S(2)}, u32[]{:S(2)}) collective-permute-start(bf16[32,3072]{1,0:T(8,128)(2,1)S(1)} %pad_maximum_fusion), channel_id=1, source_target_pairs={{0,2},{2,0},{4,6},{6,4},{8,10},{10,8},{12,14},{14,12},{1,3},{3,1},... | collective-permute-start | bytes 589832 | tf_op jit(solution)/shard_map/ppermute | solution.py:373
  53.6 7.2 %collective-permute-start.10 = (bf16[8,3072]{1,0:T(8,128)(2,1)S(1)}, bf16[8,3072]{1,0:T(8,128)(2,1)S(1)}, u32[]{:S(2)}, u32[]{:S(2)}) collective-permute-start(bf16[8,3072]{1,0:T(8,128)(2,1)S(1)} %get-tuple-element.55), channel_id=1, source_target_pairs={{0,8},{2,10},{4,12},{6,14},{8,0},{10,2},{12,4},{14,6},{1,9},{3,11}... | collective-permute-start | bytes 147464 | tf_op jit(solution)/shard_map/ppermute | solution.py:379
  54.0 6.8 %collective-permute-start.11 = (bf16[8,3072]{1,0:T(8,128)(2,1)S(1)}, bf16[8,3072]{1,0:T(8,128)(2,1)S(1)}, u32[]{:S(2)}, u32[]{:S(2)}) collective-permute-start(bf16[8,3072]{1,0:T(8,128)(2,1)S(1)} %get-tuple-element.54), channel_id=1, source_target_pairs={{0,4},{2,6},{4,8},{6,10},{8,12},{10,14},{12,0},{14,2},{1,5},{3,7},... | collective-permute-start | bytes 147464 | tf_op jit(solution)/shard_map/ppermute | solution.py:379
  55.7 5.2 %collective-permute-start.9 = (bf16[8,3072]{1,0:T(8,128)(2,1)S(1)}, bf16[8,3072]{1,0:T(8,128)(2,1)S(1)}, u32[]{:S(2)}, u32[]{:S(2)}) collective-permute-start(bf16[8,3072]{1,0:T(8,128)(2,1)S(1)} %get-tuple-element.53), channel_id=1, source_target_pairs={{0,12},{2,14},{4,0},{6,2},{8,4},{10,6},{12,8},{14,10},{1,13},{3,15... | collective-permute-start | bytes 147464 | tf_op jit(solution)/shard_map/ppermute | solution.py:379

commit v9 on v5

--- a/solution.py
+++ b/solution.py
@@ -53,6 +53,8 @@
 
 def stream(held, count, fetch, ahead, begin, from_held, from_ring):
     rest = count - held
+    early, late = max(rest - SLOTS, 0), max(min(rest - SLOTS + (rest > SLOTS), rest - 1), 0)
+    several = -(-len(ahead) // 2)
     for at in range(min(SLOTS, rest)):
         for copy in fetch(held + at, at):
             copy.start()
@@ -76,9 +78,14 @@
             for copy in fetch(held + later, lax.rem(later, SLOTS)):
                 copy.start()
 
-        @pl.when(at == max(rest - SLOTS, 0))
+        @pl.when(at == early)
         def _():
-            for copy in ahead:
+            for copy in ahead[:several]:
+                copy.start()
+
+        @pl.when(at == late)
+        def _():
+            for copy in ahead[several:]:
                 copy.start()
 
         slot = lax.rem(at, SLOTS)

time: 60.9 us -> 60.8 us (level)
  no operation moved by 1% of the time
where the time goes in v9:
time: 60.8 us; the launch traced here: 60.6 us
  Pallas kernels  39.7 us (65%)
  starting transfers between devices  15.2 us (25%)
  waiting for transfers between devices  4.61 us (8%)
  other arithmetic  0.78 us (1%)
    pallas_call x7, Pallas kernels, call(): pl.pallas_call(kernel, out_shape=outs, in_specs=[pl.BlockSpec(memory_spac...  39.7 us
    ppermute x3, starting transfers between devices, body(): lax.ppermute(packed, 'expert', along(k))  7.01 us
    ppermute x3, starting transfers between devices, body(): mixed = mixed + lax.ppermute(piece, 'expert', along(-k)).astype(F32)  4.22 us
    ppermute x3, waiting for transfers between devices, body(): mixed = mixed + lax.ppermute(piece, 'expert', along(-k)).astype(F32)  3.16 us
    ppermute x1, starting transfers between devices, body(): lax.ppermute(away[j - 1], 'blk', across(j))[:, :width]  1.56 us
    ppermute x1, starting transfers between devices, body(): sent.append(lax.ppermute(bare, 'blk', across(-j)))  1.56 us
    ppermute x1, waiting for transfers between devices, body(): summed = kept + lax.ppermute(given, 'expert', swap).astype(F32)  1.43 us
  transfers between devices with their start and end apart: 12, of which 3 were waited for; matrix products, arithmetic and copies ran while one was open for 0% of the time, Pallas kernels for 37%

profile of v9, /device:TPU:0, one launch (start us, length us, event | category | flops | bytes accessed | tf_op | source)
XLA Modules:
  0.0 60.6 jit_solution(14534018981878489383)
XLA Ops:
  0.0 0.9 %shard_map.64.after = bf16[8,3200]{1,0:T(8,128)(2,1)S(1)} custom-call(bf16[8,3072]{1,0:T(8,128)(2,1)} %tokens.1, s32[4,8]{1,0:T(4,128)} %bitcast.12, f32[4,8]{1,0:T(4,128)} %bitcast.13), custom_call_target="tpu_custom_call" | custom-call | flops 1024 | bytes 98304 | tf_op jit(solution)/shard_map/pallas_call | solution.py:27
  0.9 3.1 %collective-permute-start = (bf16[8,3200]{1,0:T(8,128)(2,1)S(1)}, bf16[8,3200]{1,0:T(8,128)(2,1)S(1)}, u32[]{:S(2)}, u32[]{:S(2)}) collective-permute-start(bf16[8,3200]{1,0:T(8,128)(2,1)S(1)} %shard_map.64.after), channel_id=1, source_target_pairs={{0,4},{2,6},{4,8},{6,10},{8,12},{10,14},{12,0},{14,2},{1,5},{3,7},... | collective-permute-start | bytes 153608 | tf_op jit(solution)/shard_map/ppermute | solution.py:302
  3.9 2.6 %collective-permute-start.1 = (bf16[8,3200]{1,0:T(8,128)(2,1)S(1)}, bf16[8,3200]{1,0:T(8,128)(2,1)S(1)}, u32[]{:S(2)}, u32[]{:S(2)}) collective-permute-start(bf16[8,3200]{1,0:T(8,128)(2,1)S(1)} %shard_map.64.after), channel_id=1, source_target_pairs={{0,8},{2,10},{4,12},{6,14},{8,0},{10,2},{12,4},{14,6},{1,9},{3,11}... | collective-permute-start | bytes 153608 | tf_op jit(solution)/shard_map/ppermute | solution.py:302
  6.5 1.3 %collective-permute-start.2 = (bf16[8,3200]{1,0:T(8,128)(2,1)S(1)}, bf16[8,3200]{1,0:T(8,128)(2,1)S(1)}, u32[]{:S(2)}, u32[]{:S(2)}) collective-permute-start(bf16[8,3200]{1,0:T(8,128)(2,1)S(1)} %shard_map.64.after), channel_id=1, source_target_pairs={{0,12},{2,14},{4,0},{6,2},{8,4},{10,6},{12,8},{14,10},{1,13},{3,15... | collective-permute-start | bytes 153608 | tf_op jit(solution)/shard_map/ppermute | solution.py:302
  7.9 4.3 %shard_map.65 = (bf16[2,2688,512]{2,1,0:T(8,128)(2,1)S(1)}, bf16[2,2688,512]{2,1,0:T(8,128)(2,1)S(1)}) custom-call(bf16[8,3200]{1,0:T(8,128)(2,1)S(1)} %shard_map.64.after, bf16[1,2688,6144]{2,1,0:T(8,128)(2,1)} %refs_6_.1, bf16[1,2688,6144]{2,1,0:T(8,128)(2,1)} %refs_7_.1), custom_call_target="tpu_custom_call" | custom-call | bytes 11010048 | tf_op jit(solution)/shard_map/pallas_call | solution.py:27
  12.2 0.0 collective-permute-done
  12.2 0.0 collective-permute-done.1
  12.2 0.0 collective-permute-done.2
  12.3 0.1 collective-permute-start.5
  12.4 1.6 %collective-permute-start.3 = (bf16[32,3072]{1,0:T(8,128)(2,1)S(1)}, bf16[32,3072]{1,0:T(8,128)(2,1)S(1)}, u32[]{:S(2)}, u32[]{:S(2)}) collective-permute-start(bf16[32,3072]{1,0:T(8,128)(2,1)S(1)} %slice.27), channel_id=1, source_target_pairs={{0,1},{1,0},{2,3},{3,2},{4,5},{5,4},{6,7},{7,6},{8,9},{9,8},{10,11... | collective-permute-start | bytes 589832 | tf_op jit(solution)/shard_map/ppermute | solution.py:309
  13.9 0.4 collective-permute-start.4
  14.3 0.0 collective-permute-done.5.refs_1_.other
  14.3 11.5 %shard_map.66 = (f32[2688,64]{1,0:T(8,128)S(1)}, f32[2688,64]{1,0:T(8,128)S(1)}, bf16[2,2688,512]{2,1,0:T(8,128)(2,1)S(1)}, bf16[2,2688,512]{2,1,0:T(8,128)(2,1)S(1)}) custom-call(bf16[32,3200]{1,0:T(8,128)(2,1)S(1)} %constant_dynamic-update-slice_fusion.refs_0_.own, bf16[32,3200]{1,0:T(8,128)(2,1)S(1)} %collective-permute-done.5.refs_1_.other, ...), custom_call_target="tpu_custom_call" | custom-call | flops 2113929216 | bytes 33030144 | tf_op jit(solution)/shard_map/pallas_call | solution.py:27
  25.8 0.0 collective-permute-done.3.refs_0_
  25.8 11.3 %shard_map.67 = (bf16[64,2688]{1,0:T(8,128)(2,1)S(1)}, bf16[3,2688,512]{2,1,0:T(8,128)(2,1)S(1)}) custom-call(bf16[32,3072]{1,0:T(8,128)(2,1)S(1)} %collective-permute-done.3.refs_0_, bf16[32,3072]{1,0:T(8,128)(2,1)S(1)} %collective-permute-done.4.refs_1_, f32[2688,64]{1,0:T(8,128)S(1)} %get-tuple-element.36.refs_2_, ...), custom_call_target="tpu_custom_call" | custom-call | flops 2113929216 | bytes 33030144 | tf_op jit(solution)/shard_map/pallas_call | solution.py:27
  37.1 5.3 %shard_map.68 = (f32[1,32,3072]{2,1,0:T(8,128)S(1)}, bf16[1,32,3072]{2,1,0:T(8,128)(2,1)S(1)}, bf16[2,2688,512]{2,1,0:T(8,128)(2,1)S(1)}) custom-call(bf16[64,2688]{1,0:T(8,128)(2,1)S(1)} %get-tuple-element.46.hidden, bf16[32,3200]{1,0:T(8,128)(2,1)S(1)} %constant_dynamic-update-slice_fusion.refs_0_.own, ...), custom_call_target="tpu_custom_call" | custom-call | flops 1056964608 | bytes 16515072 | tf_op jit(solution)/shard_map/pallas_call | solution.py:27
  42.5 0.4 collective-permute-start.6
  42.9 1.3 %shard_map.69 = (f32[1,32,1024]{2,1,0:T(8,128)S(1)}, bf16[1,32,1024]{2,1,0:T(8,128)(2,1)S(1)}) custom-call(bf16[64,2688]{1,0:T(8,128)(2,1)S(1)} %get-tuple-element.46.hidden, bf16[32,3200]{1,0:T(8,128)(2,1)S(1)} %constant_dynamic-update-slice_fusion.refs_0_.own, bf16[32,3200]{1,0:T(8,128)(2,1)S(1)} %collective-permute-done.5.refs_1_.other, ...), custom_call_target="tpu_custom_call" | custom-call | flops 352321536 | bytes 5505024 | tf_op jit(solution)/shard_map/pallas_call | solution.py:27
  44.2 0.0 collective-permute-done.6
  44.2 0.1 add_convert_fusion
  44.3 1.6 %collective-permute-start.8 = (bf16[32,3200]{1,0:T(8,128)(2,1)S(1)}, bf16[32,3200]{1,0:T(8,128)(2,1)S(1)}, u32[]{:S(2)}, u32[]{:S(2)}) collective-permute-start(bf16[32,3200]{1,0:T(8,128)(2,1)S(1)} %pad_bitcast_fusion), channel_id=1, source_target_pairs={{0,1},{1,0},{2,3},{3,2},{4,5},{5,4},{6,7},{7,6},{8,9},{9,8},{10,11... | collective-permute-start | bytes 614408 | tf_op jit(solution)/shard_map/ppermute | solution.py:372
  45.8 5.1 %shard_map.70 = (f32[1,32,2048]{2,1,0:T(8,128)S(1)}, bf16[1,32,2048]{2,1,0:T(8,128)(2,1)S(1)}) custom-call(bf16[64,2688]{1,0:T(8,128)(2,1)S(1)} %get-tuple-element.46.hidden, bf16[32,3200]{1,0:T(8,128)(2,1)S(1)} %constant_dynamic-update-slice_fusion.refs_0_.own, bf16[32,3200]{1,0:T(8,128)(2,1)S(1)} %collective-permute-done.5.refs_1_.other, ...), custom_call_target="tpu_custom_call" | custom-call | flops 704643072 | bytes 11010048 | tf_op jit(solution)/shard_map/pallas_call | solution.py:27
  51.0 0.1 collective-permute-start.7
  51.1 1.4 %collective-permute-done.7 = bf16[32,3072]{1,0:T(8,128)(2,1)S(1)} collective-permute-done((bf16[32,3072]{1,0:T(8,128)(2,1)S(1)}, bf16[32,3072]{1,0:T(8,128)(2,1)S(1)}, u32[]{:S(2)}, u32[]{:S(2)}) %collective-permute-start.7) | collective-permute-done | bytes 196640 | tf_op jit(solution)/shard_map/ppermute | solution.py:375
  52.5 0.0 collective-permute-done.8
  52.5 0.1 fusion.4
  52.6 0.4 collective-permute-start.10
  53.0 1.8 %collective-permute-start.11 = (bf16[8,3072]{1,0:T(8,128)(2,1)S(1)}, bf16[8,3072]{1,0:T(8,128)(2,1)S(1)}, u32[]{:S(2)}, u32[]{:S(2)}) collective-permute-start(bf16[8,3072]{1,0:T(8,128)(2,1)S(1)} %get-tuple-element.54), channel_id=1, source_target_pairs={{0,4},{2,6},{4,8},{6,10},{8,12},{10,14},{12,0},{14,2},{1,5},{3,7},... | collective-permute-start | bytes 147464 | tf_op jit(solution)/shard_map/ppermute | solution.py:381
  54.8 2.0 %collective-permute-start.9 = (bf16[8,3072]{1,0:T(8,128)(2,1)S(1)}, bf16[8,3072]{1,0:T(8,128)(2,1)S(1)}, u32[]{:S(2)}, u32[]{:S(2)}) collective-permute-start(bf16[8,3072]{1,0:T(8,128)(2,1)S(1)} %get-tuple-element.53), channel_id=1, source_target_pairs={{0,12},{2,14},{4,0},{6,2},{8,4},{10,6},{12,8},{14,10},{1,13},{3,15... | collective-permute-start | bytes 147464 | tf_op jit(solution)/shard_map/ppermute | solution.py:381
  56.8 2.9 %collective-permute-done.10 = bf16[8,3072]{1,0:T(8,128)(2,1)S(1)} collective-permute-done((bf16[8,3072]{1,0:T(8,128)(2,1)S(1)}, bf16[8,3072]{1,0:T(8,128)(2,1)S(1)}, u32[]{:S(2)}, u32[]{:S(2)}) %collective-permute-start.10) | collective-permute-done | bytes 49184 | tf_op jit(solution)/shard_map/ppermute | solution.py:381
  59.7 0.2 collective-permute-done.9
  60.0 0.6 %fusion.3 = bf16[8,3072]{1,0:T(8,128)(2,1)} fusion(f32[32,3072]{1,0:T(8,128)S(1)} %get-tuple-element.52, bf16[8,3072]{1,0:T(8,128)(2,1)S(1)} %collective-permute-done.11, bf16[8,3072]{1,0:T(8,128)(2,1)S(1)} %collective-permute-done.10, bf16[8,3072]{1,0:T(8,128)(2,1)S(1)} %collective-permute-done.9), kind=kLoop, calls=%fused_computation.8 | loop fusion | flops 172032 | bytes 294912 | tf_op jit(solution)/shard_map/convert_element_type | solution.py:382
  (10 shorter events, 0.1 us)
Async XLA Ops:
  0.9 11.3 %collective-permute-start = (bf16[8,3200]{1,0:T(8,128)(2,1)S(1)}, bf16[8,3200]{1,0:T(8,128)(2,1)S(1)}, u32[]{:S(2)}, u32[]{:S(2)}) collective-permute-start(bf16[8,3200]{1,0:T(8,128)(2,1)S(1)} %shard_map.64.after), channel_id=1, source_target_pairs={{0,4},{2,6},{4,8},{6,10},{8,12},{10,14},{12,0},{14,2},{1,5},{3,7},... | collective-permute-start | bytes 153608 | tf_op jit(solution)/shard_map/ppermute | solution.py:302
  3.9 8.2 %collective-permute-start.1 = (bf16[8,3200]{1,0:T(8,128)(2,1)S(1)}, bf16[8,3200]{1,0:T(8,128)(2,1)S(1)}, u32[]{:S(2)}, u32[]{:S(2)}) collective-permute-start(bf16[8,3200]{1,0:T(8,128)(2,1)S(1)} %shard_map.64.after), channel_id=1, source_target_pairs={{0,8},{2,10},{4,12},{6,14},{8,0},{10,2},{12,4},{14,6},{1,9},{3,11}... | collective-permute-start | bytes 153608 | tf_op jit(solution)/shard_map/ppermute | solution.py:302
  6.5 5.7 %collective-permute-start.2 = (bf16[8,3200]{1,0:T(8,128)(2,1)S(1)}, bf16[8,3200]{1,0:T(8,128)(2,1)S(1)}, u32[]{:S(2)}, u32[]{:S(2)}) collective-permute-start(bf16[8,3200]{1,0:T(8,128)(2,1)S(1)} %shard_map.64.after), channel_id=1, source_target_pairs={{0,12},{2,14},{4,0},{6,2},{8,4},{10,6},{12,8},{14,10},{1,13},{3,15... | collective-permute-start | bytes 153608 | tf_op jit(solution)/shard_map/ppermute | solution.py:302
  12.3 2.0 %collective-permute-start.5 = (bf16[32,3200]{1,0:T(8,128)(2,1)S(1)}, bf16[32,3200]{1,0:T(8,128)(2,1)S(1)}, u32[]{:S(2)}, u32[]{:S(2)}) collective-permute-start(bf16[32,3200]{1,0:T(8,128)(2,1)S(1)} %constant_dynamic-update-slice_fusion.refs_0_.own), channel_id=1, source_target_pairs={{0,2},{2,0},{4,6},{6,4},{8,10},{10,8},{12,14},{14,12},{1,3},{3,1},... | collective-permute-start | bytes 614408 | tf_op jit(solution)/shard_map/ppermute | solution.py:305
  12.4 13.4 %collective-permute-start.3 = (bf16[32,3072]{1,0:T(8,128)(2,1)S(1)}, bf16[32,3072]{1,0:T(8,128)(2,1)S(1)}, u32[]{:S(2)}, u32[]{:S(2)}) collective-permute-start(bf16[32,3072]{1,0:T(8,128)(2,1)S(1)} %slice.27), channel_id=1, source_target_pairs={{0,1},{1,0},{2,3},{3,2},{4,5},{5,4},{6,7},{7,6},{8,9},{9,8},{10,11... | collective-permute-start | bytes 589832 | tf_op jit(solution)/shard_map/ppermute | solution.py:309
  13.9 11.9 %collective-permute-start.4 = (bf16[32,3072]{1,0:T(8,128)(2,1)S(1)}, bf16[32,3072]{1,0:T(8,128)(2,1)S(1)}, u32[]{:S(2)}, u32[]{:S(2)}) collective-permute-start(bf16[32,3072]{1,0:T(8,128)(2,1)S(1)} %slice.27), channel_id=1, source_target_pairs={{0,3},{1,2},{2,1},{3,0},{4,7},{5,6},{6,5},{7,4},{8,11},{9,10},{10,... | collective-permute-start | bytes 589832 | tf_op jit(solution)/shard_map/ppermute | solution.py:310
  42.5 1.7 %collective-permute-start.6 = (bf16[1,32,3072]{2,1,0:T(8,128)(2,1)S(1)}, bf16[1,32,3072]{2,1,0:T(8,128)(2,1)S(1)}, u32[]{:S(2)}, u32[]{:S(2)}) collective-permute-start(bf16[1,32,3072]{2,1,0:T(8,128)(2,1)S(1)} %get-tuple-element.45), channel_id=1, source_target_pairs={{0,2},{2,0},{4,6},{6,4},{8,10},{10,8},{12,14},{14,12},{1,3},{3,1},... | collective-permute-start | bytes 589832 | tf_op jit(solution)/shard_map/ppermute | solution.py:367
  44.3 8.2 %collective-permute-start.8 = (bf16[32,3200]{1,0:T(8,128)(2,1)S(1)}, bf16[32,3200]{1,0:T(8,128)(2,1)S(1)}, u32[]{:S(2)}, u32[]{:S(2)}) collective-permute-start(bf16[32,3200]{1,0:T(8,128)(2,1)S(1)} %pad_bitcast_fusion), channel_id=1, source_target_pairs={{0,1},{1,0},{2,3},{3,2},{4,5},{5,4},{6,7},{7,6},{8,9},{9,8},{10,11... | collective-permute-start | bytes 614408 | tf_op jit(solution)/shard_map/ppermute | solution.py:372
  51.0 1.5 %collective-permute-start.7 = (bf16[32,3072]{1,0:T(8,128)(2,1)S(1)}, bf16[32,3072]{1,0:T(8,128)(2,1)S(1)}, u32[]{:S(2)}, u32[]{:S(2)}) collective-permute-start(bf16[32,3072]{1,0:T(8,128)(2,1)S(1)} %pad_maximum_fusion), channel_id=1, source_target_pairs={{0,2},{2,0},{4,6},{6,4},{8,10},{10,8},{12,14},{14,12},{1,3},{3,1},... | collective-permute-start | bytes 589832 | tf_op jit(solution)/shard_map/ppermute | solution.py:375
  52.6 7.2 %collective-permute-start.10 = (bf16[8,3072]{1,0:T(8,128)(2,1)S(1)}, bf16[8,3072]{1,0:T(8,128)(2,1)S(1)}, u32[]{:S(2)}, u32[]{:S(2)}) collective-permute-start(bf16[8,3072]{1,0:T(8,128)(2,1)S(1)} %get-tuple-element.55), channel_id=1, source_target_pairs={{0,8},{2,10},{4,12},{6,14},{8,0},{10,2},{12,4},{14,6},{1,9},{3,11}... | collective-permute-start | bytes 147464 | tf_op jit(solution)/shard_map/ppermute | solution.py:381
  53.0 6.8 %collective-permute-start.11 = (bf16[8,3072]{1,0:T(8,128)(2,1)S(1)}, bf16[8,3072]{1,0:T(8,128)(2,1)S(1)}, u32[]{:S(2)}, u32[]{:S(2)}) collective-permute-start(bf16[8,3072]{1,0:T(8,128)(2,1)S(1)} %get-tuple-element.54), channel_id=1, source_target_pairs={{0,4},{2,6},{4,8},{6,10},{8,12},{10,14},{12,0},{14,2},{1,5},{3,7},... | collective-permute-start | bytes 147464 | tf_op jit(solution)/shard_map/ppermute | solution.py:381
  54.8 5.2 %collective-permute-start.9 = (bf16[8,3072]{1,0:T(8,128)(2,1)S(1)}, bf16[8,3072]{1,0:T(8,128)(2,1)S(1)}, u32[]{:S(2)}, u32[]{:S(2)}) collective-permute-start(bf16[8,3072]{1,0:T(8,128)(2,1)S(1)} %get-tuple-element.53), channel_id=1, source_target_pairs={{0,12},{2,14},{4,0},{6,2},{8,4},{10,6},{12,8},{14,10},{1,13},{3,15... | collective-permute-start | bytes 147464 | tf_op jit(solution)/shard_map/ppermute | solution.py:381
